TPU v7x, 32 devices: a whole 2x2x4 slice. The times are simulated.
32 devices in a mesh: frames: 2 (over x), chain: 16 (over z, y, core).
Axes of the slice: x: 2, y: 2, z: 4, core: 2. Of those that a mesh axis runs over, the one named last changes fastest.
Arguments:
- species: int32 [8192], P(('frames', 'chain')), parts along dimension 0, may hold values from 0 to 127
- positions: float32 [3, 8192], P(None, ('frames', 'chain')), parts along dimension 1, may hold values from -18 to 18
- block_list: int32 [64, 3], P(('frames', 'chain')), parts along dimension 0, may hold values from -1 to 31, as said below
- embed_table: bfloat16 [128, 512], replicated, may hold values from -6 to 6
- w_query: bfloat16 [2, 512, 512], replicated, may hold values from -0.25 to 0.25
- w_key: bfloat16 [2, 512, 512], replicated, may hold values from -0.25 to 0.25
- w_value: bfloat16 [2, 512, 512], replicated, may hold values from -0.25 to 0.25
- w_out: bfloat16 [2, 512, 512], replicated, may hold values from -0.25 to 0.25
- w_up: bfloat16 [2, 512, 1024], replicated, may hold values from -0.25 to 0.25
- w_down: bfloat16 [2, 1024, 512], replicated, may hold values from -0.1875 to 0.1875
- norm_gains: float32 [2, 2, 512], replicated, may hold values from 0.5 to 1.5
- gammas: float32 [2, 16], replicated, may hold values from 0.005 to 0.1
- out_gain: float32 [512], replicated, may hold values from 0.5 to 1.5
- readout: float32 [512], replicated, may hold values from -0.25 to 0.25
Outputs:
- energy: float32 [2], P('frames'), parts along dimension 0
- forces: float32 [3, 8192], P(None, ('frames', 'chain')), parts along dimension 1
There are 2 independent parts, one for each index of `frames`. A program takes and returns all parts, laid end to end along the dimension named above; an argument that names none is the same for every part. Nothing has to cross between parts.
Inputs may be any that keep to these rules, and one draw needn't show every extreme that they name: `block_list`: row b holds b-1 or -1, then b, then b+1 or -1; -1 marks a neighbouring block outside the cutoff.
All inputs are finite; a program needn't handle non-finite values.
Results may differ from a plain program's by a relative error of at most 0.022.
Values may be sent and summed in bfloat16 or wider, within the bound.
No kernel may reach another device: no remote copies, remote signals or barrier semaphores. Data moves between devices by JAX's collectives and lax.ppermute only.
A program may use at most 128 MiB of HBM per device.

v0:
```python
from functools import partial

import jax
import jax.numpy as jnp
from jax import lax
from jax.sharding import PartitionSpec as P

BLOCK = 128


def padded(block, sides, width):
    for axis, dim in sides:
        count = lax.axis_size(axis)
        forward = [(i, i + 1) for i in range(count - 1)]
        backward = [(target, source) for source, target in forward]
        low = lax.ppermute(
            lax.slice_in_dim(block, block.shape[dim] - width, None, axis=dim), axis, forward
        )
        high = lax.ppermute(lax.slice_in_dim(block, 0, width, axis=dim), axis, backward)
        block = jnp.concatenate([low, block, high], axis=dim)
    return block


def shifted(value, axis, steps):
    count = lax.axis_size(axis)
    leading, last = (max(0, -steps), min(count, count - steps))
    return lax.ppermute(value, axis, [(source, source + steps) for source in range(leading, last)])


def rms(x, gain):
    return x * lax.rsqrt(jnp.mean(x * x, axis=-1, keepdims=True) + 1e-06) * gain


def windows(ext, nblk):
    blocks = ext.reshape(nblk + 2, 128, ext.shape[-1])
    return jnp.concatenate([blocks[:-2], blocks[1:-1], blocks[2:]], axis=1)


def attend(query, key_ext, value_ext, coord, coord_ext, valid, gamma, heads):
    atoms, width = query.shape
    nblk = atoms // 128
    hdim = width // heads
    key_win = windows(key_ext, nblk).astype(jnp.bfloat16).reshape(nblk, 384, heads, hdim)
    value_win = windows(value_ext, nblk).astype(jnp.bfloat16).reshape(nblk, 384, heads, hdim)
    query_blk = query.reshape(nblk, 128, heads, hdim)
    scores = jnp.einsum(
        "bqhd,bkhd->bhqk", query_blk, key_win, preferred_element_type=jnp.float32
    ) * hdim ** (-0.5)
    coord_blk = coord_ext.reshape(3, nblk + 2, 128)
    coord_win = jnp.concatenate([coord_blk[:, :-2], coord_blk[:, 1:-1], coord_blk[:, 2:]], axis=2)
    coord_q = coord.reshape(3, nblk, 128)
    dist_sq = jnp.sum((coord_q[:, :, :, None] - coord_win[:, :, None, :]) ** 2, axis=0)
    scores = scores - gamma[None, :, None, None] * dist_sq[:, None]
    keymask = jnp.repeat(valid, 128, axis=1)
    scores = jnp.where(keymask[:, None, None, :], scores, -1e30)
    peak = lax.stop_gradient(jnp.max(scores, axis=-1, keepdims=True))
    expo = jnp.exp(scores - peak)
    probs = (expo / jnp.sum(expo, axis=-1, keepdims=True)).astype(jnp.bfloat16)
    mixed = jnp.einsum("bhqk,bkhd->bqhd", probs, value_win, preferred_element_type=jnp.float32)
    return mixed.reshape(atoms, width).astype(jnp.bfloat16)


def finish(weights, valid, state, query, key_ext, value_ext, coord, coord_ext):
    att = attend(
        query, key_ext, value_ext, coord, coord_ext, valid, weights[7], weights[7].shape[0]
    )
    state = state + jnp.dot(att, weights[3], preferred_element_type=jnp.float32)
    inner = rms(state, weights[6][1]).astype(jnp.bfloat16)
    hidden = jax.nn.gelu(jnp.dot(inner, weights[4], preferred_element_type=jnp.float32)).astype(
        jnp.bfloat16
    )
    return state + jnp.dot(hidden, weights[5], preferred_element_type=jnp.float32)


def payload_inputs(state, weights):
    return rms(state, weights[6][0]).astype(jnp.bfloat16)


def mix_inputs(
    weights, valid, state, coord, coord_low, coord_high, normed_own, normed_low, normed_high
):
    query = jnp.dot(
        normed_own.astype(jnp.bfloat16), weights[0], preferred_element_type=jnp.float32
    ).astype(jnp.bfloat16)
    normed_ext = jnp.concatenate([normed_low, normed_own, normed_high], axis=0).astype(jnp.bfloat16)
    key_ext = (
        jnp.dot(normed_ext, weights[1], preferred_element_type=jnp.float32)
        .astype(jnp.bfloat16)
        .astype(jnp.float32)
    )
    value_ext = (
        jnp.dot(normed_ext, weights[2], preferred_element_type=jnp.float32)
        .astype(jnp.bfloat16)
        .astype(jnp.float32)
    )
    coord_ext = jnp.concatenate([coord_low, coord, coord_high], axis=1)
    return finish(weights, valid, state, query, key_ext, value_ext, coord, coord_ext)


def place_first(rows, atoms):
    return jnp.pad(rows, ((0, atoms - rows.shape[0]), (0, 0)))


def place_last(rows, atoms):
    return jnp.pad(rows, ((atoms - rows.shape[0], 0), (0, 0)))


def energy_local(state, out_gain, readout):
    return jnp.sum(jnp.dot(rms(state, out_gain), readout, precision=lax.Precision.HIGHEST))


def local(
    species,
    positions,
    block_list,
    embed_table,
    w_query,
    w_key,
    w_value,
    w_out,
    w_up,
    w_down,
    norm_gains,
    gammas,
    out_gain,
    readout,
):
    atoms = species.shape[0]
    nblk = atoms // BLOCK
    width = embed_table.shape[1]
    layers = w_query.shape[0]
    ids = lax.axis_index("chain") * nblk + jnp.arange(nblk, dtype=jnp.int32)
    expect = ids[:, None] - 1 + jnp.arange(3, dtype=jnp.int32)[None, :]
    valid = (block_list == expect) & (block_list >= 0)
    coord_ext = padded(positions, (("chain", 1),), BLOCK)
    coord_low = coord_ext[:, :BLOCK]
    coord_high = coord_ext[:, -BLOCK:]
    onehot = jax.nn.one_hot(species, embed_table.shape[0], dtype=jnp.bfloat16)
    state = jnp.dot(onehot, embed_table, preferred_element_type=jnp.float32)
    saved = []
    for layer in range(layers):
        weights = (
            w_query[layer],
            w_key[layer],
            w_value[layer],
            w_out[layer],
            w_up[layer],
            w_down[layer],
            norm_gains[layer],
            gammas[layer],
        )
        normed = payload_inputs(state, weights)
        normed_ext = padded(normed, (("chain", 0),), BLOCK)
        rims = (
            normed.astype(jnp.float32),
            normed_ext[:BLOCK].astype(jnp.float32),
            normed_ext[-BLOCK:].astype(jnp.float32),
        )
        layer_fn = partial(mix_inputs, weights, valid)
        saved.append((state, rims, weights))
        state = layer_fn(state, positions, coord_low, coord_high, *rims)
    local_total, pullback = jax.vjp(lambda final: energy_local(final, out_gain, readout), state)
    energy = lax.psum(local_total, "chain").reshape(1)
    (grad_state,) = pullback(jnp.ones((), jnp.float32))
    grad_coord = jnp.zeros_like(positions)
    span = BLOCK * width
    for layer in reversed(range(layers)):
        state_in, rims, weights = saved[layer]
        layer_fn = partial(mix_inputs, weights, valid)
        _, layer_pull = jax.vjp(layer_fn, state_in, positions, coord_low, coord_high, *rims)
        (
            grad_mix,
            grad_pos,
            gradient_position_lower_band,
            gradient_position_upper_band,
            grad_nown,
            grad_nlow,
            grad_nhigh,
        ) = layer_pull(grad_state)
        packed_low = jnp.concatenate(
            [grad_nlow.reshape(-1), gradient_position_lower_band.reshape(-1)]
        )
        packed_high = jnp.concatenate(
            [grad_nhigh.reshape(-1), gradient_position_upper_band.reshape(-1)]
        )
        from_after = shifted(packed_low.astype(jnp.bfloat16), "chain", -1).astype(packed_low.dtype)
        from_before = shifted(packed_high.astype(jnp.bfloat16), "chain", 1).astype(
            packed_high.dtype
        )
        grad_nown = (
            grad_nown
            + place_last(from_after[:span].reshape(BLOCK, width), atoms)
            + place_first(from_before[:span].reshape(BLOCK, width), atoms)
        )
        coordinate_following = from_after[span:].reshape(3, BLOCK)
        coord_before = from_before[span:].reshape(3, BLOCK)
        _, own_pull = jax.vjp(lambda inner: payload_inputs(inner, weights), state_in)
        (grad_own,) = own_pull(grad_nown.astype(jnp.bfloat16))
        grad_coord = (
            grad_coord
            + grad_pos
            + jnp.pad(coordinate_following, ((0, 0), (atoms - BLOCK, 0)))
            + jnp.pad(coord_before, ((0, 0), (0, atoms - BLOCK)))
        )
        grad_state = grad_mix + grad_own
    return (energy, -grad_coord)


def solution(mesh):
    return jax.shard_map(
        local,
        mesh=mesh,
        in_specs=(
            P(("frames", "chain")),
            P(None, ("frames", "chain")),
            P(("frames", "chain"), None),
            P(),
            P(),
            P(),
            P(),
            P(),
            P(),
            P(),
            P(),
            P(),
            P(),
            P(),
        ),
        out_specs=(P("frames"), P(None, ("frames", "chain"))),
        check_vma=False,
    )
```

profile of v0, /device:TPU:0, one launch (start us, length us, event | category | flops | bytes accessed | tf_op | source)
XLA Modules:
  0.0 241.2 jit_solution(14874150779433154821)
XLA Ops:
  1.4 2.3 collective-permute-start.2
  7.8 5.2 %collective-permute-start = (bf16[128,512]{1,0:T(8,128)(2,1)S(1)}, bf16[128,512]{1,0:T(8,128)(2,1)S(1)}, u32[]{:S(2)}, u32[]{:S(2)}) collective-permute-start(bf16[128,512]{1,0:T(8,128)(2,1)S(1)} %get-tuple-element.40), channel_id=1, source_target_pairs={{0,1},{1,2},{2,3},{3,4},{4,5},{5,6},{6,7},{7,8},{8,9},{9,10},{10,1... | collective-permute-start | bytes 393224 | tf_op jit(solution)/shard_map/ppermute | solution.py:16
  19.9 1.6 convolution_convert_fusion.11
  22.3 1.5 convolution_convert_fusion.10
  26.9 5.0 %fusion.301 = (f32[2,16,128]{2,1,0:T(8,128)S(1)}, f32[2,16,128,384]{3,2,1,0:T(8,128)}) fusion(f32[2,128,384]{2,1,0:T(8,128)S(1)} %fusion.62, f32[16]{0:T(128)S(1)} %get-tuple-element.64, pred[2,384]{1,0:T(4,128)(4,1)S(1)} %bitcast.297, bf16[2,128,16,32]{1,3,2,0:T(8,128)(2,1)S(1)} %copy.101, bf16[2,128,16,32]{1,3,2,0:T(8,128)(2,1)S(1)} %copy.100, ...), kind=kOutput, calls=%fused_computation.385 | convolution fusion | flops 112460160 | bytes 7750464 | tf_op jit(solution)/shard_map/sub | solution.py:57
  32.0 3.4 %divide_convert_fusion.1 = bf16[2,16,128,384]{3,2,1,0:T(8,128)(2,1)S(1)} fusion(f32[2,16,128,384]{3,2,1,0:T(8,128)} %get-tuple-element.68, f32[2,16,128]{2,1,0:T(8,128)S(1)} %get-tuple-element.67), kind=kLoop, calls=%fused_computation.23 | loop fusion | flops 3145728 | bytes 9453568 | tf_op jit(solution)/shard_map/convert_element_type | solution.py:58
  35.4 2.5 %fusion.66 = bf16[2,128,16,32]{1,3,2,0:T(8,128)(2,1)S(1)} fusion(bf16[2,384,16,32]{1,3,2,0:T(8,128)(2,1)} %copy_dynamic-update-slice_fusion.6, bf16[2,16,128,384]{3,2,1,0:T(8,128)(2,1)S(1)} %divide_convert_fusion.1), kind=kOutput, calls=%fused_computation.104 | convolution fusion | flops 100794368 | bytes 4194304 | tf_op jit(solution)/shard_map/bhqk,bkhd->bqhd/dot_general | solution.py:59
  44.0 4.3 %collective-permute-start.4 = (bf16[128,512]{1,0:T(8,128)(2,1)}, bf16[128,512]{1,0:T(8,128)(2,1)S(1)}, u32[]{:S(2)}, u32[]{:S(2)}) collective-permute-start(bf16[128,512]{1,0:T(8,128)(2,1)} %get-tuple-element.38), channel_id=1, source_target_pairs={{0,1},{1,2},{2,3},{3,4},{4,5},{5,6},{6,7},{7,8},{8,9},{9,10},{10,1... | collective-permute-start | bytes 393224 | tf_op jit(solution)/shard_map/ppermute | solution.py:16
  48.3 1.5 collective-permute-start.5
  50.4 2.6 %collective-permute-done.5 = bf16[128,512]{1,0:T(8,128)(2,1)S(1)} collective-permute-done((bf16[128,512]{1,0:T(8,128)(2,1)}, bf16[128,512]{1,0:T(8,128)(2,1)S(1)}, u32[]{:S(2)}, u32[]{:S(2)}) %collective-permute-start.5) | collective-permute-done | bytes 131104 | tf_op jit(solution)/shard_map/ppermute | solution.py:19
  53.0 1.6 convolution_convert_fusion.9
  55.5 1.8 copy.106
  57.3 1.7 concatenate.100
  59.0 1.8 copy.105
  60.8 1.7 concatenate.99
  62.5 1.8 copy.104
  64.3 1.7 concatenate.98
  66.0 1.7 convolution_convert_fusion.8
  68.7 1.8 copy.113
  70.5 1.7 concatenate.104
  72.2 1.8 copy.112
  74.0 1.7 concatenate.103
  75.7 1.8 copy.111
  77.5 1.7 concatenate.102
  79.3 1.8 copy_dynamic-update-slice_fusion.2
  81.0 1.7 copy_dynamic-update-slice_fusion.5
  82.7 1.7 copy_dynamic-update-slice_fusion.1
  84.4 1.7 copy_dynamic-update-slice_fusion
  86.1 6.2 %fusion.304 = (f32[2,16,128]{2,1,0:T(8,128)S(1)}, f32[2,16,128,384]{3,2,1,0:T(8,128)}) fusion(f32[16]{0:T(128)S(1)} %get-tuple-element.63, f32[2,128,384]{2,1,0:T(8,128)} %copy-done.28, pred[2,384]{1,0:T(4,128)(4,1)S(1)} %bitcast.298, bf16[2,384,16,32]{1,3,2,0:T(8,128)(2,1)} %copy_dynamic-update-slice_fusion, bf16[2,128,16,32]{1,0,3,2:T(2,128)(2,1)S(1)} %reshape.352), kind=kOutput, calls=%fused_computation.386 | convolution fusion | flops 110100864 | bytes 7750464 | tf_op jit(solution)/shard_map/sub | solution.py:57
  92.4 3.4 %divide_convert_fusion = bf16[2,16,128,384]{3,2,1,0:T(8,128)(2,1)S(1)} fusion(f32[2,16,128,384]{3,2,1,0:T(8,128)} %get-tuple-element.74, f32[2,16,128]{2,1,0:T(8,128)S(1)} %get-tuple-element.73), kind=kLoop, calls=%fused_computation.20 | loop fusion | flops 3145728 | bytes 9453568 | tf_op jit(solution)/shard_map/convert_element_type | solution.py:58
  100.4 4.2 %multiply_reduce_fusion.4 = (f32[256]{0:T(256)S(1)}, f32[256,512]{1,0:T(8,128)}) fusion(f32[256,512]{1,0:T(8,128)} %copy-done.5, f32[512]{0:T(512)S(1)} %bitcast.311, bf16[2,512,1024]{2,1,0:T(8,128)(2,1)} %param.22, f32[256,1024]{1,0:T(8,128)} %copy-done.24, bf16[2,1024,512]{2,1,0:T(8,128)(2,1)} %param.23, f32[256,512]{1,0:T(8,128)} %get-tuple-element.77, ...), kind=kOutput, calls=%fused_computation.192 | convolution fusion | flops 543555328 | bytes 4725760 | tf_op jit(solution)/shard_map/transpose(jvp())/dot_general | solution.py:69
  104.6 1.6 add_add_fusion.2
  110.3 2.7 %fusion.50 = f32[2,16,32,384]{3,2,1,0:T(8,128)S(1)} fusion(bf16[2,16,128,384]{3,2,1,0:T(8,128)(2,1)} %copy-done.2, bf16[2,16,32,128]{3,0,2,1:T(2,128)(2,1)S(1)} %bitcast.275), kind=kOutput, calls=%fused_computation.65 | convolution fusion | flops 101449728 | bytes 4980736 | tf_op jit(solution)/shard_map/transpose(jvp(bhqk,bkhd->bqhd))/dot_general | solution.py:59
  113.0 4.9 %fusion.6 = (f32[2,16,128]{2,1,0:T(8,128)S(1)}, bf16[2,16,128,384]{3,2,1,0:T(8,128)(2,1)S(1)}) fusion(f32[2,16,128,384]{3,2,1,0:T(8,128)} %get-tuple-element.74, f32[2,16,128]{2,1,0:T(8,128)S(1)} %multiply_divide_fusion.1, bf16[2,384,16,32]{1,3,2,0:T(8,128)(2,1)} %copy-done.11, bf16[2,16,32,128]{3,0,2,1:T(2,128)(2,1)S(1)} %bitcast.276), kind=kOutput, calls=%fused_computation.10 | convolution fusion | flops 108523520 | bytes 10518528 | tf_op jit(solution)/shard_map/transpose(jvp(bhqk,bkhd->bqhd))/dot_general | solution.py:59
  117.9 3.1 %multiply_reduce_fusion.1 = (f32[2,128,384]{2,1,0:T(8,128)}, f32[2,16,128,384]{3,2,1,0:T(8,128)S(1)}) fusion(f32[16]{0:T(128)S(1)} %get-tuple-element.63, f32[2,16,128,384]{3,2,1,0:T(8,128)S(1)} %bitcast.271, f32[2,16,128]{2,1,0:T(8,128)S(1)} %neg.27, f32[2,16,128]{2,1,0:T(8,128)S(1)} %get-tuple-element.73, ...), kind=kLoop, calls=%fused_computation.19 | loop fusion | flops 12484608 | bytes 16155456 | tf_op jit(solution)/shard_map/transpose(jvp())/reduce_sum | solution.py:53
  121.0 3.1 %fusion.63 = bf16[2,128,16,32]{1,3,2,0:T(8,128)(2,1)} fusion(bf16[2,384,16,32]{1,3,2,0:T(8,128)(2,1)} %copy_dynamic-update-slice_fusion, f32[2,16,128,384]{3,2,1,0:T(8,128)S(1)} %get-tuple-element.9), kind=kOutput, calls=%fused_computation.103 | convolution fusion | flops 102367232 | bytes 7340032 | tf_op jit(solution)/shard_map/transpose(jvp(bqhd,bkhd->bhqk))/dot_general | solution.py:46
  124.1 1.8 fusion.40
  127.2 2.1 copy.144
  129.2 2.0 copy.145
  131.2 2.0 copy.146
  135.3 2.6 %fusion.289 = (f32[2,128,512]{1,2,0:T(8,128)}, f32[2,128,512]{1,2,0:T(8,128)}, f32[2,128,512]{1,2,0:T(8,128)}) fusion(f32[2,384,512]{1,2,0:T(8,128)} %bitcast.274), kind=kLoop, calls=%fused_computation.373 | loop fusion | bytes 3145728 | tf_op jit(solution)/shard_map/transpose(jvp())/split | solution.py:36
  138.0 2.0 copy.147
  140.0 2.0 copy.148
  142.0 2.1 copy.149
  144.1 1.5 add_convert_fusion.2
  145.6 1.5 convolution_convert_fusion.6
  147.2 1.5 add_convert_fusion.3
  148.6 1.5 fusion.51
  151.0 5.4 %collective-permute-start.7 = (bf16[65920]{0:T(1024)(128)(2,1)}, bf16[65920]{0:T(1024)(128)(2,1)S(1)}, u32[]{:S(2)}, u32[]{:S(2)}) collective-permute-start(bf16[65920]{0:T(1024)(128)(2,1)} %pad_maximum_fusion.13), channel_id=1, source_target_pairs={{0,1},{1,2},{2,3},{3,4},{4,5},{5,6},{6,7},{7,8},{8,9},{9,10},{10,1... | collective-permute-start | bytes 395528 | tf_op jit(solution)/shard_map/ppermute | solution.py:27
  157.1 1.5 collective-permute-start.6
  160.6 34.1 %psum.7 = f32[1]{0:T(128)} all-reduce(f32[1]{0:T(128)} %bitcast.22), channel_id=1, replica_groups=mesh['frames'=2,'chain'=16] {'chain'}, use_global_device_ids=true, to_apply=%region_11.12 | all-reduce | flops 1 | bytes 8 | tf_op jit(solution)/shard_map/psum | solution.py:163
  195.2 1.9 copy.131
  197.9 1.7 reshape.362
  200.4 1.7 reshape.363
  202.1 2.6 %multiply_reduce_fusion.3 = (f32[256]{0:T(256)S(1)}, bf16[256,512]{1,0:T(8,128)(2,1)}) fusion(f32[256,512]{1,0:T(8,128)} %copy-done.6, f32[512]{0:T(512)} %bitcast.294, f32[128,512]{1,0:T(8,128)} %reshape.363, f32[128,512]{1,0:T(8,128)} %reshape.362, bf16[2,512,512]{2,1,0:T(8,128)(2,1)} %param.18, bf16[64,8,2,128]{3,2,1,0:T(2,128)(2,1)} %bitcast.290, ...), kind=kOutput, calls=%fused_computation.189 | convolution fusion | flops 135659264 | bytes 2362368 | tf_op jit(solution)/shard_map/transpose(jvp())/dot_general | solution.py:82
  205.3 4.5 %multiply_reduce_fusion.2 = (f32[256]{0:T(256)S(1)}, f32[256,512]{1,0:T(8,128)}) fusion(f32[256,512]{1,0:T(8,128)} %copy-done.9, f32[512]{0:T(512)} %bitcast.309, bf16[2,512,1024]{2,1,0:T(8,128)(2,1)} %param.22, f32[256,1024]{1,0:T(8,128)} %copy-done.23, bf16[2,1024,512]{2,1,0:T(8,128)(2,1)} %param.23, f32[256,512]{1,0:T(8,128)} %copy-done.8, ...), kind=kOutput, calls=%fused_computation.186 | convolution fusion | flops 543948544 | bytes 5512192 | tf_op jit(solution)/shard_map/transpose(jvp())/dot_general | solution.py:69
  209.9 2.2 convolution_convert_fusion.21
  214.7 5.1 %fusion.11 = (f32[2,16,128]{2,1,0:T(8,128)S(1)}, bf16[2,16,128,384]{3,2,1,0:T(8,128)(2,1)S(1)}) fusion(f32[2,16,128,384]{3,2,1,0:T(8,128)} %get-tuple-element.68, f32[2,16,128]{2,1,0:T(8,128)S(1)} %copy-done.36, bf16[2,384,16,32]{1,3,2,0:T(8,128)(2,1)} %copy_dynamic-update-slice_fusion.6, bf16[2,16,32,128]{3,0,2,1:T(2,128)(2,1)S(1)} %bitcast.278), kind=kOutput, calls=%fused_computation.15 | convolution fusion | flops 108523520 | bytes 10518528 | tf_op jit(solution)/shard_map/transpose(jvp(bhqk,bkhd->bqhd))/dot_general | solution.py:59
  219.9 2.3 multiply_reduce_fusion
  222.2 3.2 %fusion.46 = f32[2,16,384,32]{2,3,1,0:T(8,128)} fusion(bf16[2,128,16,32]{1,0,3,2:T(2,128)(2,1)S(1)} %copy-done.30, f32[2,16,128,384]{3,2,1,0:T(8,128)S(1)} %bitcast.269, bf16[2,16,128,384]{3,2,1,0:T(8,128)(2,1)S(1)} %get-tuple-element.87, f32[2,16,128]{2,1,0:T(8,128)S(1)} %neg.30, f32[2,16,128]{2,1,0:T(8,128)S(1)} %copy-done.32, ...), kind=kOutput, calls=%fused_computation.61 | convolution fusion | flops 110886912 | bytes 11305728 | tf_op jit(solution)/shard_map/transpose(jvp(bqhd,bkhd->bhqk))/dot_general | solution.py:46
  226.7 2.3 fusion.287
  232.6 1.5 convolution_convert_fusion.4
  234.3 1.5 fusion.52
  238.7 1.9 collective-permute-done.8
  (267 shorter events, 52.6 us)
Async XLA Ops:
  0.6 5.2 %copy-start = (bf16[128,512]{1,0:T(8,128)(2,1)S(1)}, bf16[128,512]{1,0:T(8,128)(2,1)}, u32[]{:S(2)}) copy-start(bf16[128,512]{1,0:T(8,128)(2,1)} %param.17) | copy-start | bytes 393220
  1.4 17.6 %collective-permute-start.2 = (f32[3,128]{1,0:T(4,128)S(1)}, f32[3,128]{1,0:T(4,128)S(1)}, u32[]{:S(2)}, u32[]{:S(2)}) collective-permute-start(f32[3,128]{1,0:T(4,128)S(1)} %get-tuple-element.59), channel_id=1, source_target_pairs={{0,1},{1,2},{2,3},{3,4},{4,5},{5,6},{6,7},{7,8},{8,9},{9,10},{10,1... | collective-permute-start | bytes 4616 | tf_op jit(solution)/shard_map/ppermute | solution.py:16
  3.7 15.2 %collective-permute-start.3 = (f32[3,128]{1,0:T(4,128)S(1)}, f32[3,128]{1,0:T(4,128)S(1)}, u32[]{:S(2)}, u32[]{:S(2)}) collective-permute-start(f32[3,128]{1,0:T(4,128)S(1)} %get-tuple-element.60), channel_id=1, source_target_pairs={{1,0},{2,1},{3,2},{4,3},{5,4},{6,5},{7,6},{8,7},{9,8},{10,9},{11,1... | collective-permute-start | bytes 4616 | tf_op jit(solution)/shard_map/ppermute | solution.py:19
  5.8 32.8 %copy-start.52 = (f32[1,1,512]{2,1,0:T(1,128)}, f32[1,1,512]{2,1,0:T(1,128)S(1)}, u32[]{:S(2)}) copy-start(f32[1,1,512]{2,1,0:T(1,128)S(1)} %get-tuple-element.49) | copy-start | bytes 6148
  5.8 34.0 %copy-start.40 = (f32[1,1,512]{2,1,0:T(1,128)}, f32[1,1,512]{2,1,0:T(1,128)S(1)}, u32[]{:S(2)}) copy-start(f32[1,1,512]{2,1,0:T(1,128)S(1)} %get-tuple-element.51) | copy-start | bytes 6148
  7.8 12.1 %collective-permute-start = (bf16[128,512]{1,0:T(8,128)(2,1)S(1)}, bf16[128,512]{1,0:T(8,128)(2,1)S(1)}, u32[]{:S(2)}, u32[]{:S(2)}) collective-permute-start(bf16[128,512]{1,0:T(8,128)(2,1)S(1)} %get-tuple-element.40), channel_id=1, source_target_pairs={{0,1},{1,2},{2,3},{3,4},{4,5},{5,6},{6,7},{7,8},{8,9},{9,10},{10,1... | collective-permute-start | bytes 393224 | tf_op jit(solution)/shard_map/ppermute | solution.py:16
  13.0 6.9 %collective-permute-start.1 = (bf16[128,512]{1,0:T(8,128)(2,1)S(1)}, bf16[128,512]{1,0:T(8,128)(2,1)S(1)}, u32[]{:S(2)}, u32[]{:S(2)}) collective-permute-start(bf16[128,512]{1,0:T(8,128)(2,1)S(1)} %get-tuple-element.41), channel_id=1, source_target_pairs={{1,0},{2,1},{3,2},{4,3},{5,4},{6,5},{7,6},{8,7},{9,8},{10,9},{11,1... | collective-permute-start | bytes 393224 | tf_op jit(solution)/shard_map/ppermute | solution.py:19
  15.1 11.8 %copy-start.54 = (f32[16]{0:T(128)}, f32[16]{0:T(128)S(1)}, u32[]{:S(2)}) copy-start(f32[16]{0:T(128)S(1)} %get-tuple-element.64) | copy-start | bytes 196
  18.0 116.3 %copy-start.37 = (f32[3,2,128]{2,1,0:T(2,128)}, f32[3,2,128]{2,1,0:T(2,128)S(1)}, u32[]{:S(2)}) copy-start(f32[3,2,128]{2,1,0:T(2,128)S(1)} %sub.27) | copy-start | bytes 9220
  18.0 99.9 %copy-start.42 = (pred[1,2,3,128]{3,1,2,0:T(4,128)(4,1)}, pred[1,2,3,128]{3,1,2,0:T(4,128)(4,1)S(1)}, u32[]{:S(2)}) copy-start(pred[1,2,3,128]{3,1,2,0:T(4,128)(4,1)S(1)} %copy.238) | copy-start | bytes 2308
  18.2 8.7 %copy-start.29 = (bf16[2,128,16,32]{1,0,3,2:T(2,128)(2,1)}, bf16[2,128,16,32]{1,0,3,2:T(2,128)(2,1)S(1)}, u32[]{:S(2)}) copy-start(bf16[2,128,16,32]{1,0,3,2:T(2,128)(2,1)S(1)} %reshape.350) | copy-start | bytes 786436
  19.7 114.6 %copy-start.33 = (f32[3,2,384]{2,1,0:T(2,128)}, f32[3,2,384]{2,1,0:T(2,128)S(1)}, u32[]{:S(2)}) copy-start(f32[3,2,384]{2,1,0:T(2,128)S(1)} %pad_maximum_fusion.16) | copy-start | bytes 27652
  19.9 7.0 %copy-start.28 = (f32[2,128,384]{2,1,0:T(8,128)}, f32[2,128,384]{2,1,0:T(8,128)S(1)}, u32[]{:S(2)}) copy-start(f32[2,128,384]{2,1,0:T(8,128)S(1)} %fusion.62) | copy-start | bytes 1179652
  32.0 17.8 %copy-start.31 = (f32[2,16,128]{2,1,0:T(8,128)}, f32[2,16,128]{2,1,0:T(8,128)S(1)}, u32[]{:S(2)}) copy-start(f32[2,16,128]{2,1,0:T(8,128)S(1)} %get-tuple-element.67) | copy-start | bytes 49156
  32.0 6.2 %copy-start.4 = (f32[256,512]{1,0:T(8,128)S(1)}, f32[256,512]{1,0:T(8,128)}, u32[]{:S(2)}) copy-start(f32[256,512]{1,0:T(8,128)} %copy-done.3) | copy-start | bytes 1572868
  32.0 6.2 %copy-start.12 = (bf16[2,512,512]{2,1,0:T(8,128)(2,1)S(1)}, bf16[2,512,512]{2,1,0:T(8,128)(2,1)}, u32[]{:S(2)}) copy-start(bf16[2,512,512]{2,1,0:T(8,128)(2,1)} %param.21) | copy-start | bytes 3145732
  32.0 6.7 %copy-start.15 = (bf16[2,512,1024]{2,1,0:T(8,128)(2,1)S(1)}, bf16[2,512,1024]{2,1,0:T(8,128)(2,1)}, u32[]{:S(2)}) copy-start(bf16[2,512,1024]{2,1,0:T(8,128)(2,1)} %param.22) | copy-start | bytes 6291460
  35.3 3.8 %copy-start.56 = (bf16[2,1024,512]{2,1,0:T(8,128)(2,1)S(1)}, bf16[2,1024,512]{2,1,0:T(8,128)(2,1)}, u32[]{:S(2)}) copy-start(bf16[2,1024,512]{2,1,0:T(8,128)(2,1)} %param.23) | copy-start | bytes 6291460
  35.3 5.3 %copy-start.58 = (bf16[2,512,512]{2,1,0:T(8,128)(2,1)S(1)}, bf16[2,512,512]{2,1,0:T(8,128)(2,1)}, u32[]{:S(2)}) copy-start(bf16[2,512,512]{2,1,0:T(8,128)(2,1)} %param.18) | copy-start | bytes 3145732
  38.6 16.0 %copy-start.46 = (f32[256]{0:T(256)}, f32[256]{0:T(256)S(1)}, u32[]{:S(2)}) copy-start(f32[256]{0:T(256)S(1)} %fusion.241) | copy-start | bytes 3076
  39.8 28.0 %copy-start.53 = (f32[256]{0:T(256)}, f32[256]{0:T(256)S(1)}, u32[]{:S(2)}) copy-start(f32[256]{0:T(256)S(1)} %get-tuple-element.71) | copy-start | bytes 3076
  39.8 28.0 %copy-start.48 = (f32[256]{0:T(256)}, f32[256]{0:T(256)S(1)}, u32[]{:S(2)}) copy-start(f32[256]{0:T(256)S(1)} %fusion.242) | copy-start | bytes 3076
  44.0 42.1 %copy-start.21 = (bf16[2,128,16,32]{1,0,3,2:T(2,128)(2,1)}, bf16[2,128,16,32]{1,0,3,2:T(2,128)(2,1)S(1)}, u32[]{:S(2)}) copy-start(bf16[2,128,16,32]{1,0,3,2:T(2,128)(2,1)S(1)} %reshape.352) | copy-start | bytes 786436
  44.0 6.4 %collective-permute-start.4 = (bf16[128,512]{1,0:T(8,128)(2,1)}, bf16[128,512]{1,0:T(8,128)(2,1)S(1)}, u32[]{:S(2)}, u32[]{:S(2)}) collective-permute-start(bf16[128,512]{1,0:T(8,128)(2,1)} %get-tuple-element.38), channel_id=1, source_target_pairs={{0,1},{1,2},{2,3},{3,4},{4,5},{5,6},{6,7},{7,8},{8,9},{9,10},{10,1... | collective-permute-start | bytes 393224 | tf_op jit(solution)/shard_map/ppermute | solution.py:16
  48.3 4.7 %collective-permute-start.5 = (bf16[128,512]{1,0:T(8,128)(2,1)}, bf16[128,512]{1,0:T(8,128)(2,1)S(1)}, u32[]{:S(2)}, u32[]{:S(2)}) collective-permute-start(bf16[128,512]{1,0:T(8,128)(2,1)} %get-tuple-element.39), channel_id=1, source_target_pairs={{1,0},{2,1},{3,2},{4,3},{5,4},{6,5},{7,6},{8,7},{9,8},{10,9},{11,1... | collective-permute-start | bytes 393224 | tf_op jit(solution)/shard_map/ppermute | solution.py:19
  50.4 5.1 %copy-start.59 = (bf16[128,512]{1,0:T(8,128)(2,1)}, bf16[128,512]{1,0:T(8,128)(2,1)S(1)}, u32[]{:S(2)}) copy-start(bf16[128,512]{1,0:T(8,128)(2,1)S(1)} %collective-permute-done.4) | copy-start | bytes 393220
  92.4 3.4 %copy-start.10 = (bf16[2,384,16,32]{1,3,2,0:T(8,128)(2,1)S(1)}, bf16[2,384,16,32]{1,3,2,0:T(8,128)(2,1)}, u32[]{:S(2)}) copy-start(bf16[2,384,16,32]{1,3,2,0:T(8,128)(2,1)} %copy_dynamic-update-slice_fusion.5) | copy-start | bytes 2359300
  92.4 3.4 %copy-start.26 = (bf16[2,128,16,32]{1,0,3,2:T(2,128)(2,1)S(1)}, bf16[2,128,16,32]{1,0,3,2:T(2,128)(2,1)}, u32[]{:S(2)}) copy-start(bf16[2,128,16,32]{1,0,3,2:T(2,128)(2,1)} %concatenate.99) | copy-start | bytes 786436
  92.4 3.5 %copy-start.25 = (bf16[2,128,16,32]{1,0,3,2:T(2,128)(2,1)S(1)}, bf16[2,128,16,32]{1,0,3,2:T(2,128)(2,1)}, u32[]{:S(2)}) copy-start(bf16[2,128,16,32]{1,0,3,2:T(2,128)(2,1)} %concatenate.100) | copy-start | bytes 786436
  92.4 5.1 %copy-start.7 = (f32[256,512]{1,0:T(8,128)S(1)}, f32[256,512]{1,0:T(8,128)}, u32[]{:S(2)}) copy-start(f32[256,512]{1,0:T(8,128)} %copy-done.6) | copy-start | bytes 1572868
  92.4 5.1 %copy-start.13 = (bf16[2,512,512]{2,1,0:T(8,128)(2,1)S(1)}, bf16[2,512,512]{2,1,0:T(8,128)(2,1)}, u32[]{:S(2)}) copy-start(bf16[2,512,512]{2,1,0:T(8,128)(2,1)} %param.21) | copy-start | bytes 3145732
  92.4 5.6 %copy-start.16 = (bf16[2,512,1024]{2,1,0:T(8,128)(2,1)S(1)}, bf16[2,512,1024]{2,1,0:T(8,128)(2,1)}, u32[]{:S(2)}) copy-start(bf16[2,512,1024]{2,1,0:T(8,128)(2,1)} %param.22) | copy-start | bytes 6291460
  95.8 4.5 %copy-start.2 = (bf16[2,16,128,384]{3,2,1,0:T(8,128)(2,1)}, bf16[2,16,128,384]{3,2,1,0:T(8,128)(2,1)S(1)}, u32[]{:S(2)}) copy-start(bf16[2,16,128,384]{3,2,1,0:T(8,128)(2,1)S(1)} %divide_convert_fusion) | copy-start | bytes 9437188
  95.8 3.2 %copy-start.57 = (bf16[2,1024,512]{2,1,0:T(8,128)(2,1)S(1)}, bf16[2,1024,512]{2,1,0:T(8,128)(2,1)}, u32[]{:S(2)}) copy-start(bf16[2,1024,512]{2,1,0:T(8,128)(2,1)} %param.23) | copy-start | bytes 6291460
  96.0 4.3 %copy-start.11 = (bf16[2,384,16,32]{1,3,2,0:T(8,128)(2,1)}, bf16[2,384,16,32]{1,3,2,0:T(8,128)(2,1)S(1)}, u32[]{:S(2)}) copy-start(bf16[2,384,16,32]{1,3,2,0:T(8,128)(2,1)S(1)} %copy_dynamic-update-slice_fusion.3) | copy-start | bytes 2359300
  100.4 8.0 %copy-start.45 = (f32[256]{0:T(256)}, f32[256]{0:T(256)S(1)}, u32[]{:S(2)}) copy-start(f32[256]{0:T(256)S(1)} %get-tuple-element.62) | copy-start | bytes 3076
  110.3 7.6 %slice-start.2 = ((s8[6291456]{0:T(1024)(128)(4,1)}), s8[4194304]{0:T(1024)(128)(4,1)S(1)}, s32[]{:S(2)}) async-start(s8[6291456]{0:T(1024)(128)(4,1)} %bitcast.270), calls=%async_computation.2 | async-start | bytes 8388608
  113.0 4.9 %slice-start.3 = ((s8[6291456]{0:T(1024)(128)(4,1)}), s8[2097152]{0:T(1024)(128)(4,1)S(1)}, s32[]{:S(2)}) async-start(s8[6291456]{0:T(1024)(128)(4,1)} %bitcast.270), calls=%async_computation.3 | async-start | bytes 4194304
  121.0 3.1 %copy-start.22 = (bf16[2,128,16,32]{1,0,3,2:T(2,128)(2,1)S(1)}, bf16[2,128,16,32]{1,0,3,2:T(2,128)(2,1)}, u32[]{:S(2)}) copy-start(bf16[2,128,16,32]{1,0,3,2:T(2,128)(2,1)} %copy-done.21) | copy-start | bytes 786436
  144.1 14.5 %copy-start.14 = (f32[256,512]{1,0:T(8,128)S(1)}, f32[256,512]{1,0:T(8,128)}, u32[]{:S(2)}) copy-start(f32[256,512]{1,0:T(8,128)} %get-tuple-element.77) | copy-start | bytes 1572868
  150.1 9.8 %copy-start.35 = (bf16[512,512]{1,0:T(8,128)(2,1)}, bf16[512,512]{1,0:T(8,128)(2,1)S(1)}, u32[]{:S(2)}) copy-start(bf16[512,512]{1,0:T(8,128)(2,1)S(1)} %fusion.51) | copy-start | bytes 1572868
  151.0 48.6 %collective-permute-start.7 = (bf16[65920]{0:T(1024)(128)(2,1)}, bf16[65920]{0:T(1024)(128)(2,1)S(1)}, u32[]{:S(2)}, u32[]{:S(2)}) collective-permute-start(bf16[65920]{0:T(1024)(128)(2,1)} %pad_maximum_fusion.13), channel_id=1, source_target_pairs={{0,1},{1,2},{2,3},{3,4},{4,5},{5,6},{6,7},{7,8},{8,9},{9,10},{10,1... | collective-permute-start | bytes 395528 | tf_op jit(solution)/shard_map/ppermute | solution.py:27
  157.1 40.0 %collective-permute-start.6 = (bf16[65920]{0:T(1024)(128)(2,1)}, bf16[65920]{0:T(1024)(128)(2,1)S(1)}, u32[]{:S(2)}, u32[]{:S(2)}) collective-permute-start(bf16[65920]{0:T(1024)(128)(2,1)} %pad_maximum_fusion.12), channel_id=1, source_target_pairs={{1,0},{2,1},{3,2},{4,3},{5,4},{6,5},{7,6},{8,7},{9,8},{10,9},{11,1... | collective-permute-start | bytes 395528 | tf_op jit(solution)/shard_map/ppermute | solution.py:27
  197.2 12.7 %copy-start.19 = (bf16[65920]{0:T(1024)(128)(2,1)}, bf16[65920]{0:T(1024)(128)(2,1)S(1)}, u32[]{:S(2)}) copy-start(bf16[65920]{0:T(1024)(128)(2,1)S(1)} %collective-permute-done.6) | copy-start | bytes 395524
  199.6 10.2 %copy-start.17 = (bf16[65920]{0:T(1024)(128)(2,1)}, bf16[65920]{0:T(1024)(128)(2,1)S(1)}, u32[]{:S(2)}) copy-start(bf16[65920]{0:T(1024)(128)(2,1)S(1)} %collective-permute-done.7) | copy-start | bytes 395524
  202.1 7.8 %copy-start.51 = (f32[256]{0:T(256)S(1)}, f32[256]{0:T(256)}, u32[]{:S(2)}) copy-start(f32[256]{0:T(256)} %copy-done.50) | copy-start | bytes 3076
  202.1 7.8 %copy-start.41 = (f32[1,1,512]{2,1,0:T(1,128)S(1)}, f32[1,1,512]{2,1,0:T(1,128)}, u32[]{:S(2)}) copy-start(f32[1,1,512]{2,1,0:T(1,128)} %copy-done.40) | copy-start | bytes 6148
  202.1 7.8 %copy-start.47 = (f32[256]{0:T(256)S(1)}, f32[256]{0:T(256)}, u32[]{:S(2)}) copy-start(f32[256]{0:T(256)} %copy-done.46) | copy-start | bytes 3076
  202.1 7.8 %copy-start.49 = (f32[256]{0:T(256)S(1)}, f32[256]{0:T(256)}, u32[]{:S(2)}) copy-start(f32[256]{0:T(256)} %copy-done.48) | copy-start | bytes 3076
  209.8 4.8 %copy-start.36 = (f32[2,16,128]{2,1,0:T(8,128)S(1)}, f32[2,16,128]{2,1,0:T(8,128)}, u32[]{:S(2)}) copy-start(f32[2,16,128]{2,1,0:T(8,128)} %multiply_divide_fusion) | copy-start | bytes 49156
  214.0 5.8 %slice-start = ((s8[6291456]{0:T(1024)(128)(4,1)}), s8[4194304]{0:T(1024)(128)(4,1)S(1)}, s32[]{:S(2)}) async-start(s8[6291456]{0:T(1024)(128)(4,1)} %bitcast.268), calls=%async_computation | async-start | bytes 8388608
  214.6 5.2 %slice-start.1 = ((s8[6291456]{0:T(1024)(128)(4,1)}), s8[2097152]{0:T(1024)(128)(4,1)S(1)}, s32[]{:S(2)}) async-start(s8[6291456]{0:T(1024)(128)(4,1)} %bitcast.268), calls=%async_computation.1 | async-start | bytes 4194304
  214.7 5.2 %copy-start.32 = (f32[2,16,128]{2,1,0:T(8,128)S(1)}, f32[2,16,128]{2,1,0:T(8,128)}, u32[]{:S(2)}) copy-start(f32[2,16,128]{2,1,0:T(8,128)} %copy-done.31) | copy-start | bytes 49156
  214.7 5.2 %copy-start.43 = (pred[1,2,3,128]{3,1,2,0:T(4,128)(4,1)S(1)}, pred[1,2,3,128]{3,1,2,0:T(4,128)(4,1)}, u32[]{:S(2)}) copy-start(pred[1,2,3,128]{3,1,2,0:T(4,128)(4,1)} %copy-done.42) | copy-start | bytes 2308
  214.7 5.2 %copy-start.55 = (f32[16]{0:T(128)S(1)}, f32[16]{0:T(128)}, u32[]{:S(2)}) copy-start(f32[16]{0:T(128)} %copy-done.54) | copy-start | bytes 196
  222.2 3.3 %copy-start.34 = (f32[3,2,384]{2,1,0:T(2,128)S(1)}, f32[3,2,384]{2,1,0:T(2,128)}, u32[]{:S(2)}) copy-start(f32[3,2,384]{2,1,0:T(2,128)} %copy-done.33) | copy-start | bytes 27652
  222.2 3.3 %copy-start.38 = (f32[3,2,128]{2,1,0:T(2,128)S(1)}, f32[3,2,128]{2,1,0:T(2,128)}, u32[]{:S(2)}) copy-start(f32[3,2,128]{2,1,0:T(2,128)} %copy-done.37) | copy-start | bytes 9220
  222.2 3.7 %copy-start.20 = (bf16[65920]{0:T(1024)(128)(2,1)S(1)}, bf16[65920]{0:T(1024)(128)(2,1)}, u32[]{:S(2)}) copy-start(bf16[65920]{0:T(1024)(128)(2,1)} %copy-done.19) | copy-start | bytes 395524
  229.0 9.6 %copy-start.18 = (bf16[65920]{0:T(1024)(128)(2,1)S(1)}, bf16[65920]{0:T(1024)(128)(2,1)}, u32[]{:S(2)}) copy-start(bf16[65920]{0:T(1024)(128)(2,1)} %copy-done.17) | copy-start | bytes 395524
  229.0 12.2 %copy-start.1 = (bf16[128,512]{1,0:T(8,128)(2,1)S(1)}, bf16[128,512]{1,0:T(8,128)(2,1)}, u32[]{:S(2)}) copy-start(bf16[128,512]{1,0:T(8,128)(2,1)} %param.17) | copy-start | bytes 393220
  230.3 10.3 %copy-start.39 = (f32[1,3,4,128]{3,1,2,0:T(4,128)S(1)}, f32[1,3,4,128]{3,1,2,0:T(4,128)}, u32[]{:S(2)}) copy-start(f32[1,3,4,128]{3,1,2,0:T(4,128)} %copy.237) | copy-start | bytes 18436
  230.3 10.3 %copy-start.44 = (f32[3,2,128]{2,1,0:T(2,128)S(1)}, f32[3,2,128]{2,1,0:T(2,128)}, u32[]{:S(2)}) copy-start(f32[3,2,128]{2,1,0:T(2,128)} %get-tuple-element.6) | copy-start | bytes 9220
  236.0 2.7 %collective-permute-start.9 = (bf16[65920]{0:T(1024)(128)(2,1)S(1)}, bf16[65920]{0:T(1024)(128)(2,1)S(1)}, u32[]{:S(2)}, u32[]{:S(2)}) collective-permute-start(bf16[65920]{0:T(1024)(128)(2,1)S(1)} %pad_maximum_fusion.15), channel_id=1, source_target_pairs={{0,1},{1,2},{2,3},{3,4},{4,5},{5,6},{6,7},{7,8},{8,9},{9,10},{10,1... | collective-permute-start | bytes 395528 | tf_op jit(solution)/shard_map/ppermute | solution.py:27
  237.3 3.2 %collective-permute-start.8 = (bf16[65920]{0:T(1024)(128)(2,1)S(1)}, bf16[65920]{0:T(1024)(128)(2,1)S(1)}, u32[]{:S(2)}, u32[]{:S(2)}) collective-permute-start(bf16[65920]{0:T(1024)(128)(2,1)S(1)} %pad_maximum_fusion.14), channel_id=1, source_target_pairs={{1,0},{2,1},{3,2},{4,3},{5,4},{6,5},{7,6},{8,7},{9,8},{10,9},{11,1... | collective-permute-start | bytes 395528 | tf_op jit(solution)/shard_map/ppermute | solution.py:27
  (11 other events, 17.0 us)
where the time goes:
time: 244 us; the launch traced here: 241 us
  local copies, waits for them, and re-layouts  76.6 us (31%)
  matrix products  71.5 us (29%)
  blocking collectives  34.1 us (14%)
  other arithmetic  27 us (11%)
  starting transfers between devices  25.4 us (10%)
  waiting for transfers between devices  4.48 us (2%)
    psum x1, blocking collectives, local(): energy = lax.psum(local_total, 'chain').reshape(1)  34.1 us
    unnamed x160, local copies, waits for them, and re-layouts  26.6 us
    dot_general x6, matrix products, attend(): jnp.einsum('bhqk,bkhd->bqhd', probs, value_win, preferred_element_type=jn...  17 us
    slice x16, local copies, waits for them, and re-layouts, windows(): return jnp.concatenate([blocks[:-2], blocks[1:-1], blocks[2:]], axis=1)  13.5 us
    concatenate x18, local copies, waits for them, and re-layouts, windows(): return jnp.concatenate([blocks[:-2], blocks[1:-1], blocks[2:]], axis=1)  13.4 us
    ppermute x3, starting transfers between devices, padded(): lax.ppermute(lax.slice_in_dim(block, block.shape[dim] - width, None, axis...  11.8 us
    sub x2, matrix products, attend(): expo = jnp.exp(scores - peak)  11.2 us
    dot_general x4, matrix products, finish(): jnp.dot(inner, weights[4], preferred_element_type=jnp.float32)  9.74 us
  transfers between devices with their start and end apart: 10, of which 2 were waited for; matrix products, arithmetic and copies ran while one was open for 6% of the time, Pallas kernels for 0%

commit v1 on v0

v1 whole, which is shorter than its diff:
```python
import functools
import math

import jax
import jax.numpy as jnp
from jax import lax
from jax.experimental import pallas as pl
from jax.experimental.pallas import tpu as pltpu
from jax.sharding import PartitionSpec as P

BLK = 128
LANES = 128
EPS = 1e-06
LOG2E = math.log2(math.e)
LN2 = math.log(2.0)
FAR = 1e30
F32 = jnp.float32
BF16 = jnp.bfloat16
C0 = math.sqrt(2.0 / math.pi)
C1 = 0.044715


def mm(a, b):
    return jnp.dot(a, b, preferred_element_type=F32)


def mm_nt(a, b):
    return lax.dot_general(a, b, (((1,), (1,)), ((), ())), preferred_element_type=F32)


def mm_tn(a, b):
    return lax.dot_general(a, b, (((0,), (0,)), ((), ())), preferred_element_type=F32)


def inv_rms(x):
    return lax.rsqrt(jnp.mean(x * x, axis=-1, keepdims=True) + EPS)


def rms_back(x, gain, cot):
    r = inv_rms(x)
    t = cot * gain
    return r * (t - x * (r * r * jnp.mean(x * t, axis=-1, keepdims=True)))


def gelu_both(x):
    t = jnp.tanh(C0 * (x + C1 * x * x * x))
    half = 0.5 * (1.0 + t)
    return x * half, half + 0.5 * x * (1.0 - t * t) * (C0 + 3.0 * C0 * C1 * x * x)


def head_masks(rows, heads_per_group, hdim):
    lane = lax.broadcasted_iota(jnp.int32, (rows, LANES), 1) // hdim
    return [(lane == h).astype(F32).astype(BF16) for h in range(heads_per_group)]


def arrange(par, own, from_a, from_b):
    before = jnp.where(par == 0, from_b, from_a)
    after = jnp.where(par == 0, from_a, from_b)
    return before, own, after


def distances(ext, ext_t, first, d2_ref, count):
    for i in range(count):
        q = ext_t[(first + i) * BLK : (first + i + 1) * BLK]
        for s in range(3):
            k0 = (first + i - 1 + s) * BLK
            tot = None
            for c in range(3):
                diff = q[:, c : c + 1] - ext[c : c + 1, k0 : k0 + BLK]
                tot = diff * diff if tot is None else tot + diff * diff
            d2_ref[i, :, s * BLK : (s + 1) * BLK] = jnp.where(q[:, 4 + s : 5 + s] > 0.5, tot, FAR)


def attend(q_ref, k_ref, v_ref, o_ref, rl_ref, e_ref, d2_ref, d2_first, gam_ref, layer, heads, hdim, count):
    per = LANES // hdim
    groups = heads // per
    mask = head_masks(BLK, per, hdim)
    mask3 = head_masks(3 * BLK, per, hdim)
    for i in range(count):
        for g in range(groups):
            cols = slice(g * LANES, (g + 1) * LANES)
            q = q_ref[i * BLK : (i + 1) * BLK, cols]
            k = k_ref[i * BLK : (i + 3) * BLK, cols]
            v = v_ref[i * BLK : (i + 3) * BLK, cols]
            qs = jnp.concatenate([q * m for m in mask], axis=0)
            scores = mm_nt(qs, k)
            d2 = d2_ref[d2_first + i]
            parts = []
            for h in range(per):
                gam = gam_ref[layer, g * per + h] * LOG2E
                s = scores[h * BLK : (h + 1) * BLK] - gam * d2
                e = jnp.exp2(s - jnp.max(s, axis=1, keepdims=True)).astype(BF16)
                e_ref[i, g * per + h] = e
                parts.append(e)
            vs = jnp.concatenate(
                [jnp.concatenate([v * m for m in mask3], axis=0), jnp.concatenate(mask3, axis=0)], axis=1
            )
            out = mm(jnp.concatenate(parts, axis=1), vs)
            rl = 1.0 / out[:, LANES:]
            rl_ref[i * BLK : (i + 1) * BLK, cols] = rl
            o_ref[i * BLK : (i + 1) * BLK, cols] = (out[:, :LANES] * rl).astype(BF16)


def delta_of(prod, per, hdim):
    lane = lax.broadcasted_iota(jnp.int32, prod.shape, 1) // hdim
    return [jnp.sum(jnp.where(lane == h, prod, 0.0), axis=1, keepdims=True) for h in range(per)]


def fold(grad, ext, ext_t, qb, kb):
    cols, rows = [], []
    for c in range(3):
        diff = ext_t[qb * BLK : (qb + 1) * BLK, c : c + 1] - ext[c : c + 1, kb * BLK : (kb + 1) * BLK]
        t = grad * diff
        cols.append(2.0 * jnp.sum(t, axis=1, keepdims=True))
        rows.append(-2.0 * jnp.sum(t, axis=0, keepdims=True))
    return cols, rows


def columns_to_rows(cols):
    lane = lax.broadcasted_iota(jnp.int32, (BLK, LANES), 1)
    wide = jnp.zeros((BLK, LANES), F32)
    for c in range(3):
        wide = jnp.where(lane == c, cols[c], wide)
    return wide.T[:8]


def three_rows(rows):
    sub = lax.broadcasted_iota(jnp.int32, (8, LANES), 0)
    out = jnp.zeros((8, LANES), F32)
    for c in range(3):
        out = jnp.where(sub == c, rows[c], out)
    return out


def first_kernel(
    nb, heads, hdim,
    par_ref, gam_ref, own_ref, ra_ref, rb_ref, embed_ref, gains_ref, outg_ref, ro_ref,
    wq_h, wk_h, wv_h, wo_h, wu_h, wd_h,
    e_out, paya_ref, payb_ref, part_ref, halo_ref, g1_ref,
    s_o, s_rl, s_v, s_x1, s_gd, s_e, s_el, s_er,
    wq, wk, wv, wo, wu, wd, wsem, osem,
    d2_ref, x0_ref, q_ref, k_ref, v_ref, o_ref, rl_ref, e_ref, x1_ref, gd_ref, st_ref,
    q1_ref, k1_ref, v1_ref, o1_ref, rl1_ref, e1_ref, dq_ref, dk_ref, dv_ref,
):
    layers = 2
    qb = nb + 2
    kb = nb + 4
    mid = slice(BLK, (nb + 1) * BLK)
    copies = {}
    for layer in range(layers):
        for n, (src, dst) in enumerate(((wq_h, wq), (wk_h, wk), (wv_h, wv), (wo_h, wo), (wu_h, wu), (wd_h, wd))):
            copies[n, layer] = pltpu.make_async_copy(src.at[layer], dst.at[layer], wsem.at[n, layer])
            copies[n, layer].start()

    par = par_ref[0]
    before, own, after = arrange(par, own_ref[...], ra_ref[...], rb_ref[...])
    ext = jnp.concatenate([before, own, after], axis=1)
    ext_t = ext.T
    distances(ext, ext_t, 1, d2_ref, qb)

    embed = embed_ref[...].astype(F32)
    normed = (embed * inv_rms(embed) * gains_ref[0:1]).astype(BF16)
    scale = hdim ** (-0.5)
    spec = ext_t[:, 3:4].astype(jnp.int32)
    nspec = embed_ref.shape[0]
    onehot = (spec == lax.broadcasted_iota(jnp.int32, (kb * BLK, nspec), 1)).astype(F32).astype(BF16)
    onehot_q = onehot[BLK : (qb + 1) * BLK]
    x0_ref[...] = mm(onehot_q, embed_ref[...])
    copies[0, 0].wait()
    q_ref[...] = mm(onehot_q, (mm(normed, wq[0]) * (scale * LOG2E)).astype(BF16)).astype(BF16)
    copies[1, 0].wait()
    k_ref[...] = mm(onehot, mm(normed, wk[0]).astype(BF16)).astype(BF16)
    copies[2, 0].wait()
    v_ref[...] = mm(onehot, mm(normed, wv[0]).astype(BF16)).astype(BF16)
    attend(q_ref, k_ref, v_ref, o_ref, rl_ref, e_ref, d2_ref, 0, gam_ref, 0, heads, hdim, qb)
    outs = [
        pltpu.make_async_copy(o_ref, s_o, osem.at[0]),
        pltpu.make_async_copy(rl_ref, s_rl, osem.at[1]),
        pltpu.make_async_copy(v_ref.at[pl.ds(BLK, qb * BLK)], s_v, osem.at[2]),
        pltpu.make_async_copy(e_ref.at[pl.ds(1, nb)], s_e, osem.at[3]),
        pltpu.make_async_copy(e_ref.at[0, :, :, pl.ds(2 * BLK, BLK)], s_el, osem.at[4]),
        pltpu.make_async_copy(e_ref.at[qb - 1, :, :, pl.ds(0, BLK)], s_er, osem.at[5]),
    ]
    for c in outs:
        c.start()
    copies[3, 0].wait()
    copies[4, 0].wait()
    copies[5, 0].wait()

    def feed(layer, x1, keep):
        inner = (x1 * inv_rms(x1) * gains_ref[2 * layer + 1 : 2 * layer + 2]).astype(BF16)
        act, slope = gelu_both(mm(inner, wu[layer]))
        keep(slope.astype(BF16))
        return x1 + mm(act.astype(BF16), wd[layer])

    step = 2 * BLK
    for r in range(0, qb * BLK, step):
        rows = slice(r, r + step)
        x1 = x0_ref[rows] + mm(o_ref[rows], wo[0])
        x1_ref[rows] = x1
        st_ref[rows] = feed(0, x1, lambda slope: gd_ref.__setitem__(rows, slope))
    outs += [
        pltpu.make_async_copy(x1_ref, s_x1, osem.at[6]),
        pltpu.make_async_copy(gd_ref, s_gd, osem.at[7]),
    ]
    for c in outs[6:]:
        c.start()

    for n in range(6):
        copies[n, 1].wait()
    gain = gains_ref[2:3]
    st = st_ref[...]
    normed = (st * inv_rms(st) * gain).astype(BF16)
    q1_ref[...] = (mm(normed[mid], wq[1]) * (scale * LOG2E)).astype(BF16)
    k1_ref[...] = mm(normed, wk[1]).astype(BF16)
    v1_ref[...] = mm(normed, wv[1]).astype(BF16)
    attend(q1_ref, k1_ref, v1_ref, o1_ref, rl1_ref, e1_ref, d2_ref, 1, gam_ref, 1, heads, hdim, nb)
    x1 = st_ref[mid] + mm(o1_ref[...], wo[1])
    slopes = []
    x2 = feed(1, x1, slopes.append)
    (slope,) = slopes

    w = outg_ref[...] * ro_ref[...]
    r = inv_rms(x2)
    along = jnp.sum(x2 * w, axis=1, keepdims=True)
    e_out[...] = jnp.broadcast_to(jnp.sum(along * r), e_out.shape)
    width = x2.shape[1]
    grad = r * (w - x2 * (r * r * along * (1.0 / width)))

    du = mm_nt(grad.astype(BF16), wd[1]).astype(BF16).astype(F32)
    dinner = mm_nt((du * slope.astype(F32)).astype(BF16), wu[1]).astype(BF16).astype(F32)
    grad = grad + rms_back(x1, gains_ref[3:4], dinner)
    datt = mm_nt(grad.astype(BF16), wo[1]).astype(BF16).astype(F32)

    per = LANES // hdim
    groups = heads // per
    mask = head_masks(BLK, per, hdim)
    mask3 = head_masks(3 * BLK, per, hdim)
    dk_ref[...] = jnp.zeros_like(dk_ref)
    dv_ref[...] = jnp.zeros_like(dv_ref)
    for i in range(nb):
        rows = slice(i * BLK, (i + 1) * BLK)
        win = slice(i * BLK, (i + 3) * BLK)
        pair = jnp.zeros((BLK, 3 * BLK), F32)
        for g in range(groups):
            cols = slice(g * LANES, (g + 1) * LANES)
            d_o = datt[rows, cols] * rl1_ref[rows, cols]
            delta = delta_of(d_o * o1_ref[rows, cols].astype(F32), per, hdim)
            d_o = d_o.astype(BF16)
            dos = jnp.concatenate([d_o * m for m in mask], axis=0)
            k = k1_ref[win, cols]
            q = q1_ref[rows, cols]
            qs = jnp.concatenate([q * m for m in mask], axis=0)
            dp = mm_nt(dos, v1_ref[win, cols])
            parts, es = [], []
            for h in range(per):
                e = e1_ref[i, g * per + h]
                ds = e.astype(F32) * (dp[h * BLK : (h + 1) * BLK] - delta[h])
                pair = pair + gam_ref[1, g * per + h] * ds
                parts.append(ds.astype(BF16))
                es.append(e)
            ks = jnp.concatenate([k * m for m in mask3], axis=0)
            dq_ref[rows, cols] = (mm(jnp.concatenate(parts, axis=1), ks) * scale).astype(BF16)
            dk_ref[win, cols] += mm_tn(jnp.concatenate(parts, axis=0), qs)
            dv_ref[win, cols] += mm_tn(jnp.concatenate(es, axis=0), dos)
        g1_ref[i] = pair
    dk = (dk_ref[...] * LN2).astype(BF16)
    dv = dv_ref[...].astype(BF16)
    dnorm = mm_nt(dk, wk[1]) + mm_nt(dv, wv[1])
    dq = mm_nt(dq_ref[...], wq[1])
    zeros = jnp.zeros((BLK, width), F32)
    dnorm = dnorm + jnp.concatenate([zeros, dq, zeros], axis=0)
    back = rms_back(st_ref[...], gain, dnorm.astype(BF16).astype(F32))
    part = grad + back[mid]
    part_ref[...] = part
    halo_ref[:BLK] = back[:BLK]
    halo_ref[BLK:] = back[(qb - 1) * BLK :]

    _, rows_low = fold(g1_ref[0, :, :BLK], ext, ext_t, 2, 1)
    _, rows_high = fold(g1_ref[nb - 1, :, 2 * BLK :], ext, ext_t, nb + 1, nb + 2)
    pad = jnp.zeros((8, width - LANES), F32)

    def payload(ref, halo, edge, rows):
        ref[:BLK] = halo.astype(BF16)
        ref[BLK : 2 * BLK] = edge.astype(BF16)
        tail = jnp.concatenate([three_rows(rows), pad], axis=1)
        ref[2 * BLK :] = jnp.concatenate([tail, jnp.zeros_like(tail)], axis=0).astype(BF16)

    def low(ref):
        payload(ref, back[:BLK], part[:BLK], rows_low)

    def high(ref):
        payload(ref, back[(qb - 1) * BLK :], part[(nb - 1) * BLK :], rows_high)

    @pl.when(par == 0)
    def _():
        high(paya_ref)
        low(payb_ref)

    @pl.when(par != 0)
    def _():
        low(paya_ref)
        high(payb_ref)

    for c in outs:
        c.wait()


def second_kernel(
    nb, heads, hdim,
    par_ref, gam_ref, own_ref, ra_ref, rb_ref, gains_ref, paya_ref, payb_ref, part_ref, halo_ref, g1_ref,
    s_o, s_rl, s_v, s_x1, s_gd, s_e, s_el, s_er, wo_h, wu_h, wd_h,
    f_ref,
    o_ref, rl_ref, v_ref, x1_ref, gd_ref, e_ref, el_ref, er_ref, wo, wu, wd, sem,
    datt_ref,
):
    qb = nb + 2
    pairs = (
        (wd_h.at[0], wd), (s_gd, gd_ref), (wu_h.at[0], wu), (s_x1, x1_ref), (wo_h.at[0], wo),
        (s_rl, rl_ref), (s_o, o_ref), (s_v, v_ref), (s_e, e_ref), (s_el, el_ref), (s_er, er_ref),
    )
    copies = [pltpu.make_async_copy(src, dst, sem.at[n]) for n, (src, dst) in enumerate(pairs)]
    for c in copies:
        c.start()
    par = par_ref[0]
    before, own, after = arrange(par, own_ref[...], ra_ref[...], rb_ref[...])
    ext = jnp.concatenate([before, own, after], axis=1)
    ext_t = ext.T
    from_low, _, from_high = arrange(par, None, paya_ref[...], payb_ref[...])
    from_low = from_low.astype(F32)
    from_high = from_high.astype(F32)
    part = part_ref[...]
    pieces = [halo_ref[:BLK] + from_low[BLK : 2 * BLK]]
    own_parts = [part[i * BLK : (i + 1) * BLK] for i in range(nb)]
    own_parts[0] = own_parts[0] + from_low[:BLK]
    own_parts[-1] = own_parts[-1] + from_high[:BLK]
    pieces += own_parts
    pieces.append(halo_ref[BLK:] + from_high[BLK : 2 * BLK])
    grad = jnp.concatenate(pieces, axis=0)
    copies[0].wait()
    du = mm_nt(grad.astype(BF16), wd[...]).astype(BF16).astype(F32)
    copies[1].wait()
    copies[2].wait()
    dinner = mm_nt((du * gd_ref[...].astype(F32)).astype(BF16), wu[...]).astype(BF16).astype(F32)
    copies[3].wait()
    grad = grad + rms_back(x1_ref[...], gains_ref[1:2], dinner)
    copies[4].wait()
    datt_ref[...] = mm_nt(grad.astype(BF16), wo[...]).astype(BF16).astype(F32)
    for c in copies[5:]:
        c.wait()

    per = LANES // hdim
    groups = heads // per
    mask = head_masks(BLK, per, hdim)

    def pair_of(rows, keys, e_of, total):
        for g in range(groups):
            cols = slice(g * LANES, (g + 1) * LANES)
            d_o = datt_ref[rows, cols] * rl_ref[rows, cols]
            delta = delta_of(d_o * o_ref[rows, cols].astype(F32), per, hdim)
            d_o = d_o.astype(BF16)
            dos = jnp.concatenate([d_o * m for m in mask], axis=0)
            dp = mm_nt(dos, v_ref[keys, cols])
            for h in range(per):
                ds = e_of(g * per + h).astype(F32) * (dp[h * BLK : (h + 1) * BLK] - delta[h])
                total = total + gam_ref[0, g * per + h] * ds
        return total

    forces = [jnp.zeros((8, LANES), F32) for _ in range(nb)]
    forces[0] = forces[0] + from_low[2 * BLK : 2 * BLK + 8, :LANES]
    forces[-1] = forces[-1] + from_high[2 * BLK : 2 * BLK + 8, :LANES]
    for i in range(nb):
        total = pair_of(
            slice((i + 1) * BLK, (i + 2) * BLK), slice(i * BLK, (i + 3) * BLK), lambda h: e_ref[i, h], g1_ref[i]
        )
        sums = None
        for s in range(3):
            cols, rows = fold(total[:, s * BLK : (s + 1) * BLK], ext, ext_t, i + 2, i + 1 + s)
            sums = cols if sums is None else [a + b for a, b in zip(sums, cols)]
            j = i - 1 + s
            if 0 <= j < nb:
                forces[j] = forces[j] + three_rows(rows)
        forces[i] = forces[i] + columns_to_rows(sums)
    zero = jnp.zeros((BLK, BLK), F32)
    total = pair_of(slice(0, BLK), slice(BLK, 2 * BLK), lambda h: el_ref[h], zero)
    _, rows = fold(total, ext, ext_t, 1, 2)
    forces[0] = forces[0] + three_rows(rows)
    total = pair_of(slice((qb - 1) * BLK, qb * BLK), slice((qb - 2) * BLK, (qb - 1) * BLK), lambda h: er_ref[h], zero)
    _, rows = fold(total, ext, ext_t, nb + 2, nb + 1)
    forces[-1] = forces[-1] + three_rows(rows)
    f_ref[...] = jnp.concatenate(forces, axis=1)[:3]


def swap_a(x):
    n = lax.axis_size("chain")
    return lax.ppermute(x, "chain", [(i, i ^ 1) for i in range(n)])


def swap_b(x):
    n = lax.axis_size("chain")
    return lax.ppermute(x, "chain", [(i, ((i + 1) ^ 1) - 1) for i in range(1, n - 1)])


def total_of(x):
    n = lax.axis_size("chain")
    if n & (n - 1):
        return lax.psum(x, "chain")
    step = 1
    while step < n:
        x = x + lax.ppermute(x, "chain", [(i, i ^ step) for i in range(n)])
        step *= 2
    return x


def local(
    species, positions, block_list, embed, w_query, w_key, w_value, w_out, w_up, w_down, norm_gains, gammas, out_gain, readout
):
    atoms = species.shape[0]
    nb = atoms // BLK
    width = embed.shape[1]
    layers, heads = gammas.shape
    hdim = width // heads
    ff = w_up.shape[2]
    qb, kb = nb + 2, nb + 4
    assert nb >= 2 and layers == 2 and LANES % hdim == 0
    me = lax.axis_index("chain")
    par = (me % 2).astype(jnp.int32).reshape(1)
    expect = (me * nb + jnp.arange(nb, dtype=jnp.int32))[:, None] - 1 + jnp.arange(3, dtype=jnp.int32)[None, :]
    valid = ((block_list == expect) & (block_list >= 0)).astype(F32)
    own = jnp.concatenate(
        [positions, species.astype(F32)[None], jnp.repeat(valid.T, BLK, axis=1), jnp.zeros((1, atoms), F32)], axis=0
    )
    edge = 2 * BLK
    if atoms == edge:
        send_a = send_b = own
    else:
        first, last = own[:, :edge], own[:, -edge:]
        send_a = jnp.where(par[0] == 0, last, first)
        send_b = jnp.where(par[0] == 0, first, last)
    near_a, near_b = swap_a(send_a), swap_b(send_b)
    gains = norm_gains.reshape(2 * layers, width)
    smem = pl.BlockSpec(memory_space=pltpu.SMEM)
    vmem = pl.BlockSpec(memory_space=pltpu.VMEM)
    hbm = pl.BlockSpec(memory_space=pltpu.HBM)

    def out(*shape, dtype=F32):
        return jax.ShapeDtypeStruct(shape, dtype)

    pay = out(2 * BLK + 16, width, dtype=BF16)
    saved = [
        out(qb * BLK, width, dtype=BF16),
        out(qb * BLK, width),
        out(qb * BLK, width, dtype=BF16),
        out(qb * BLK, width),
        out(qb * BLK, ff, dtype=BF16),
        out(nb, heads, BLK, 3 * BLK, dtype=BF16),
        out(heads, BLK, BLK, dtype=BF16),
        out(heads, BLK, BLK, dtype=BF16),
    ]
    vm = pltpu.VMEM
    first = pl.pallas_call(
        functools.partial(first_kernel, nb, heads, hdim),
        out_shape=[
            out(8, LANES), pay, pay, out(nb * BLK, width), out(2 * BLK, width), out(nb, BLK, 3 * BLK), *saved,
        ],
        in_specs=[smem, smem] + [vmem] * 7 + [hbm] * 6,
        out_specs=[vmem] * 6 + [hbm] * 8,
        scratch_shapes=[
            vm((layers, width, width), BF16), vm((layers, width, width), BF16), vm((layers, width, width), BF16),
            vm((layers, width, width), BF16), vm((layers, width, ff), BF16), vm((layers, ff, width), BF16),
            pltpu.SemaphoreType.DMA((6, layers)), pltpu.SemaphoreType.DMA((8,)),
            vm((qb, BLK, 3 * BLK), F32), vm((qb * BLK, width), F32), vm((qb * BLK, width), BF16),
            vm((kb * BLK, width), BF16), vm((kb * BLK, width), BF16), vm((qb * BLK, width), BF16),
            vm((qb * BLK, width), F32), vm((qb, heads, BLK, 3 * BLK), BF16), vm((qb * BLK, width), F32),
            vm((qb * BLK, ff), BF16), vm((qb * BLK, width), F32),
            vm((nb * BLK, width), BF16), vm((qb * BLK, width), BF16), vm((qb * BLK, width), BF16),
            vm((nb * BLK, width), BF16), vm((nb * BLK, width), F32), vm((nb, heads, BLK, 3 * BLK), BF16),
            vm((nb * BLK, width), BF16), vm((qb * BLK, width), F32), vm((qb * BLK, width), F32),
        ],
        compiler_params=pltpu.CompilerParams(vmem_limit_bytes=62 * 1024 * 1024),
    )(
        par, gammas, own, near_a, near_b, embed, gains, out_gain.reshape(1, width), readout.reshape(1, width),
        w_query, w_key, w_value, w_out, w_up, w_down,
    )
    e_part, pay_a, pay_b, part, halo, g1 = first[:6]
    got_a, got_b = swap_a(pay_a), swap_b(pay_b)
    energy = total_of(e_part[:1, :1]).reshape(1)
    forces = pl.pallas_call(
        functools.partial(second_kernel, nb, heads, hdim),
        out_shape=out(3, atoms),
        in_specs=[smem, smem] + [vmem] * 9 + [hbm] * 11,
        out_specs=vmem,
        scratch_shapes=[
            vm((qb * BLK, width), BF16), vm((qb * BLK, width), F32), vm((qb * BLK, width), BF16),
            vm((qb * BLK, width), F32), vm((qb * BLK, ff), BF16), vm((nb, heads, BLK, 3 * BLK), BF16),
            vm((heads, BLK, BLK), BF16), vm((heads, BLK, BLK), BF16),
            vm((width, width), BF16), vm((width, ff), BF16), vm((ff, width), BF16),
            pltpu.SemaphoreType.DMA((11,)),
            vm((qb * BLK, width), F32),
        ],
        compiler_params=pltpu.CompilerParams(vmem_limit_bytes=62 * 1024 * 1024),
    )(par, gammas, own, near_a, near_b, gains, got_a, got_b, part, halo, g1, *first[6:], w_out, w_up, w_down)
    return energy, forces


def solution(mesh):
    sharded = ("frames", "chain")
    return jax.shard_map(
        local,
        mesh=mesh,
        in_specs=(P(sharded), P(None, sharded), P(sharded, None)) + (P(),) * 11,
        out_specs=(P("frames"), P(None, sharded)),
        check_vma=False,
    )
```

time: 244 us -> 67.7 us (0.28); the launches traced: 241 us -> 67.4 us
  local copies, waits for them, and re-layouts: 76.6 us -> 4.12 us
  matrix products: 71.5 us -> 0 us
  blocking collectives: 34.1 us -> 0 us
  Pallas kernels: 0 us -> 32.6 us
  other arithmetic: 27 us -> 2.2 us
  starting transfers between devices: 25.4 us -> 21 us
  between operations: 2.16 us -> 5.07 us
    dot_general x32 -> x0, matrix products: 60.2 us -> none  [the longest x6 17 us: attend(): jnp.einsum('bhqk,bkhd->bqhd', probs, value_win, preferred_element_type=jn...]
    psum x1 -> x0, blocking collectives: 34.1 us -> none  [local(): energy = lax.psum(local_total, 'chain').reshape(1)]
    pallas_call x0 -> x2, Pallas kernels: none -> 32.6 us  [the longest x1 23.3 us: local(): pl.pallas_call(functools.partial(first_kernel, nb, heads, hdim), out_shap...]
    unnamed x160 -> x12, local copies, waits for them, and re-layouts: 26.6 us -> 1.44 us
    slice x27 -> x1, local copies, waits for them, and re-layouts: 17.3 us -> 1.2 us  [local(): energy = total_of(e_part[:1, :1]).reshape(1)]
    concatenate x18 -> x1, local copies, waits for them, and re-layouts: 13.4 us -> 0.07 us  [local(): jnp.concatenate([positions, species.astype(F32)[None], jnp.repeat(valid.T...]
    sub x2 -> x0, matrix products: 11.2 us -> none  [attend(): expo = jnp.exp(scores - peak)]
    convert_element_type x10 -> x1, other arithmetic: 11.2 us -> 0.68 us  [local(): species.astype(F32)[None]]
  transfers between devices with their start and end apart: 10 -> 8, of which waited for: 2 -> 4; matrix products, arithmetic and copies ran while one was open for 6% -> 4% of each run, Pallas kernels for 0% -> 0%
where the time goes in v1:
time: 67.7 us; the launch traced here: 67.4 us
  Pallas kernels  32.6 us (48%)
  starting transfers between devices  21 us (31%)
  between operations  5.07 us (7%)
  local copies, waits for them, and re-layouts  4.12 us (6%)
  waiting for transfers between devices  2.4 us (4%)
  other arithmetic  2.2 us (3%)
    pallas_call x1, Pallas kernels, local(): pl.pallas_call(functools.partial(first_kernel, nb, heads, hdim), out_shap...  23.3 us
    ppermute x4, starting transfers between devices, total_of(): x = x + lax.ppermute(x, 'chain', [(i, i ^ step) for i in range(n)])  15 us
    pallas_call x1, Pallas kernels, local(): pl.pallas_call(functools.partial(second_kernel, nb, heads, hdim), out_sha...  9.29 us
    ppermute x2, starting transfers between devices, swap_a(): return lax.ppermute(x, 'chain', [(i, i ^ 1) for i in range(n)])  4.48 us
    ppermute x4, waiting for transfers between devices, total_of(): x = x + lax.ppermute(x, 'chain', [(i, i ^ step) for i in range(n)])  2.38 us
    ppermute x2, starting transfers between devices, swap_b(): lax.ppermute(x, 'chain', [(i, (i + 1 ^ 1) - 1) for i in range(1, n - 1)])  1.54 us
    unnamed x12, local copies, waits for them, and re-layouts  1.44 us
  transfers between devices with their start and end apart: 8, of which 4 were waited for; matrix products, arithmetic and copies ran while one was open for 4% of the time, Pallas kernels for 0%

profile of v1, /device:TPU:0, one launch (start us, length us, event | category | flops | bytes accessed | tf_op | source)
XLA Modules:
  0.0 67.4 jit_solution(8555183854691661401)
XLA Ops:
  0.6 0.8 %fusion = f32[3,2]{0,1:T(2,128)S(1)} fusion(s32[2,3]{1,0:T(2,128)} %param.16, s32[2]{0:T(128)S(1)} %add_add_fusion), kind=kLoop, calls=%fused_computation.4 | loop fusion | flops 30 | bytes 56 | tf_op jit(solution)/shard_map/transpose | solution.py:431
  1.4 0.1 copy.16
  1.5 0.1 broadcast_bitcast_fusion
  1.6 0.7 %convert_element_type.4 = f32[256]{0:T(256)S(1)} convert(s32[256]{0:T(256)} %param.14) | non-fusion elementwise | flops 256 | bytes 2048 | tf_op jit(solution)/shard_map/convert_element_type | solution.py:431
  2.3 0.1 pad.3.clone
  2.3 0.8 %maximum_maximum_fusion.own_ref = f32[8,256]{1,0:T(8,128)S(1)} fusion(f32[3,256]{1,0:T(4,128)S(1)} %bitcast.13, f32[1,256]{1,0:T(1,128)S(1)} %bitcast.14, f32[3,256]{1,0:T(4,128)} %param.15, f32[8]{0:T(128)S(1)} %pad.3.clone), kind=kLoop, calls=%fused_computation | loop fusion | flops 6144 | bytes 15392 | tf_op jit(solution)/shard_map/concatenate | solution.py:430
  3.1 0.0 copy-start.2
  3.1 0.6 collective-permute-start.1
  3.7 4.4 %collective-permute-start = (f32[8,256]{1,0:T(8,128)S(1)}, f32[8,256]{1,0:T(8,128)S(1)}, u32[]{:S(2)}, u32[]{:S(2)}) collective-permute-start(f32[8,256]{1,0:T(8,128)S(1)} %maximum_maximum_fusion.own_ref), channel_id=1, source_target_pairs={{0,1},{1,0},{2,3},{3,2},{4,5},{5,4},{6,7},{7,6},{8,9},{9,8},{10,11... | collective-permute-start | bytes 24584 | tf_op jit(solution)/shard_map/ppermute | solution.py:396
  8.1 1.3 %reshape.30.gains_ref = f32[4,512]{1,0:T(4,128)} reshape(f32[2,2,512]{2,1,0:T(2,128)} %param.24) | data formatting | bytes 16384 | tf_op jit(solution)/shard_map/reshape | solution.py:441
  9.4 0.0 collective-permute-done.1.rb_ref
  9.4 0.0 copy-start.3
  9.5 0.0 collective-permute-done.ra_ref
  9.5 0.0 copy-start.4
  9.5 0.0 copy-done.2
  9.5 0.6 copy-done.3
  10.1 0.0 copy-done.4
  10.1 23.3 %shard_map.149 = (f32[8,128]{1,0:T(8,128)}, bf16[272,512]{1,0:T(8,128)(2,1)}, bf16[272,512]{1,0:T(8,128)(2,1)}, f32[256,512]{1,0:T(8,128)}, f32[256,512]{1,0:T(8...) custom-call(s32[1]{0:T(128)} %bitcast.par_ref, ...), custom_call_target="tpu_custom_call" | custom-call | tf_op jit(solution)/shard_map/pallas_call | solution.py:461
  33.4 0.1 collective-permute-start.6
  33.5 0.9 %collective-permute-start.7 = (bf16[272,512]{1,0:T(8,128)(2,1)}, bf16[272,512]{1,0:T(8,128)(2,1)S(1)}, u32[]{:S(2)}, u32[]{:S(2)}) collective-permute-start(bf16[272,512]{1,0:T(8,128)(2,1)} %get-tuple-element.18), channel_id=1, source_target_pairs={{1,2},{2,1},{3,4},{4,3},{5,6},{6,5},{7,8},{8,7},{9,10},{10,9},{11,... | collective-permute-start | bytes 835592 | tf_op jit(solution)/shard_map/ppermute | solution.py:401
  34.4 1.2 %slice.3 = f32[1,1]{1,0:T(1,128)} slice(f32[8,128]{1,0:T(8,128)} %get-tuple-element.16), slice={[0:1], [0:1]} | slice | bytes 8 | tf_op jit(solution)/shard_map/slice | solution.py:487
  35.6 3.6 %collective-permute-start.2 = (f32[1,1]{1,0:T(1,128)}, f32[1,1]{1,0:T(1,128)}, u32[]{:S(2)}, u32[]{:S(2)}) collective-permute-start(f32[1,1]{1,0:T(1,128)} %slice.3), channel_id=1, source_target_pairs={{0,1},{1,0},{2,3},{3,2},{4,5},{5,4},{6,7},{7,6},{8,9},{9,8},{10,11... | collective-permute-start | bytes 20 | tf_op jit(solution)/shard_map/ppermute | solution.py:410
  39.2 1.1 %collective-permute-done.2 = f32[1,1]{1,0:T(1,128)} collective-permute-done((f32[1,1]{1,0:T(1,128)}, f32[1,1]{1,0:T(1,128)}, u32[]{:S(2)}, u32[]{:S(2)}) %collective-permute-start.2) | collective-permute-done | bytes 36 | tf_op jit(solution)/shard_map/ppermute | solution.py:410
  41.5 3.1 %collective-permute-start.3 = (f32[1,1]{1,0:T(1,128)}, f32[1,1]{1,0:T(1,128)}, u32[]{:S(2)}, u32[]{:S(2)}) collective-permute-start(f32[1,1]{1,0:T(1,128)} %add.51), channel_id=1, source_target_pairs={{0,2},{1,3},{2,0},{3,1},{4,6},{5,7},{6,4},{7,5},{8,10},{9,11},{10,... | collective-permute-start | bytes 20 | tf_op jit(solution)/shard_map/ppermute | solution.py:410
  44.6 0.6 collective-permute-done.3
  45.9 3.9 %collective-permute-start.4 = (f32[1,1]{1,0:T(1,128)}, f32[1,1]{1,0:T(1,128)}, u32[]{:S(2)}, u32[]{:S(2)}) collective-permute-start(f32[1,1]{1,0:T(1,128)} %add.52), channel_id=1, source_target_pairs={{0,4},{1,5},{2,6},{3,7},{4,0},{5,1},{6,2},{7,3},{8,12},{9,13},{10,... | collective-permute-start | bytes 20 | tf_op jit(solution)/shard_map/ppermute | solution.py:410
  49.8 0.3 collective-permute-done.4
  50.7 4.4 %collective-permute-start.5 = (f32[1,1]{1,0:T(1,128)}, f32[1,1]{1,0:T(1,128)}, u32[]{:S(2)}, u32[]{:S(2)}) collective-permute-start(f32[1,1]{1,0:T(1,128)} %add.53), channel_id=1, source_target_pairs={{0,8},{1,9},{2,10},{3,11},{4,12},{5,13},{6,14},{7,15},{8,0},{9,1},... | collective-permute-start | bytes 20 | tf_op jit(solution)/shard_map/ppermute | solution.py:410
  55.1 0.3 collective-permute-done.5
  56.1 0.0 collective-permute-done.6.paya_ref
  56.1 0.0 copy-start
  56.1 0.0 collective-permute-done.7.payb_ref
  56.1 0.0 copy-start.1
  56.2 0.7 %copy-done = bf16[272,512]{1,0:T(8,128)(2,1)} copy-done((bf16[272,512]{1,0:T(8,128)(2,1)}, bf16[272,512]{1,0:T(8,128)(2,1)S(1)}, u32[]{:S(2)}) %copy-start) | copy-done | bytes 278552
  56.8 0.1 copy-done.1
  56.9 9.3 %shard_map.150 = f32[3,256]{1,0:T(4,128)} custom-call(s32[1]{0:T(128)} %bitcast.par_ref, f32[2,16]{1,0:T(2,128)} %gam_ref.3, f32[8,256]{1,0:T(8,128)} %copy-done.2, f32[8,256]{1,0:T(8,128)} %copy-done.4, f32[8,256]{1,0:T(8,128)} %copy-done.3, f32[4,512]{1,0:T(4,128)} %reshape.30.gains_ref, bf16[272,512]{1,0:T(8,128)(2,1)} %copy-done, ...), custom_call_target="tpu_custom_call" | custom-call | tf_op jit(solution)/shard_map/pallas_call | solution.py:488
  (2 shorter events, 0.0 us)
Async XLA Ops:
  3.1 6.4 %copy-start.2 = (f32[8,256]{1,0:T(8,128)}, f32[8,256]{1,0:T(8,128)S(1)}, u32[]{:S(2)}) copy-start(f32[8,256]{1,0:T(8,128)S(1)} %maximum_maximum_fusion.own_ref) | copy-start | bytes 24580
  3.1 6.4 %collective-permute-start.1 = (f32[8,256]{1,0:T(8,128)S(1)}, f32[8,256]{1,0:T(8,128)S(1)}, u32[]{:S(2)}, u32[]{:S(2)}) collective-permute-start(f32[8,256]{1,0:T(8,128)S(1)} %maximum_maximum_fusion.own_ref), channel_id=1, source_target_pairs={{1,2},{2,1},{3,4},{4,3},{5,6},{6,5},{7,8},{8,7},{9,10},{10,9},{11,... | collective-permute-start | bytes 24584 | tf_op jit(solution)/shard_map/ppermute | solution.py:401
  3.7 5.7 %collective-permute-start = (f32[8,256]{1,0:T(8,128)S(1)}, f32[8,256]{1,0:T(8,128)S(1)}, u32[]{:S(2)}, u32[]{:S(2)}) collective-permute-start(f32[8,256]{1,0:T(8,128)S(1)} %maximum_maximum_fusion.own_ref), channel_id=1, source_target_pairs={{0,1},{1,0},{2,3},{3,2},{4,5},{5,4},{6,7},{7,6},{8,9},{9,8},{10,11... | collective-permute-start | bytes 24584 | tf_op jit(solution)/shard_map/ppermute | solution.py:396
  9.4 0.6 copy-start.3
  9.5 0.6 copy-start.4
  33.4 22.7 %collective-permute-start.6 = (bf16[272,512]{1,0:T(8,128)(2,1)}, bf16[272,512]{1,0:T(8,128)(2,1)S(1)}, u32[]{:S(2)}, u32[]{:S(2)}) collective-permute-start(bf16[272,512]{1,0:T(8,128)(2,1)} %get-tuple-element.17), channel_id=1, source_target_pairs={{0,1},{1,0},{2,3},{3,2},{4,5},{5,4},{6,7},{7,6},{8,9},{9,8},{10,11... | collective-permute-start | bytes 835592 | tf_op jit(solution)/shard_map/ppermute | solution.py:396
  33.5 22.7 %collective-permute-start.7 = (bf16[272,512]{1,0:T(8,128)(2,1)}, bf16[272,512]{1,0:T(8,128)(2,1)S(1)}, u32[]{:S(2)}, u32[]{:S(2)}) collective-permute-start(bf16[272,512]{1,0:T(8,128)(2,1)} %get-tuple-element.18), channel_id=1, source_target_pairs={{1,2},{2,1},{3,4},{4,3},{5,6},{6,5},{7,8},{8,7},{9,10},{10,9},{11,... | collective-permute-start | bytes 835592 | tf_op jit(solution)/shard_map/ppermute | solution.py:401
  35.6 4.7 %collective-permute-start.2 = (f32[1,1]{1,0:T(1,128)}, f32[1,1]{1,0:T(1,128)}, u32[]{:S(2)}, u32[]{:S(2)}) collective-permute-start(f32[1,1]{1,0:T(1,128)} %slice.3), channel_id=1, source_target_pairs={{0,1},{1,0},{2,3},{3,2},{4,5},{5,4},{6,7},{7,6},{8,9},{9,8},{10,11... | collective-permute-start | bytes 20 | tf_op jit(solution)/shard_map/ppermute | solution.py:410
  41.5 3.7 %collective-permute-start.3 = (f32[1,1]{1,0:T(1,128)}, f32[1,1]{1,0:T(1,128)}, u32[]{:S(2)}, u32[]{:S(2)}) collective-permute-start(f32[1,1]{1,0:T(1,128)} %add.51), channel_id=1, source_target_pairs={{0,2},{1,3},{2,0},{3,1},{4,6},{5,7},{6,4},{7,5},{8,10},{9,11},{10,... | collective-permute-start | bytes 20 | tf_op jit(solution)/shard_map/ppermute | solution.py:410
  45.9 4.2 %collective-permute-start.4 = (f32[1,1]{1,0:T(1,128)}, f32[1,1]{1,0:T(1,128)}, u32[]{:S(2)}, u32[]{:S(2)}) collective-permute-start(f32[1,1]{1,0:T(1,128)} %add.52), channel_id=1, source_target_pairs={{0,4},{1,5},{2,6},{3,7},{4,0},{5,1},{6,2},{7,3},{8,12},{9,13},{10,... | collective-permute-start | bytes 20 | tf_op jit(solution)/shard_map/ppermute | solution.py:410
  50.7 4.7 %collective-permute-start.5 = (f32[1,1]{1,0:T(1,128)}, f32[1,1]{1,0:T(1,128)}, u32[]{:S(2)}, u32[]{:S(2)}) collective-permute-start(f32[1,1]{1,0:T(1,128)} %add.53), channel_id=1, source_target_pairs={{0,8},{1,9},{2,10},{3,11},{4,12},{5,13},{6,14},{7,15},{8,0},{9,1},... | collective-permute-start | bytes 20 | tf_op jit(solution)/shard_map/ppermute | solution.py:410
  56.1 0.7 %copy-start = (bf16[272,512]{1,0:T(8,128)(2,1)}, bf16[272,512]{1,0:T(8,128)(2,1)S(1)}, u32[]{:S(2)}) copy-start(bf16[272,512]{1,0:T(8,128)(2,1)S(1)} %collective-permute-done.6.paya_ref) | copy-start | bytes 835588
  56.1 0.8 %copy-start.1 = (bf16[272,512]{1,0:T(8,128)(2,1)}, bf16[272,512]{1,0:T(8,128)(2,1)S(1)}, u32[]{:S(2)}) copy-start(bf16[272,512]{1,0:T(8,128)(2,1)S(1)} %collective-permute-done.7.payb_ref) | copy-start | bytes 835588

commit v2 on v1

v2 whole, which is shorter than its diff:
```python
import functools
import math

import jax
import jax.numpy as jnp
from jax import lax
from jax.experimental import pallas as pl
from jax.experimental.pallas import tpu as pltpu
from jax.sharding import PartitionSpec as P

BLK = 128
LANES = 128
EPS = 1e-06
LOG2E = math.log2(math.e)
LN2 = math.log(2.0)
FAR = 1e30
F32 = jnp.float32
BF16 = jnp.bfloat16
C0 = math.sqrt(2.0 / math.pi)
C1 = 0.044715


def mm(a, b):
    return jnp.dot(a, b, preferred_element_type=F32)


def mm_nt(a, b):
    return lax.dot_general(a, b, (((1,), (1,)), ((), ())), preferred_element_type=F32)


def mm_tn(a, b):
    return lax.dot_general(a, b, (((0,), (0,)), ((), ())), preferred_element_type=F32)


def inv_rms(x):
    return lax.rsqrt(jnp.mean(x * x, axis=-1, keepdims=True) + EPS)


def rms_back(x, gain, cot):
    r = inv_rms(x)
    t = cot * gain
    return r * (t - x * (r * r * jnp.mean(x * t, axis=-1, keepdims=True)))


def gelu_both(x):
    t = jnp.tanh(C0 * (x + C1 * x * x * x))
    half = 0.5 * (1.0 + t)
    return x * half, half + 0.5 * x * (1.0 - t * t) * (C0 + 3.0 * C0 * C1 * x * x)


def head_masks(rows, heads_per_group, hdim):
    lane = lax.broadcasted_iota(jnp.int32, (rows, LANES), 1) // hdim
    return [(lane == h).astype(F32).astype(BF16) for h in range(heads_per_group)]


def arrange(par, own, from_a, from_b):
    before = jnp.where(par == 0, from_b, from_a)
    after = jnp.where(par == 0, from_a, from_b)
    return before, own, after


def distances(ext, ext_t, first, d2_ref, count):
    for i in range(count):
        q = ext_t[(first + i) * BLK : (first + i + 1) * BLK]
        for s in range(3):
            k0 = (first + i - 1 + s) * BLK
            tot = None
            for c in range(3):
                diff = q[:, c : c + 1] - ext[c : c + 1, k0 : k0 + BLK]
                tot = diff * diff if tot is None else tot + diff * diff
            d2_ref[i, :, s * BLK : (s + 1) * BLK] = jnp.where(q[:, 4 + s : 5 + s] > 0.5, tot, FAR)


def stacked(x, masks):
    return jnp.concatenate([x * m for m in masks], axis=0)


def beside(x, y):
    zero = jnp.zeros_like(x)
    return jnp.concatenate([jnp.concatenate([x, zero], axis=1), jnp.concatenate([zero, y], axis=1)], axis=0)


def pair_products(a, b, masks, masks2, per):
    shared = mm_nt(stacked(a, masks2), b[BLK : 3 * BLK])
    both = jnp.concatenate([a[:BLK], a[BLK:]], axis=1)
    both = jnp.concatenate([both * jnp.concatenate([m, m], axis=1) for m in masks], axis=0)
    outer = mm_nt(both, beside(b[:BLK], b[3 * BLK :]))
    got = []
    for t in range(2):
        got.append([
            (outer[h * BLK : (h + 1) * BLK, t * BLK : (t + 1) * BLK], shared[(2 * h + t) * BLK : (2 * h + t + 1) * BLK])
            for h in range(per)
        ])
    return got


def window_parts(t):
    return (slice(0, BLK), slice(BLK, 3 * BLK)) if t == 0 else (slice(2 * BLK, 3 * BLK), slice(0, 2 * BLK))


def attend(q_ref, k_ref, v_ref, o_ref, rl_ref, e_ref, d2_ref, d2_first, gam_ref, layer, heads, hdim, count):
    per = LANES // hdim
    groups = heads // per
    masks = head_masks(BLK, per, hdim)
    masks2 = head_masks(2 * BLK, per, hdim)
    masks3 = head_masks(3 * BLK, per, hdim)
    ones = jnp.concatenate(masks3, axis=0)
    for i in range(0, count, 2):
        for g in range(groups):
            cols = slice(g * LANES, (g + 1) * LANES)
            scores = pair_products(
                q_ref[i * BLK : (i + 2) * BLK, cols], k_ref[i * BLK : (i + 4) * BLK, cols], masks, masks2, per
            )
            for t in range(2):
                outer_cols, shared_cols = window_parts(t)
                parts = []
                for h in range(per):
                    gam = gam_ref[layer, g * per + h] * LOG2E
                    outer, shared = scores[t][h]
                    outer = outer - gam * d2_ref[d2_first + i + t, :, outer_cols]
                    shared = shared - gam * d2_ref[d2_first + i + t, :, shared_cols]
                    peak = jnp.maximum(jnp.maximum(outer, shared[:, :BLK]), shared[:, BLK:])
                    peak = jnp.max(peak, axis=1, keepdims=True)
                    outer = jnp.exp2(outer - peak).astype(BF16)
                    shared = jnp.exp2(shared - peak).astype(BF16)
                    e = jnp.concatenate([outer, shared] if t == 0 else [shared, outer], axis=1)
                    e_ref[i + t, g * per + h] = e
                    parts.append(e)
                rows = slice((i + t) * BLK, (i + t + 1) * BLK)
                v = v_ref[(i + t) * BLK : (i + t + 3) * BLK, cols]
                out = mm(jnp.concatenate(parts, axis=1), jnp.concatenate([stacked(v, masks3), ones], axis=1))
                rl = 1.0 / out[:, LANES:]
                rl_ref[rows, cols] = rl
                o_ref[rows, cols] = (out[:, :LANES] * rl).astype(BF16)


def delta_of(prod, per, hdim):
    lane = lax.broadcasted_iota(jnp.int32, prod.shape, 1) // hdim
    return [jnp.sum(jnp.where(lane == h, prod, 0.0), axis=1, keepdims=True) for h in range(per)]


def fold(grad, ext, ext_t, qb, kb):
    cols, rows = [], []
    for c in range(3):
        diff = ext_t[qb * BLK : (qb + 1) * BLK, c : c + 1] - ext[c : c + 1, kb * BLK : (kb + 1) * BLK]
        t = grad * diff
        cols.append(2.0 * jnp.sum(t, axis=1, keepdims=True))
        rows.append(-2.0 * jnp.sum(t, axis=0, keepdims=True))
    return cols, rows


def columns_to_rows(cols):
    lane = lax.broadcasted_iota(jnp.int32, (BLK, LANES), 1)
    wide = jnp.zeros((BLK, LANES), F32)
    for c in range(3):
        wide = jnp.where(lane == c, cols[c], wide)
    return wide.T[:8]


def three_rows(rows):
    sub = lax.broadcasted_iota(jnp.int32, (8, LANES), 0)
    out = jnp.zeros((8, LANES), F32)
    for c in range(3):
        out = jnp.where(sub == c, rows[c], out)
    return out


def pack_kernel(nb, me_ref, list_ref, pos_ref, spec_ref, own_ref):
    own_ref[...] = jnp.zeros_like(own_ref)
    own_ref[0:3] = pos_ref[...]
    own_ref[3:4] = spec_ref[...].astype(F32)
    for b in range(nb):
        for s in range(3):
            listed = list_ref[b, s]
            ok = jnp.logical_and(listed == me_ref[0] * nb + (b - 1 + s), listed >= 0)
            own_ref[4 + s : 5 + s, b * BLK : (b + 1) * BLK] = jnp.full((1, BLK), ok.astype(F32))


def first_kernel(
    nb, heads, hdim,
    me_ref, gam_ref, own_ref, ra_ref, rb_ref, embed_ref, gains_ref, outg_ref, ro_ref,
    wq_h, wk_h, wv_h, wo_h, wu_h, wd_h,
    e_out, ext_ref, gk_ref, o_ref, rl_ref, v_ref, x1_ref, gd_ref, e_ref, wo0, wu0, wd0,
    st_ref, q1_ref, k1_ref, v1_ref, o1_ref, rl1_ref, e1_ref, x11_ref, gd1_ref, top_ref, wq1, wk1, wv1, wo1, wu1, wd1,
    wq0, wk0, wv0, d2_ref, x0_ref, q_ref, k_ref, sem,
):
    qb = nb + 2
    kb = nb + 4
    mid = slice(BLK, (nb + 1) * BLK)
    sources = (wq_h, wk_h, wv_h, wo_h, wu_h, wd_h)
    targets = ((wq0, wk0, wv0, wo0, wu0, wd0), (wq1, wk1, wv1, wo1, wu1, wd1))
    copies = []
    for layer in range(2):
        copies.append([
            pltpu.make_async_copy(src.at[layer], dst, sem.at[layer, n])
            for n, (src, dst) in enumerate(zip(sources, targets[layer]))
        ])
        for c in copies[layer]:
            c.start()
    par = lax.rem(me_ref[0], 2)
    before, own, after = arrange(par, own_ref[...], ra_ref[...], rb_ref[...])
    ext = jnp.concatenate([before, own, after], axis=1)
    ext_ref[...] = ext
    gk_ref[...] = gains_ref[...]
    ext_t = ext.T
    distances(ext, ext_t, 1, d2_ref, qb)

    embed = embed_ref[...].astype(F32)
    normed = (embed * inv_rms(embed) * gains_ref[0, 0:1]).astype(BF16)
    scale = hdim ** (-0.5)
    spec = ext_t[:, 3:4].astype(jnp.int32)
    nspec = embed_ref.shape[0]
    onehot = (spec == lax.broadcasted_iota(jnp.int32, (kb * BLK, nspec), 1)).astype(F32).astype(BF16)
    onehot_q = onehot[BLK : (qb + 1) * BLK]
    x0_ref[...] = mm(onehot_q, embed_ref[...])
    for c in copies[0][:3]:
        c.wait()
    q_ref[...] = mm(onehot_q, (mm(normed, wq0[...]) * (scale * LOG2E)).astype(BF16)).astype(BF16)
    k_ref[...] = mm(onehot, mm(normed, wk0[...]).astype(BF16)).astype(BF16)
    v_ref[...] = mm(onehot, mm(normed, wv0[...]).astype(BF16)).astype(BF16)
    attend(q_ref, k_ref, v_ref, o_ref, rl_ref, e_ref, d2_ref, 0, gam_ref, 0, heads, hdim, qb)

    for c in copies[0][3:]:
        c.wait()

    def feed(layer, x1, w_up, w_down, keep):
        inner = (x1 * inv_rms(x1) * gains_ref[layer, 1:2]).astype(BF16)
        act, slope = gelu_both(mm(inner, w_up[...]))
        keep(slope.astype(BF16))
        return x1 + mm(act.astype(BF16), w_down[...])

    step = 2 * BLK
    for r in range(0, qb * BLK, step):
        rows = slice(r, r + step)
        x1 = x0_ref[rows] + mm(o_ref[rows], wo0[...])
        x1_ref[rows] = x1
        st_ref[rows] = feed(0, x1, wu0, wd0, lambda slope: gd_ref.__setitem__(rows, slope))

    for c in copies[1]:
        c.wait()
    gain = gains_ref[1, 0:1]
    st = st_ref[...]
    normed = (st * inv_rms(st) * gain).astype(BF16)
    q1_ref[...] = (mm(normed[mid], wq1[...]) * (scale * LOG2E)).astype(BF16)
    k1_ref[...] = mm(normed, wk1[...]).astype(BF16)
    v1_ref[...] = mm(normed, wv1[...]).astype(BF16)
    attend(q1_ref, k1_ref, v1_ref, o1_ref, rl1_ref, e1_ref, d2_ref, 1, gam_ref, 1, heads, hdim, nb)
    x1 = st_ref[mid] + mm(o1_ref[...], wo1[...])
    x11_ref[...] = x1
    x2 = feed(1, x1, wu1, wd1, lambda slope: gd1_ref.__setitem__(..., slope))

    w = outg_ref[...] * ro_ref[...]
    r = inv_rms(x2)
    along = jnp.sum(x2 * w, axis=1, keepdims=True)
    e_out[...] = jnp.broadcast_to(jnp.sum(along * r), e_out.shape)
    width = x2.shape[1]
    top_ref[...] = r * (w - x2 * (r * r * along * (1.0 / width)))


def middle_kernel(
    nb, heads, hdim,
    me_ref, gam_ref, _, ext_ref, gains_ref, st_ref, q1_ref, k1_ref, v1_ref, o1_ref, rl1_ref, e1_ref, x1_ref, gd_ref, top_ref,
    wq, wk, wv, wo, wu, wd,
    paya_ref, payb_ref, part_ref, halo_ref, g1_ref,
    dq_ref, dk_ref, dv_ref, datt_ref,
):
    qb = nb + 2
    mid = slice(BLK, (nb + 1) * BLK)
    scale = hdim ** (-0.5)
    width = st_ref.shape[1]
    par = lax.rem(me_ref[0], 2)
    ext = ext_ref[...]
    ext_t = ext.T
    grad = top_ref[...]
    du = mm_nt(grad.astype(BF16), wd[...]).astype(BF16).astype(F32)
    dinner = mm_nt((du * gd_ref[...].astype(F32)).astype(BF16), wu[...]).astype(BF16).astype(F32)
    grad = grad + rms_back(x1_ref[...], gains_ref[1, 1:2], dinner)
    datt_ref[...] = mm_nt(grad.astype(BF16), wo[...]).astype(BF16).astype(F32)

    per = LANES // hdim
    groups = heads // per
    masks = head_masks(BLK, per, hdim)
    masks2 = head_masks(2 * BLK, per, hdim)
    masks3 = head_masks(3 * BLK, per, hdim)
    dk_ref[...] = jnp.zeros_like(dk_ref)
    dv_ref[...] = jnp.zeros_like(dv_ref)
    g1_ref[...] = jnp.zeros_like(g1_ref)
    for i in range(0, nb, 2):
        rows2 = slice(i * BLK, (i + 2) * BLK)
        for g in range(groups):
            cols = slice(g * LANES, (g + 1) * LANES)
            d_o = datt_ref[rows2, cols] * rl1_ref[rows2, cols]
            delta = delta_of(d_o * o1_ref[rows2, cols].astype(F32), per, hdim)
            d_o = d_o.astype(BF16)
            prods = pair_products(d_o, v1_ref[i * BLK : (i + 4) * BLK, cols], masks, masks2, per)
            for t in range(2):
                at = slice(t * BLK, (t + 1) * BLK)
                rows = slice((i + t) * BLK, (i + t + 1) * BLK)
                win = slice((i + t) * BLK, (i + t + 3) * BLK)
                outer_cols, shared_cols = window_parts(t)
                dos = stacked(d_o[at], masks)
                qs = stacked(q1_ref[rows, cols], masks)
                parts, es = [], []
                pair_outer = g1_ref[i + t, :, outer_cols]
                pair_shared = g1_ref[i + t, :, shared_cols]
                for h in range(per):
                    e = e1_ref[i + t, g * per + h]
                    outer, shared = prods[t][h]
                    gam = gam_ref[1, g * per + h]
                    outer = e[:, outer_cols].astype(F32) * (outer - delta[h][at])
                    shared = e[:, shared_cols].astype(F32) * (shared - delta[h][at])
                    pair_outer = pair_outer + gam * outer
                    pair_shared = pair_shared + gam * shared
                    outer, shared = outer.astype(BF16), shared.astype(BF16)
                    parts.append(jnp.concatenate([outer, shared] if t == 0 else [shared, outer], axis=1))
                    es.append(e)
                g1_ref[i + t, :, outer_cols] = pair_outer
                g1_ref[i + t, :, shared_cols] = pair_shared
                ks = stacked(k1_ref[win, cols], masks3)
                dq_ref[rows, cols] = (mm(jnp.concatenate(parts, axis=1), ks) * scale).astype(BF16)
                dk_ref[win, cols] += mm_tn(jnp.concatenate(parts, axis=0), qs)
                dv_ref[win, cols] += mm_tn(jnp.concatenate(es, axis=0), dos)
    dk = (dk_ref[...] * LN2).astype(BF16)
    dv = dv_ref[...].astype(BF16)
    dnorm = mm_nt(dk, wk[...]) + mm_nt(dv, wv[...])
    dq = mm_nt(dq_ref[...], wq[...])
    zeros = jnp.zeros((BLK, width), F32)
    dnorm = dnorm + jnp.concatenate([zeros, dq, zeros], axis=0)
    back = rms_back(st_ref[...], gains_ref[1, 0:1], dnorm.astype(BF16).astype(F32))
    part = grad + back[mid]
    part_ref[...] = part
    halo_ref[:BLK] = back[:BLK]
    halo_ref[BLK:] = back[(qb - 1) * BLK :]

    _, rows_low = fold(g1_ref[0, :, :BLK], ext, ext_t, 2, 1)
    _, rows_high = fold(g1_ref[nb - 1, :, 2 * BLK :], ext, ext_t, nb + 1, nb + 2)
    pad = jnp.zeros((8, width - LANES), F32)

    def payload(ref, halo, edge, rows):
        ref[:BLK] = halo.astype(BF16)
        ref[BLK : 2 * BLK] = edge.astype(BF16)
        tail = jnp.concatenate([three_rows(rows), pad], axis=1)
        ref[2 * BLK :] = jnp.concatenate([tail, jnp.zeros_like(tail)], axis=0).astype(BF16)

    def low(ref):
        payload(ref, back[:BLK], part[:BLK], rows_low)

    def high(ref):
        payload(ref, back[(qb - 1) * BLK :], part[(nb - 1) * BLK :], rows_high)

    @pl.when(par == 0)
    def _():
        high(paya_ref)
        low(payb_ref)

    @pl.when(par != 0)
    def _():
        low(paya_ref)
        high(payb_ref)


def last_kernel(
    nb, heads, hdim,
    me_ref, gam_ref, _, ext_ref, gains_ref, paya_ref, payb_ref, part_ref, halo_ref, g1_ref,
    o_ref, rl_ref, v_ref, x1_ref, gd_ref, e_ref, wo, wu, wd,
    f_ref,
    datt_ref,
):
    qb = nb + 2
    par = lax.rem(me_ref[0], 2)
    ext = ext_ref[...]
    ext_t = ext.T
    from_low, _, from_high = arrange(par, None, paya_ref[...], payb_ref[...])
    from_low = from_low.astype(F32)
    from_high = from_high.astype(F32)
    part = part_ref[...]
    pieces = [halo_ref[:BLK] + from_low[BLK : 2 * BLK]]
    own_parts = [part[i * BLK : (i + 1) * BLK] for i in range(nb)]
    own_parts[0] = own_parts[0] + from_low[:BLK]
    own_parts[-1] = own_parts[-1] + from_high[:BLK]
    pieces += own_parts
    pieces.append(halo_ref[BLK:] + from_high[BLK : 2 * BLK])
    grad = jnp.concatenate(pieces, axis=0)
    du = mm_nt(grad.astype(BF16), wd[...]).astype(BF16).astype(F32)
    dinner = mm_nt((du * gd_ref[...].astype(F32)).astype(BF16), wu[...]).astype(BF16).astype(F32)
    grad = grad + rms_back(x1_ref[...], gains_ref[0, 1:2], dinner)
    datt_ref[...] = mm_nt(grad.astype(BF16), wo[...]).astype(BF16).astype(F32)

    per = LANES // hdim
    groups = heads // per
    masks = head_masks(BLK, per, hdim)
    masks2 = head_masks(2 * BLK, per, hdim)

    def cotangents(rows, cols):
        d_o = datt_ref[rows, cols] * rl_ref[rows, cols]
        return d_o.astype(BF16), delta_of(d_o * o_ref[rows, cols].astype(F32), per, hdim)

    forces = [jnp.zeros((8, LANES), F32) for _ in range(nb)]
    forces[0] = forces[0] + from_low[2 * BLK : 2 * BLK + 8, :LANES]
    forces[-1] = forces[-1] + from_high[2 * BLK : 2 * BLK + 8, :LANES]
    for i in range(0, nb, 2):
        rows2 = slice((i + 1) * BLK, (i + 3) * BLK)
        parts = [[g1_ref[i + t, :, c] for c in window_parts(t)] for t in range(2)]
        for g in range(groups):
            cols = slice(g * LANES, (g + 1) * LANES)
            d_o, delta = cotangents(rows2, cols)
            prods = pair_products(d_o, v_ref[(i + 1) * BLK : (i + 5) * BLK, cols], masks, masks2, per)
            for t in range(2):
                at = slice(t * BLK, (t + 1) * BLK)
                for h in range(per):
                    gam = gam_ref[0, g * per + h]
                    for n, c in enumerate(window_parts(t)):
                        e = e_ref[i + t + 1, g * per + h, :, c].astype(F32)
                        parts[t][n] = parts[t][n] + gam * (e * (prods[t][h][n] - delta[h][at]))
        for t in range(2):
            outer, shared = parts[t]
            total = jnp.concatenate([outer, shared] if t == 0 else [shared, outer], axis=1)
            sums = None
            for s in range(3):
                cols, rows = fold(total[:, s * BLK : (s + 1) * BLK], ext, ext_t, i + t + 2, i + t + 1 + s)
                sums = cols if sums is None else [a + b for a, b in zip(sums, cols)]
                j = i + t - 1 + s
                if 0 <= j < nb:
                    forces[j] = forces[j] + three_rows(rows)
            forces[i + t] = forces[i + t] + columns_to_rows(sums)
    last = qb - 1
    ends = [jnp.zeros((BLK, BLK), F32), jnp.zeros((BLK, BLK), F32)]
    for g in range(groups):
        cols = slice(g * LANES, (g + 1) * LANES)
        low_o, low_delta = cotangents(slice(0, BLK), cols)
        high_o, high_delta = cotangents(slice(last * BLK, qb * BLK), cols)
        both = jnp.concatenate([low_o, high_o], axis=1)
        both = jnp.concatenate([both * jnp.concatenate([m, m], axis=1) for m in masks], axis=0)
        prods = mm_nt(both, beside(v_ref[2 * BLK : 3 * BLK, cols], v_ref[last * BLK : qb * BLK, cols]))
        for h in range(per):
            gam = gam_ref[0, g * per + h]
            low = prods[h * BLK : (h + 1) * BLK, :BLK] - low_delta[h]
            high = prods[h * BLK : (h + 1) * BLK, BLK:] - high_delta[h]
            ends[0] = ends[0] + gam * (e_ref[0, g * per + h, :, 2 * BLK :].astype(F32) * low)
            ends[1] = ends[1] + gam * (e_ref[last, g * per + h, :, :BLK].astype(F32) * high)
    _, rows = fold(ends[0], ext, ext_t, 1, 2)
    forces[0] = forces[0] + three_rows(rows)
    _, rows = fold(ends[1], ext, ext_t, nb + 2, nb + 1)
    forces[-1] = forces[-1] + three_rows(rows)
    f_ref[...] = jnp.concatenate(forces, axis=1)[:3]


def swap_a(x):
    n = lax.axis_size("chain")
    return lax.ppermute(x, "chain", [(i, i ^ 1) for i in range(n)])


def swap_b(x):
    n = lax.axis_size("chain")
    return lax.ppermute(x, "chain", [(i, ((i + 1) ^ 1) - 1) for i in range(1, n - 1)])


def hop(x, step):
    return lax.ppermute(x, "chain", [(i, i ^ step) for i in range(lax.axis_size("chain"))])


def local(
    species, positions, block_list, embed, w_query, w_key, w_value, w_out, w_up, w_down, norm_gains, gammas, out_gain, readout
):
    atoms = species.shape[0]
    nb = atoms // BLK
    width = embed.shape[1]
    layers, heads = gammas.shape
    hdim = width // heads
    ff = w_up.shape[2]
    qb, kb = nb + 2, nb + 4
    count = lax.axis_size("chain")
    assert nb >= 2 and layers == 2 and LANES % hdim == 0 and nb % 2 == 0 and count >= 8 and count & (count - 1) == 0
    me = lax.axis_index("chain").astype(jnp.int32)
    vm = pltpu.VMEM
    smem = pl.BlockSpec(memory_space=pltpu.SMEM)

    def work(products):
        return pl.CostEstimate(flops=products * atoms * width * width * 8, transcendentals=0, bytes_accessed=0)

    vmem = pl.BlockSpec(memory_space=vm)
    keep = functools.partial(pltpu.with_memory_space_constraint, memory_space=vm)
    place = me.reshape(1)
    own = pl.pallas_call(
        functools.partial(pack_kernel, nb),
        out_shape=vm((8, atoms), F32),
        in_specs=[smem, smem, vmem, vmem],
        out_specs=vmem,
    )(place, block_list, positions, species.reshape(1, atoms))
    edge = 2 * BLK
    if atoms == edge:
        send_a = send_b = own
    else:
        first, last = own[:, :edge], own[:, -edge:]
        send_a = jnp.where(me % 2 == 0, last, first)
        send_b = jnp.where(me % 2 == 0, first, last)
    near_a, near_b = swap_a(send_a), swap_b(send_b)
    pin = functools.partial(pltpu.with_memory_space_constraint, memory_space=pltpu.HBM)
    weights = (w_query, w_key, w_value, w_out, w_up, w_down)
    shapes = [vm((width, width), BF16)] * 4 + [vm((width, ff), BF16), vm((ff, width), BF16)]
    first = pl.pallas_call(
        functools.partial(first_kernel, nb, heads, hdim),
        out_shape=[
            vm((8, LANES), F32), vm((8, kb * BLK), F32), vm(norm_gains.shape, F32),
            vm((qb * BLK, width), BF16), vm((qb * BLK, width), F32), vm((kb * BLK, width), BF16),
            vm((qb * BLK, width), F32), vm((qb * BLK, ff), BF16), vm((qb, heads, BLK, 3 * BLK), BF16), *shapes[3:],
            vm((qb * BLK, width), F32), vm((nb * BLK, width), BF16), vm((qb * BLK, width), BF16),
            vm((qb * BLK, width), BF16), vm((nb * BLK, width), BF16), vm((nb * BLK, width), F32),
            vm((nb, heads, BLK, 3 * BLK), BF16), vm((nb * BLK, width), F32), vm((nb * BLK, ff), BF16),
            vm((nb * BLK, width), F32), *shapes,
        ],
        in_specs=[smem, smem] + [vmem] * 7 + [pl.BlockSpec(memory_space=pltpu.HBM)] * 6,
        out_specs=[vmem] * 28,
        scratch_shapes=[
            *shapes[:3], vm((qb, BLK, 3 * BLK), F32), vm((qb * BLK, width), F32), vm((qb * BLK, width), BF16),
            vm((kb * BLK, width), BF16), pltpu.SemaphoreType.DMA((2, 6)),
        ],
        compiler_params=pltpu.CompilerParams(vmem_limit_bytes=20 * 1024 * 1024),
        cost_estimate=work(qb * 7),
    )(
        place, gammas, keep(own), keep(near_a), keep(near_b), pin(embed), pin(norm_gains),
        pin(out_gain.reshape(1, width)), pin(readout.reshape(1, width)), *(pin(w) for w in weights),
    )
    energy, ext, gains = first[0], keep(first[1]), keep(first[2])
    saved0 = [keep(x) for x in first[3:12]]
    saved1 = [keep(x) for x in first[12:]]
    energy = energy + hop(energy, 1)
    pay = vm((2 * BLK + 16, width), BF16)
    pay_a, pay_b, part, halo, pairs = pl.pallas_call(
        functools.partial(middle_kernel, nb, heads, hdim),
        out_shape=[pay, pay, vm((nb * BLK, width), F32), vm((2 * BLK, width), F32), vm((nb, BLK, 3 * BLK), F32)],
        in_specs=[smem, smem] + [vmem] * 19,
        out_specs=[vmem] * 5,
        scratch_shapes=[
            vm((nb * BLK, width), BF16), vm((qb * BLK, width), F32), vm((qb * BLK, width), F32), vm((nb * BLK, width), F32),
        ],
        compiler_params=pltpu.CompilerParams(vmem_limit_bytes=20 * 1024 * 1024),
        cost_estimate=work(nb * 9),
    )(place, gammas, keep(energy), ext, gains, *saved1)
    energy = energy + hop(energy, 2)
    energy, pay_a, pay_b = lax.optimization_barrier((energy, pay_a, pay_b))
    arriving = hop(energy, 4)
    got_a, got_b = swap_a(pay_a), swap_b(pay_b)
    energy = energy + arriving
    forces = pl.pallas_call(
        functools.partial(last_kernel, nb, heads, hdim),
        out_shape=jax.ShapeDtypeStruct((3, atoms), F32),
        in_specs=[smem, smem] + [vmem] * 17,
        out_specs=vmem,
        scratch_shapes=[vm((qb * BLK, width), F32)],
        compiler_params=pltpu.CompilerParams(vmem_limit_bytes=20 * 1024 * 1024),
        cost_estimate=work(qb * 3),
    )(
        place, gammas, keep(energy), ext, gains, keep(got_a), keep(got_b), keep(part), keep(halo), keep(pairs), *saved0
    )
    if count > 8:
        arriving = hop(energy, 8)
        energy, forces = lax.optimization_barrier((energy, forces))
        energy = energy + arriving
    step = 16
    while step < count:
        energy = energy + hop(energy, step)
        step *= 2
    return energy[:1, :1].reshape(1), forces


def solution(mesh):
    sharded = ("frames", "chain")
    return jax.shard_map(
        local,
        mesh=mesh,
        in_specs=(P(sharded), P(None, sharded), P(sharded, None)) + (P(),) * 11,
        out_specs=(P("frames"), P(None, sharded)),
        check_vma=False,
    )
```

time: 67.7 us -> 54.2 us (0.80)
  starting transfers between devices: 21 us -> 15.1 us
  between operations: 5.07 us -> 0.7 us
  waiting for transfers between devices: 2.4 us -> 6.18 us
  local copies, waits for them, and re-layouts: 4.12 us -> 1.2 us
  other arithmetic: 2.2 us -> 0.01 us
  Pallas kernels: 32.6 us -> 30.7 us
    pallas_call x1, Pallas kernels: 23.3 us -> 17 us  [local(): pl.pallas_call(functools.partial(first_kernel, nb, heads, hdim), out_shap...]
    ppermute x4, starting transfers between devices: 15 us -> 9.3 us  [hop(): lax.ppermute(x, 'chain', [(i, i ^ step) for i in range(lax.axis_size('cha...]
    pallas_call x1 -> x3, Pallas kernels: 9.29 us -> 13.7 us  [the longest x1 7.04 us: local(): pl.pallas_call(functools.partial(middle_kernel, nb, heads, hdim), out_sha...]
    ppermute x4, waiting for transfers between devices: 2.38 us -> 5.35 us  [hop(): lax.ppermute(x, 'chain', [(i, i ^ step) for i in range(lax.axis_size('cha...]
    reshape x1 -> x0, local copies, waits for them, and re-layouts: 1.31 us -> none  [local(): gains = norm_gains.reshape(2 * layers, width)]
    ppermute x2, waiting for transfers between devices: 0.01 us -> 0.83 us  [swap_a(): return lax.ppermute(x, 'chain', [(i, i ^ 1) for i in range(n)])]
    unnamed x12 -> x4, local copies, waits for them, and re-layouts: 1.44 us -> 0.68 us
    concatenate x1 -> x0, other arithmetic: 0.76 us -> none  [local(): jnp.concatenate([positions, species.astype(F32)[None], jnp.repeat(valid.T...]
  transfers between devices with their start and end apart: 8 -> 8, of which waited for: 4 -> 3; matrix products, arithmetic and copies ran while one was open for 4% -> 0% of each run, Pallas kernels for 0% -> 24%
where the time goes in v2:
time: 54.2 us; the launch traced here: 54 us
  Pallas kernels  30.7 us (57%)
  starting transfers between devices  15.1 us (28%)
  waiting for transfers between devices  6.18 us (11%)
  local copies, waits for them, and re-layouts  1.2 us (2%)
  between operations  0.7 us (1%)
    pallas_call x1, Pallas kernels, local(): pl.pallas_call(functools.partial(first_kernel, nb, heads, hdim), out_shap...  17 us
    ppermute x4, starting transfers between devices, hop(): lax.ppermute(x, 'chain', [(i, i ^ step) for i in range(lax.axis_size('cha...  9.3 us
    pallas_call x1, Pallas kernels, local(): pl.pallas_call(functools.partial(middle_kernel, nb, heads, hdim), out_sha...  7.04 us
    pallas_call x1, Pallas kernels, local(): pl.pallas_call(functools.partial(last_kernel, nb, heads, hdim), out_shape...  5.96 us
    ppermute x4, waiting for transfers between devices, hop(): lax.ppermute(x, 'chain', [(i, i ^ step) for i in range(lax.axis_size('cha...  5.35 us
    ppermute x2, starting transfers between devices, swap_a(): return lax.ppermute(x, 'chain', [(i, i ^ 1) for i in range(n)])  4.52 us
    ppermute x2, starting transfers between devices, swap_b(): lax.ppermute(x, 'chain', [(i, (i + 1 ^ 1) - 1) for i in range(1, n - 1)])  1.33 us
  transfers between devices with their start and end apart: 8, of which 3 were waited for; matrix products, arithmetic and copies ran while one was open for 0% of the time, Pallas kernels for 24%

profile of v2, /device:TPU:0, one launch (start us, length us, event | category | flops | bytes accessed | tf_op | source)
XLA Modules:
  0.0 54.0 jit_solution(12598686283912565129)
XLA Ops:
  0.6 0.7 %shard_map.149.own_ref = f32[8,256]{1,0:T(8,128)S(1)} custom-call(s32[1]{0:T(128)} %bitcast.me_ref, s32[2,3]{1,0:T(2,128)} %list_ref.1, f32[3,256]{1,0:T(4,128)} %pos_ref.1, s32[1,256]{1,0:T(1,128)} %bitcast.5), custom_call_target="tpu_custom_call" | custom-call | tf_op jit(solution)/shard_map/pallas_call | solution.py:484
  1.4 0.7 %collective-permute-start.1 = (f32[8,256]{1,0:T(8,128)S(1)}, f32[8,256]{1,0:T(8,128)S(1)}, u32[]{:S(2)}, u32[]{:S(2)}) collective-permute-start(f32[8,256]{1,0:T(8,128)S(1)} %shard_map.149.own_ref), channel_id=1, source_target_pairs={{1,2},{2,1},{3,4},{4,3},{5,6},{6,5},{7,8},{8,7},{9,10},{10,9},{11,... | collective-permute-start | bytes 24584 | tf_op jit(solution)/shard_map/ppermute | solution.py:455
  2.0 4.4 %collective-permute-start = (f32[8,256]{1,0:T(8,128)S(1)}, f32[8,256]{1,0:T(8,128)S(1)}, u32[]{:S(2)}, u32[]{:S(2)}) collective-permute-start(f32[8,256]{1,0:T(8,128)S(1)} %shard_map.149.own_ref), channel_id=1, source_target_pairs={{0,1},{1,0},{2,3},{3,2},{4,5},{5,4},{6,7},{7,6},{8,9},{9,8},{10,11... | collective-permute-start | bytes 24584 | tf_op jit(solution)/shard_map/ppermute | solution.py:450
  6.4 0.0 collective-permute-done.1.rb_ref
  6.4 0.8 %collective-permute-done.ra_ref = f32[8,256]{1,0:T(8,128)S(1)} collective-permute-done((f32[8,256]{1,0:T(8,128)S(1)}, f32[8,256]{1,0:T(8,128)S(1)}, u32[]{:S(2)}, u32[]{:S(2)}) %collective-permute-start) | collective-permute-done | bytes 8224 | tf_op jit(solution)/shard_map/ppermute | solution.py:450
  7.3 0.0 copy-start
  7.3 0.7 %copy-done = f32[2,16]{1,0:T(2,128)S(1)} copy-done((f32[2,16]{1,0:T(2,128)S(1)}, f32[2,16]{1,0:T(2,128)}, u32[]{:S(2)}) %copy-start) | copy-done | bytes 152
  7.9 0.0 copy-start.1
  7.9 17.0 %shard_map.150 = (f32[8,128]{1,0:T(8,128)S(1)}, f32[8,768]{1,0:T(8,128)S(1)}, f32[2,2,512]{2,1,0:T(2,128)S(1)}, bf16[512,512]{1,0:T(8,128)(2,1)S(1)}, f32[512,51...) custom-call(s32[1]{0:T(128)} %bitcast.me_ref, ...), custom_call_target="tpu_custom_call" | custom-call | flops 15032385536 | tf_op jit(solution)/shard_map/pallas_call | solution.py:501
  25.0 0.5 collective-permute-start.2
  25.5 0.8 %collective-permute-done.2 = f32[8,128]{1,0:T(8,128)S(1)} collective-permute-done((f32[8,128]{1,0:T(8,128)S(1)}, f32[8,128]{1,0:T(8,128)S(1)}, u32[]{:S(2)}, u32[]{:S(2)}) %collective-permute-start.2) | collective-permute-done | bytes 4128 | tf_op jit(solution)/shard_map/ppermute | solution.py:459
  26.3 2.4 %collective-permute-start.3 = (f32[8,128]{1,0:T(8,128)S(1)}, f32[8,128]{1,0:T(8,128)S(1)}, u32[]{:S(2)}, u32[]{:S(2)}) collective-permute-start(f32[8,128]{1,0:T(8,128)S(1)} %add.12._), channel_id=1, source_target_pairs={{0,2},{1,3},{2,0},{3,1},{4,6},{5,7},{6,4},{7,5},{8,10},{9,11},{10,... | collective-permute-start | bytes 12296 | tf_op jit(solution)/shard_map/ppermute | solution.py:459
  28.6 0.0 copy-done.1
  28.7 7.0 %shard_map.151 = (bf16[272,512]{1,0:T(8,128)(2,1)S(1)}, bf16[272,512]{1,0:T(8,128)(2,1)S(1)}, f32[256,512]{1,0:T(8,128)S(1)}, f32[256,512]{1,0:T(8,128)S(1)}, f32[2,128,384]{2,1,0:T(8,128)S(1)}) custom-call(s32[1]{0:T(128)} %bitcast.me_ref, f32[2,16]{1,0:T(2,128)S(1)} %copy-done.1, f32[8,128]{1,0:T(8,128)S(1)} %add.12._, ...), custom_call_target="tpu_custom_call" | custom-call | flops 9663676416 | tf_op jit(solution)/shard_map/pallas_call | solution.py:529
  35.7 0.0 collective-permute-done.3
  35.7 0.1 collective-permute-start.5
  35.8 0.7 %collective-permute-start.6 = (bf16[272,512]{1,0:T(8,128)(2,1)S(1)}, bf16[272,512]{1,0:T(8,128)(2,1)S(1)}, u32[]{:S(2)}, u32[]{:S(2)}) collective-permute-start(bf16[272,512]{1,0:T(8,128)(2,1)S(1)} %get-tuple-element.63), channel_id=1, source_target_pairs={{1,2},{2,1},{3,4},{4,3},{5,6},{6,5},{7,8},{8,7},{9,10},{10,9},{11,... | collective-permute-start | bytes 835592 | tf_op jit(solution)/shard_map/ppermute | solution.py:455
  36.5 2.9 %collective-permute-start.4 = (f32[8,128]{1,0:T(8,128)S(1)}, f32[8,128]{1,0:T(8,128)S(1)}, u32[]{:S(2)}, u32[]{:S(2)}) collective-permute-start(f32[8,128]{1,0:T(8,128)S(1)} %add.13), channel_id=1, source_target_pairs={{0,4},{1,5},{2,6},{3,7},{4,0},{5,1},{6,2},{7,3},{8,12},{9,13},{10,... | collective-permute-start | bytes 12296 | tf_op jit(solution)/shard_map/ppermute | solution.py:459
  39.4 4.5 %collective-permute-done.4 = f32[8,128]{1,0:T(8,128)S(1)} collective-permute-done((f32[8,128]{1,0:T(8,128)S(1)}, f32[8,128]{1,0:T(8,128)S(1)}, u32[]{:S(2)}, u32[]{:S(2)}) %collective-permute-start.4) | collective-permute-done | bytes 4128 | tf_op jit(solution)/shard_map/ppermute | solution.py:459
  43.9 3.6 %collective-permute-start.7 = (f32[8,128]{1,0:T(8,128)S(1)}, f32[8,128]{1,0:T(8,128)S(1)}, u32[]{:S(2)}, u32[]{:S(2)}) collective-permute-start(f32[8,128]{1,0:T(8,128)S(1)} %add.14._), channel_id=1, source_target_pairs={{0,8},{1,9},{2,10},{3,11},{4,12},{5,13},{6,14},{7,15},{8,0},{9,1},... | collective-permute-start | bytes 12296 | tf_op jit(solution)/shard_map/ppermute | solution.py:459
  47.5 0.0 collective-permute-done.5.paya_ref
  47.5 0.0 collective-permute-done.6.payb_ref
  47.5 6.0 %shard_map.152 = f32[3,256]{1,0:T(4,128)} custom-call(s32[1]{0:T(128)} %bitcast.me_ref, f32[2,16]{1,0:T(2,128)S(1)} %copy-done.1, f32[8,128]{1,0:T(8,128)S(1)} %add.14._, f32[8,768]{1,0:T(8,128)S(1)} %get-tuple-element.41.ext_ref, f32[2,2,512]{2,1,0:T(2,128)S(1)} %get-tuple-element.42.gains_ref, bf16[272,512]{1,0:T(8,128)(2,1)S(1)} %collective-permute-done.5.paya_ref, ...), custom_call_target="tpu_custom_call" | custom-call | flops 6442450944 | tf_op jit(solution)/shard_map/pallas_call | solution.py:545
  53.5 0.0 collective-permute-done.7
  53.5 0.5 slice.3
  (4 shorter events, 0.0 us)
Async XLA Ops:
  1.4 5.1 %collective-permute-start.1 = (f32[8,256]{1,0:T(8,128)S(1)}, f32[8,256]{1,0:T(8,128)S(1)}, u32[]{:S(2)}, u32[]{:S(2)}) collective-permute-start(f32[8,256]{1,0:T(8,128)S(1)} %shard_map.149.own_ref), channel_id=1, source_target_pairs={{1,2},{2,1},{3,4},{4,3},{5,6},{6,5},{7,8},{8,7},{9,10},{10,9},{11,... | collective-permute-start | bytes 24584 | tf_op jit(solution)/shard_map/ppermute | solution.py:455
  2.0 5.2 %collective-permute-start = (f32[8,256]{1,0:T(8,128)S(1)}, f32[8,256]{1,0:T(8,128)S(1)}, u32[]{:S(2)}, u32[]{:S(2)}) collective-permute-start(f32[8,256]{1,0:T(8,128)S(1)} %shard_map.149.own_ref), channel_id=1, source_target_pairs={{0,1},{1,0},{2,3},{3,2},{4,5},{5,4},{6,7},{7,6},{8,9},{9,8},{10,11... | collective-permute-start | bytes 24584 | tf_op jit(solution)/shard_map/ppermute | solution.py:450
  7.3 0.7 %copy-start = (f32[2,16]{1,0:T(2,128)S(1)}, f32[2,16]{1,0:T(2,128)}, u32[]{:S(2)}) copy-start(f32[2,16]{1,0:T(2,128)} %gam_ref.5) | copy-start | bytes 388
  7.9 20.7 %copy-start.1 = (f32[2,16]{1,0:T(2,128)S(1)}, f32[2,16]{1,0:T(2,128)}, u32[]{:S(2)}) copy-start(f32[2,16]{1,0:T(2,128)} %gam_ref.5) | copy-start | bytes 388
  25.0 1.3 %collective-permute-start.2 = (f32[8,128]{1,0:T(8,128)S(1)}, f32[8,128]{1,0:T(8,128)S(1)}, u32[]{:S(2)}, u32[]{:S(2)}) collective-permute-start(f32[8,128]{1,0:T(8,128)S(1)} %get-tuple-element.40), channel_id=1, source_target_pairs={{0,1},{1,0},{2,3},{3,2},{4,5},{5,4},{6,7},{7,6},{8,9},{9,8},{10,11... | collective-permute-start | bytes 12296 | tf_op jit(solution)/shard_map/ppermute | solution.py:459
  26.3 9.4 %collective-permute-start.3 = (f32[8,128]{1,0:T(8,128)S(1)}, f32[8,128]{1,0:T(8,128)S(1)}, u32[]{:S(2)}, u32[]{:S(2)}) collective-permute-start(f32[8,128]{1,0:T(8,128)S(1)} %add.12._), channel_id=1, source_target_pairs={{0,2},{1,3},{2,0},{3,1},{4,6},{5,7},{6,4},{7,5},{8,10},{9,11},{10,... | collective-permute-start | bytes 12296 | tf_op jit(solution)/shard_map/ppermute | solution.py:459
  35.7 11.8 %collective-permute-start.5 = (bf16[272,512]{1,0:T(8,128)(2,1)S(1)}, bf16[272,512]{1,0:T(8,128)(2,1)S(1)}, u32[]{:S(2)}, u32[]{:S(2)}) collective-permute-start(bf16[272,512]{1,0:T(8,128)(2,1)S(1)} %get-tuple-element.62), channel_id=1, source_target_pairs={{0,1},{1,0},{2,3},{3,2},{4,5},{5,4},{6,7},{7,6},{8,9},{9,8},{10,11... | collective-permute-start | bytes 835592 | tf_op jit(solution)/shard_map/ppermute | solution.py:450
  35.8 11.7 %collective-permute-start.6 = (bf16[272,512]{1,0:T(8,128)(2,1)S(1)}, bf16[272,512]{1,0:T(8,128)(2,1)S(1)}, u32[]{:S(2)}, u32[]{:S(2)}) collective-permute-start(bf16[272,512]{1,0:T(8,128)(2,1)S(1)} %get-tuple-element.63), channel_id=1, source_target_pairs={{1,2},{2,1},{3,4},{4,3},{5,6},{6,5},{7,8},{8,7},{9,10},{10,9},{11,... | collective-permute-start | bytes 835592 | tf_op jit(solution)/shard_map/ppermute | solution.py:455
  36.5 7.4 %collective-permute-start.4 = (f32[8,128]{1,0:T(8,128)S(1)}, f32[8,128]{1,0:T(8,128)S(1)}, u32[]{:S(2)}, u32[]{:S(2)}) collective-permute-start(f32[8,128]{1,0:T(8,128)S(1)} %add.13), channel_id=1, source_target_pairs={{0,4},{1,5},{2,6},{3,7},{4,0},{5,1},{6,2},{7,3},{8,12},{9,13},{10,... | collective-permute-start | bytes 12296 | tf_op jit(solution)/shard_map/ppermute | solution.py:459
  43.9 9.5 %collective-permute-start.7 = (f32[8,128]{1,0:T(8,128)S(1)}, f32[8,128]{1,0:T(8,128)S(1)}, u32[]{:S(2)}, u32[]{:S(2)}) collective-permute-start(f32[8,128]{1,0:T(8,128)S(1)} %add.14._), channel_id=1, source_target_pairs={{0,8},{1,9},{2,10},{3,11},{4,12},{5,13},{6,14},{7,15},{8,0},{9,1},... | collective-permute-start | bytes 12296 | tf_op jit(solution)/shard_map/ppermute | solution.py:459

commit v3 on v2

--- a/solution.py
+++ b/solution.py
@@ -43,9 +43,10 @@
 
 
 def gelu_both(x):
-    t = jnp.tanh(C0 * (x + C1 * x * x * x))
-    half = 0.5 * (1.0 + t)
-    return x * half, half + 0.5 * x * (1.0 - t * t) * (C0 + 3.0 * C0 * C1 * x * x)
+    sq = x * x
+    half = 0.5 + 0.5 * jnp.tanh(x * (C0 + (C0 * C1) * sq))
+    act = x * half
+    return act, half + act * (1.0 - half) * (2.0 * C0 + (6.0 * C0 * C1) * sq)
 
 
 def head_masks(rows, heads_per_group, hdim):
@@ -80,10 +81,10 @@
     return jnp.concatenate([jnp.concatenate([x, zero], axis=1), jnp.concatenate([zero, y], axis=1)], axis=0)
 
 
-def pair_products(a, b, masks, masks2, per):
-    shared = mm_nt(stacked(a, masks2), b[BLK : 3 * BLK])
-    both = jnp.concatenate([a[:BLK], a[BLK:]], axis=1)
-    both = jnp.concatenate([both * jnp.concatenate([m, m], axis=1) for m in masks], axis=0)
+def pair_products(a, b, masks2, per):
+    each = [a * m for m in masks2]
+    shared = mm_nt(jnp.concatenate(each, axis=0), b[BLK : 3 * BLK])
+    both = jnp.concatenate([jnp.concatenate([x[:BLK], x[BLK:]], axis=1) for x in each], axis=0)
     outer = mm_nt(both, beside(b[:BLK], b[3 * BLK :]))
     got = []
     for t in range(2):
@@ -91,47 +92,97 @@
             (outer[h * BLK : (h + 1) * BLK, t * BLK : (t + 1) * BLK], shared[(2 * h + t) * BLK : (2 * h + t + 1) * BLK])
             for h in range(per)
         ])
-    return got
+    return got, each
+
+
+def span(first, size, unit):
+    if isinstance(first, int):
+        return slice(first * unit, first * unit + size)
+    return pl.ds(pl.multiple_of(first * unit, unit), size)
+
+
+def blocks_at(first, count):
+    return span(first, count * BLK, BLK)
+
+
+def group_at(g):
+    return span(g, LANES, LANES)
+
+
+def over(pairs, groups, body, rolled=False):
+    if rolled:
+        lax.fori_loop(0, pairs * groups, lambda n, _: (body(2 * lax.div(n, groups), lax.rem(n, groups)), 0)[1], 0)
+    else:
+        for n in range(pairs * groups):
+            body(2 * (n // groups), n % groups)
 
 
 def window_parts(t):
     return (slice(0, BLK), slice(BLK, 3 * BLK)) if t == 0 else (slice(2 * BLK, 3 * BLK), slice(0, 2 * BLK))
 
 
-def attend(q_ref, k_ref, v_ref, o_ref, rl_ref, e_ref, d2_ref, d2_first, gam_ref, layer, heads, hdim, count):
+def head_norms(x, hdim):
+    width = x.shape[1]
+    lane = lax.broadcasted_iota(jnp.int32, (width, LANES), 0) // hdim
+    member = (lane == lax.broadcasted_iota(jnp.int32, (width, LANES), 1)).astype(F32).astype(BF16)
+    x = x.astype(F32)
+    return jnp.max(mm((x * x).astype(BF16), member), axis=0, keepdims=True)
+
+
+def small_scores(q, k, hdim):
+    return jnp.max(head_norms(q, hdim) * head_norms(k, hdim)) < 3600.0
+
+
+def attend(exact, q_ref, k_ref, vm_ref, o_ref, rl_ref, e_ref, d2_ref, d2_first, gam_ref, layer, heads, hdim, count):
     per = LANES // hdim
     groups = heads // per
-    masks = head_masks(BLK, per, hdim)
     masks2 = head_masks(2 * BLK, per, hdim)
-    masks3 = head_masks(3 * BLK, per, hdim)
-    ones = jnp.concatenate(masks3, axis=0)
-    for i in range(0, count, 2):
-        for g in range(groups):
-            cols = slice(g * LANES, (g + 1) * LANES)
-            scores = pair_products(
-                q_ref[i * BLK : (i + 2) * BLK, cols], k_ref[i * BLK : (i + 4) * BLK, cols], masks, masks2, per
-            )
-            for t in range(2):
-                outer_cols, shared_cols = window_parts(t)
-                parts = []
-                for h in range(per):
-                    gam = gam_ref[layer, g * per + h] * LOG2E
-                    outer, shared = scores[t][h]
-                    outer = outer - gam * d2_ref[d2_first + i + t, :, outer_cols]
-                    shared = shared - gam * d2_ref[d2_first + i + t, :, shared_cols]
+    ones2 = jnp.concatenate(masks2, axis=0)
+    ones1 = jnp.concatenate([m[:BLK] for m in masks2], axis=0)
+
+    def values(first, blocks, cols, ones):
+        rows = blocks_at(first, blocks)
+        return jnp.concatenate([jnp.concatenate([vm_ref[h, rows, cols] for h in range(per)], axis=0), ones], axis=1)
+
+    def body(i, g):
+        cols = group_at(g)
+        scores, _ = pair_products(q_ref[blocks_at(i, 2), cols], k_ref[blocks_at(i, 4), cols], masks2, per)
+        sides, middles = [], []
+        for t in range(2):
+            outer_cols, shared_cols = window_parts(t)
+            outers, shareds = [], []
+            for h in range(per):
+                gam = gam_ref[layer, g * per + h] * LOG2E
+                outer, shared = scores[t][h]
+                outer = outer - gam * d2_ref[d2_first + i + t, :, outer_cols]
+                shared = shared - gam * d2_ref[d2_first + i + t, :, shared_cols]
+                if exact:
                     peak = jnp.maximum(jnp.maximum(outer, shared[:, :BLK]), shared[:, BLK:])
                     peak = jnp.max(peak, axis=1, keepdims=True)
-                    outer = jnp.exp2(outer - peak).astype(BF16)
-                    shared = jnp.exp2(shared - peak).astype(BF16)
-                    e = jnp.concatenate([outer, shared] if t == 0 else [shared, outer], axis=1)
-                    e_ref[i + t, g * per + h] = e
-                    parts.append(e)
-                rows = slice((i + t) * BLK, (i + t + 1) * BLK)
-                v = v_ref[(i + t) * BLK : (i + t + 3) * BLK, cols]
-                out = mm(jnp.concatenate(parts, axis=1), jnp.concatenate([stacked(v, masks3), ones], axis=1))
-                rl = 1.0 / out[:, LANES:]
-                rl_ref[rows, cols] = rl
-                o_ref[rows, cols] = (out[:, :LANES] * rl).astype(BF16)
+                    outer, shared = outer - peak, shared - peak
+                outer = jnp.exp2(outer).astype(BF16)
+                shared = jnp.exp2(shared).astype(BF16)
+                e_ref[i + t, g * per + h, :, outer_cols] = outer
+                e_ref[i + t, g * per + h, :, shared_cols] = shared
+                outers.append(outer)
+                shareds.append(shared)
+            middles.append(jnp.concatenate(shareds, axis=1))
+            sides.append(mm(jnp.concatenate(outers, axis=1), values(i + 3 * t, 1, cols, ones1)))
+        out = mm(jnp.concatenate(middles, axis=0), values(i + 1, 2, cols, ones2)) + jnp.concatenate(sides, axis=0)
+        rl = 1.0 / jnp.maximum(out[:, LANES:], 1e-37)
+        rl_ref[blocks_at(i, 2), cols] = rl
+        o_ref[blocks_at(i, 2), cols] = (out[:, :LANES] * rl).astype(BF16)
+
+    over(count // 2, groups, body, rolled=exact)
+
+
+def split_heads(v_ref, vm_ref, hdim):
+    rows, width = v_ref.shape
+    masks = head_masks(BLK, LANES // hdim, hdim)
+    for r in range(0, rows, BLK):
+        for c in range(0, width, LANES):
+            for h, m in enumerate(masks):
+                vm_ref[h, r : r + BLK, c : c + LANES] = v_ref[r : r + BLK, c : c + LANES] * m
 
 
 def delta_of(prod, per, hdim):
@@ -182,7 +233,7 @@
     wq_h, wk_h, wv_h, wo_h, wu_h, wd_h,
     e_out, ext_ref, gk_ref, o_ref, rl_ref, v_ref, x1_ref, gd_ref, e_ref, wo0, wu0, wd0,
     st_ref, q1_ref, k1_ref, v1_ref, o1_ref, rl1_ref, e1_ref, x11_ref, gd1_ref, top_ref, wq1, wk1, wv1, wo1, wu1, wd1,
-    wq0, wk0, wv0, d2_ref, x0_ref, q_ref, k_ref, sem,
+    wq0, wk0, wv0, d2_ref, x0_ref, q_ref, k_ref, vm_ref, vm1_ref, sem,
 ):
     qb = nb + 2
     kb = nb + 4
@@ -215,46 +266,62 @@
     x0_ref[...] = mm(onehot_q, embed_ref[...])
     for c in copies[0][:3]:
         c.wait()
-    q_ref[...] = mm(onehot_q, (mm(normed, wq0[...]) * (scale * LOG2E)).astype(BF16)).astype(BF16)
-    k_ref[...] = mm(onehot, mm(normed, wk0[...]).astype(BF16)).astype(BF16)
+    q_table = (mm(normed, wq0[...]) * (scale * LOG2E)).astype(BF16)
+    q_ref[...] = mm(onehot_q, q_table).astype(BF16)
+    k_table = mm(normed, wk0[...]).astype(BF16)
+    k_ref[...] = mm(onehot, k_table).astype(BF16)
     v_ref[...] = mm(onehot, mm(normed, wv0[...]).astype(BF16)).astype(BF16)
-    attend(q_ref, k_ref, v_ref, o_ref, rl_ref, e_ref, d2_ref, 0, gam_ref, 0, heads, hdim, qb)
-
-    for c in copies[0][3:]:
-        c.wait()
-
-    def feed(layer, x1, w_up, w_down, keep):
-        inner = (x1 * inv_rms(x1) * gains_ref[layer, 1:2]).astype(BF16)
-        act, slope = gelu_both(mm(inner, w_up[...]))
-        keep(slope.astype(BF16))
-        return x1 + mm(act.astype(BF16), w_down[...])
-
-    step = 2 * BLK
-    for r in range(0, qb * BLK, step):
-        rows = slice(r, r + step)
-        x1 = x0_ref[rows] + mm(o_ref[rows], wo0[...])
-        x1_ref[rows] = x1
-        st_ref[rows] = feed(0, x1, wu0, wd0, lambda slope: gd_ref.__setitem__(rows, slope))
-
-    for c in copies[1]:
-        c.wait()
-    gain = gains_ref[1, 0:1]
-    st = st_ref[...]
-    normed = (st * inv_rms(st) * gain).astype(BF16)
-    q1_ref[...] = (mm(normed[mid], wq1[...]) * (scale * LOG2E)).astype(BF16)
-    k1_ref[...] = mm(normed, wk1[...]).astype(BF16)
-    v1_ref[...] = mm(normed, wv1[...]).astype(BF16)
-    attend(q1_ref, k1_ref, v1_ref, o1_ref, rl1_ref, e1_ref, d2_ref, 1, gam_ref, 1, heads, hdim, nb)
-    x1 = st_ref[mid] + mm(o1_ref[...], wo1[...])
-    x11_ref[...] = x1
-    x2 = feed(1, x1, wu1, wd1, lambda slope: gd1_ref.__setitem__(..., slope))
-
-    w = outg_ref[...] * ro_ref[...]
-    r = inv_rms(x2)
-    along = jnp.sum(x2 * w, axis=1, keepdims=True)
-    e_out[...] = jnp.broadcast_to(jnp.sum(along * r), e_out.shape)
-    width = x2.shape[1]
-    top_ref[...] = r * (w - x2 * (r * r * along * (1.0 / width)))
+    split_heads(v_ref, vm_ref, hdim)
+
+    def run(exact):
+        def arrived(some):
+            if not exact:
+                for c in some:
+                    c.wait()
+
+        attend(exact, q_ref, k_ref, vm_ref, o_ref, rl_ref, e_ref, d2_ref, 0, gam_ref, 0, heads, hdim, qb)
+
+        arrived(copies[0][3:])
+
+        def feed(layer, x1, w_up, w_down, keep):
+            inner = (x1 * inv_rms(x1) * gains_ref[layer, 1:2]).astype(BF16)
+            act, slope = gelu_both(mm(inner, w_up[...]))
+            keep(slope.astype(BF16))
+            return x1 + mm(act.astype(BF16), w_down[...])
+
+        step = 4 * BLK
+        for r in range(0, qb * BLK, step):
+            rows = slice(r, r + step)
+            x1 = x0_ref[rows] + mm(o_ref[rows], wo0[...])
+            x1_ref[rows] = x1
+            st_ref[rows] = feed(0, x1, wu0, wd0, lambda slope: gd_ref.__setitem__(rows, slope))
+
+        arrived(copies[1])
+        gain = gains_ref[1, 0:1]
+        st = st_ref[...]
+        normed = (st * inv_rms(st) * gain).astype(BF16)
+        q1_ref[...] = (mm(normed[mid], wq1[...]) * (scale * LOG2E)).astype(BF16)
+        k1_ref[...] = mm(normed, wk1[...]).astype(BF16)
+        v1_ref[...] = mm(normed, wv1[...]).astype(BF16)
+        split_heads(v1_ref, vm1_ref, hdim)
+        attend(exact, q1_ref, k1_ref, vm1_ref, o1_ref, rl1_ref, e1_ref, d2_ref, 1, gam_ref, 1, heads, hdim, nb)
+        x1 = st_ref[mid] + mm(o1_ref[...], wo1[...])
+        x11_ref[...] = x1
+        x2 = feed(1, x1, wu1, wd1, lambda slope: gd1_ref.__setitem__(..., slope))
+
+        w = outg_ref[...] * ro_ref[...]
+        r = inv_rms(x2)
+        along = jnp.sum(x2 * w, axis=1, keepdims=True)
+        e_out[...] = jnp.broadcast_to(jnp.sum(along * r), e_out.shape)
+        width = x2.shape[1]
+        top_ref[...] = r * (w - x2 * (r * r * along * (1.0 / width)))
+
+    run(False)
+    small = jnp.logical_and(small_scores(q_table, k_table, hdim), small_scores(q1_ref[...], k1_ref[...], hdim))
+
+    @pl.when(jnp.logical_not(small))
+    def _():
+        run(True)
 
 
 def middle_kernel(
@@ -279,47 +346,48 @@
 
     per = LANES // hdim
     groups = heads // per
-    masks = head_masks(BLK, per, hdim)
     masks2 = head_masks(2 * BLK, per, hdim)
     masks3 = head_masks(3 * BLK, per, hdim)
     dk_ref[...] = jnp.zeros_like(dk_ref)
     dv_ref[...] = jnp.zeros_like(dv_ref)
     g1_ref[...] = jnp.zeros_like(g1_ref)
-    for i in range(0, nb, 2):
-        rows2 = slice(i * BLK, (i + 2) * BLK)
-        for g in range(groups):
-            cols = slice(g * LANES, (g + 1) * LANES)
-            d_o = datt_ref[rows2, cols] * rl1_ref[rows2, cols]
-            delta = delta_of(d_o * o1_ref[rows2, cols].astype(F32), per, hdim)
-            d_o = d_o.astype(BF16)
-            prods = pair_products(d_o, v1_ref[i * BLK : (i + 4) * BLK, cols], masks, masks2, per)
-            for t in range(2):
-                at = slice(t * BLK, (t + 1) * BLK)
-                rows = slice((i + t) * BLK, (i + t + 1) * BLK)
-                win = slice((i + t) * BLK, (i + t + 3) * BLK)
-                outer_cols, shared_cols = window_parts(t)
-                dos = stacked(d_o[at], masks)
-                qs = stacked(q1_ref[rows, cols], masks)
-                parts, es = [], []
-                pair_outer = g1_ref[i + t, :, outer_cols]
-                pair_shared = g1_ref[i + t, :, shared_cols]
-                for h in range(per):
-                    e = e1_ref[i + t, g * per + h]
-                    outer, shared = prods[t][h]
-                    gam = gam_ref[1, g * per + h]
-                    outer = e[:, outer_cols].astype(F32) * (outer - delta[h][at])
-                    shared = e[:, shared_cols].astype(F32) * (shared - delta[h][at])
-                    pair_outer = pair_outer + gam * outer
-                    pair_shared = pair_shared + gam * shared
-                    outer, shared = outer.astype(BF16), shared.astype(BF16)
-                    parts.append(jnp.concatenate([outer, shared] if t == 0 else [shared, outer], axis=1))
-                    es.append(e)
-                g1_ref[i + t, :, outer_cols] = pair_outer
-                g1_ref[i + t, :, shared_cols] = pair_shared
-                ks = stacked(k1_ref[win, cols], masks3)
-                dq_ref[rows, cols] = (mm(jnp.concatenate(parts, axis=1), ks) * scale).astype(BF16)
-                dk_ref[win, cols] += mm_tn(jnp.concatenate(parts, axis=0), qs)
-                dv_ref[win, cols] += mm_tn(jnp.concatenate(es, axis=0), dos)
+
+    def body(i, g):
+        cols = group_at(g)
+        rows2 = blocks_at(i, 2)
+        d_o = datt_ref[rows2, cols] * rl1_ref[rows2, cols]
+        delta = delta_of(d_o * o1_ref[rows2, cols].astype(F32), per, hdim)
+        prods, each_do = pair_products(d_o.astype(BF16), v1_ref[blocks_at(i, 4), cols], masks2, per)
+        q = q1_ref[rows2, cols]
+        each_q = [q * m for m in masks2]
+        for t in range(2):
+            at = slice(t * BLK, (t + 1) * BLK)
+            rows, win = blocks_at(i + t, 1), blocks_at(i + t, 3)
+            outer_cols, shared_cols = window_parts(t)
+            dos = jnp.concatenate([x[at] for x in each_do], axis=0)
+            qs = jnp.concatenate([x[at] for x in each_q], axis=0)
+            parts, es = [], []
+            pair_outer = g1_ref[i + t, :, outer_cols]
+            pair_shared = g1_ref[i + t, :, shared_cols]
+            for h in range(per):
+                e = e1_ref[i + t, g * per + h]
+                outer, shared = prods[t][h]
+                gam = gam_ref[1, g * per + h]
+                outer = e[:, outer_cols].astype(F32) * (outer - delta[h][at])
+                shared = e[:, shared_cols].astype(F32) * (shared - delta[h][at])
+                pair_outer = pair_outer + gam * outer
+                pair_shared = pair_shared + gam * shared
+                outer, shared = outer.astype(BF16), shared.astype(BF16)
+                parts.append(jnp.concatenate([outer, shared] if t == 0 else [shared, outer], axis=1))
+                es.append(e)
+            g1_ref[i + t, :, outer_cols] = pair_outer
+            g1_ref[i + t, :, shared_cols] = pair_shared
+            ks = stacked(k1_ref[win, cols], masks3)
+            dq_ref[rows, cols] = (mm(jnp.concatenate(parts, axis=1), ks) * scale).astype(BF16)
+            dk_ref[win, cols] += mm_tn(jnp.concatenate(parts, axis=0), qs)
+            dv_ref[win, cols] += mm_tn(jnp.concatenate(es, axis=0), dos)
+
+    over(nb // 2, groups, body)
     dk = (dk_ref[...] * LN2).astype(BF16)
     dv = dv_ref[...].astype(BF16)
     dnorm = mm_nt(dk, wk[...]) + mm_nt(dv, wv[...])
@@ -364,7 +432,7 @@
     me_ref, gam_ref, _, ext_ref, gains_ref, paya_ref, payb_ref, part_ref, halo_ref, g1_ref,
     o_ref, rl_ref, v_ref, x1_ref, gd_ref, e_ref, wo, wu, wd,
     f_ref,
-    datt_ref,
+    datt_ref, sum_ref, ends_ref,
 ):
     qb = nb + 2
     par = lax.rem(me_ref[0], 2)
@@ -391,56 +459,64 @@
     masks = head_masks(BLK, per, hdim)
     masks2 = head_masks(2 * BLK, per, hdim)
 
-    def cotangents(rows, cols):
-        d_o = datt_ref[rows, cols] * rl_ref[rows, cols]
+    def cotangents(rows, g):
+        cols = group_at(g)
+        lane = lax.broadcasted_iota(jnp.int32, (1, LANES), 1) // hdim
+        gam = jnp.zeros((1, LANES), F32)
+        for h in range(per):
+            gam = jnp.where(lane == h, gam_ref[0, g * per + h], gam)
+        d_o = datt_ref[rows, cols] * rl_ref[rows, cols] * gam
         return d_o.astype(BF16), delta_of(d_o * o_ref[rows, cols].astype(F32), per, hdim)
 
+    last = qb - 1
+    sum_ref[...] = g1_ref[...]
+    ends_ref[...] = jnp.zeros_like(ends_ref)
+
+    def body(i, g):
+        d_o, delta = cotangents(blocks_at(i + 1, 2), g)
+        prods, _ = pair_products(d_o, v_ref[blocks_at(i + 1, 4), group_at(g)], masks2, per)
+        for t in range(2):
+            at = slice(t * BLK, (t + 1) * BLK)
+            for n, c in enumerate(window_parts(t)):
+                total = sum_ref[i + t, :, c]
+                for h in range(per):
+                    total = total + e_ref[i + t + 1, g * per + h, :, c].astype(F32) * (prods[t][h][n] - delta[h][at])
+                sum_ref[i + t, :, c] = total
+
+    def ends(_, g):
+        cols = group_at(g)
+        low_o, low_delta = cotangents(slice(0, BLK), g)
+        high_o, high_delta = cotangents(slice(last * BLK, qb * BLK), g)
+        both = jnp.concatenate([low_o, high_o], axis=1)
+        both = jnp.concatenate([both * jnp.concatenate([m, m], axis=1) for m in masks], axis=0)
+        prods = mm_nt(both, beside(v_ref[2 * BLK : 3 * BLK, cols], v_ref[last * BLK : qb * BLK, cols]))
+        low_sum, high_sum = ends_ref[0], ends_ref[1]
+        for h in range(per):
+            low = prods[h * BLK : (h + 1) * BLK, :BLK] - low_delta[h]
+            high = prods[h * BLK : (h + 1) * BLK, BLK:] - high_delta[h]
+            low_sum = low_sum + e_ref[0, g * per + h, :, 2 * BLK :].astype(F32) * low
+            high_sum = high_sum + e_ref[last, g * per + h, :, :BLK].astype(F32) * high
+        ends_ref[0] = low_sum
+        ends_ref[1] = high_sum
+
+    over(nb // 2, groups, body)
+    over(1, groups, ends)
     forces = [jnp.zeros((8, LANES), F32) for _ in range(nb)]
     forces[0] = forces[0] + from_low[2 * BLK : 2 * BLK + 8, :LANES]
     forces[-1] = forces[-1] + from_high[2 * BLK : 2 * BLK + 8, :LANES]
-    for i in range(0, nb, 2):
-        rows2 = slice((i + 1) * BLK, (i + 3) * BLK)
-        parts = [[g1_ref[i + t, :, c] for c in window_parts(t)] for t in range(2)]
-        for g in range(groups):
-            cols = slice(g * LANES, (g + 1) * LANES)
-            d_o, delta = cotangents(rows2, cols)
-            prods = pair_products(d_o, v_ref[(i + 1) * BLK : (i + 5) * BLK, cols], masks, masks2, per)
-            for t in range(2):
-                at = slice(t * BLK, (t + 1) * BLK)
-                for h in range(per):
-                    gam = gam_ref[0, g * per + h]
-                    for n, c in enumerate(window_parts(t)):
-                        e = e_ref[i + t + 1, g * per + h, :, c].astype(F32)
-                        parts[t][n] = parts[t][n] + gam * (e * (prods[t][h][n] - delta[h][at]))
-        for t in range(2):
-            outer, shared = parts[t]
-            total = jnp.concatenate([outer, shared] if t == 0 else [shared, outer], axis=1)
-            sums = None
-            for s in range(3):
-                cols, rows = fold(total[:, s * BLK : (s + 1) * BLK], ext, ext_t, i + t + 2, i + t + 1 + s)
-                sums = cols if sums is None else [a + b for a, b in zip(sums, cols)]
-                j = i + t - 1 + s
-                if 0 <= j < nb:
-                    forces[j] = forces[j] + three_rows(rows)
-            forces[i + t] = forces[i + t] + columns_to_rows(sums)
-    last = qb - 1
-    ends = [jnp.zeros((BLK, BLK), F32), jnp.zeros((BLK, BLK), F32)]
-    for g in range(groups):
-        cols = slice(g * LANES, (g + 1) * LANES)
-        low_o, low_delta = cotangents(slice(0, BLK), cols)
-        high_o, high_delta = cotangents(slice(last * BLK, qb * BLK), cols)
-        both = jnp.concatenate([low_o, high_o], axis=1)
-        both = jnp.concatenate([both * jnp.concatenate([m, m], axis=1) for m in masks], axis=0)
-        prods = mm_nt(both, beside(v_ref[2 * BLK : 3 * BLK, cols], v_ref[last * BLK : qb * BLK, cols]))
-        for h in range(per):
-            gam = gam_ref[0, g * per + h]
-            low = prods[h * BLK : (h + 1) * BLK, :BLK] - low_delta[h]
-            high = prods[h * BLK : (h + 1) * BLK, BLK:] - high_delta[h]
-            ends[0] = ends[0] + gam * (e_ref[0, g * per + h, :, 2 * BLK :].astype(F32) * low)
-            ends[1] = ends[1] + gam * (e_ref[last, g * per + h, :, :BLK].astype(F32) * high)
-    _, rows = fold(ends[0], ext, ext_t, 1, 2)
+    for i in range(nb):
+        total = sum_ref[i]
+        sums = None
+        for s in range(3):
+            cols, rows = fold(total[:, s * BLK : (s + 1) * BLK], ext, ext_t, i + 2, i + 1 + s)
+            sums = cols if sums is None else [a + b for a, b in zip(sums, cols)]
+            j = i - 1 + s
+            if 0 <= j < nb:
+                forces[j] = forces[j] + three_rows(rows)
+        forces[i] = forces[i] + columns_to_rows(sums)
+    _, rows = fold(ends_ref[0], ext, ext_t, 1, 2)
     forces[0] = forces[0] + three_rows(rows)
-    _, rows = fold(ends[1], ext, ext_t, nb + 2, nb + 1)
+    _, rows = fold(ends_ref[1], ext, ext_t, nb + 2, nb + 1)
     forces[-1] = forces[-1] + three_rows(rows)
     f_ref[...] = jnp.concatenate(forces, axis=1)[:3]
 
@@ -513,7 +589,8 @@
         out_specs=[vmem] * 28,
         scratch_shapes=[
             *shapes[:3], vm((qb, BLK, 3 * BLK), F32), vm((qb * BLK, width), F32), vm((qb * BLK, width), BF16),
-            vm((kb * BLK, width), BF16), pltpu.SemaphoreType.DMA((2, 6)),
+            vm((kb * BLK, width), BF16), vm((LANES // hdim, kb * BLK, width), BF16),
+            vm((LANES // hdim, qb * BLK, width), BF16), pltpu.SemaphoreType.DMA((2, 6)),
         ],
         compiler_params=pltpu.CompilerParams(vmem_limit_bytes=20 * 1024 * 1024),
         cost_estimate=work(qb * 7),
@@ -547,7 +624,7 @@
         out_shape=jax.ShapeDtypeStruct((3, atoms), F32),
         in_specs=[smem, smem] + [vmem] * 17,
         out_specs=vmem,
-        scratch_shapes=[vm((qb * BLK, width), F32)],
+        scratch_shapes=[vm((qb * BLK, width), F32), vm((nb, BLK, 3 * BLK), F32), vm((2, BLK, BLK), F32)],
         compiler_params=pltpu.CompilerParams(vmem_limit_bytes=20 * 1024 * 1024),
         cost_estimate=work(qb * 3),
     )(

time: 54.2 us -> 52.8 us (0.974)
  Pallas kernels: 30.7 us -> 29.3 us
    pallas_call x1, Pallas kernels: 17 us -> 15.8 us  [local(): pl.pallas_call(functools.partial(first_kernel, nb, heads, hdim), out_shap...]
where the time goes in v3:
time: 52.8 us; the launch traced here: 52.6 us
  Pallas kernels  29.3 us (55%)
  starting transfers between devices  15.4 us (29%)
  waiting for transfers between devices  5.96 us (11%)
  local copies, waits for them, and re-layouts  1.2 us (2%)
  between operations  0.7 us (1%)
    pallas_call x1, Pallas kernels, local(): pl.pallas_call(functools.partial(first_kernel, nb, heads, hdim), out_shap...  15.8 us
    ppermute x4, starting transfers between devices, hop(): lax.ppermute(x, 'chain', [(i, i ^ step) for i in range(lax.axis_size('cha...  9.3 us
    pallas_call x1, Pallas kernels, local(): pl.pallas_call(functools.partial(middle_kernel, nb, heads, hdim), out_sha...  7.03 us
    pallas_call x1, Pallas kernels, local(): pl.pallas_call(functools.partial(last_kernel, nb, heads, hdim), out_shape...  5.79 us
    ppermute x4, waiting for transfers between devices, hop(): lax.ppermute(x, 'chain', [(i, i ^ step) for i in range(lax.axis_size('cha...  5.13 us
    ppermute x2, starting transfers between devices, swap_a(): return lax.ppermute(x, 'chain', [(i, i ^ 1) for i in range(n)])  4.52 us
    ppermute x2, starting transfers between devices, swap_b(): lax.ppermute(x, 'chain', [(i, (i + 1 ^ 1) - 1) for i in range(1, n - 1)])  1.55 us
  transfers between devices with their start and end apart: 8, of which 3 were waited for; matrix products, arithmetic and copies ran while one was open for 0% of the time, Pallas kernels for 24%

profile of v3, /device:TPU:0, one launch (start us, length us, event | category | flops | bytes accessed | tf_op | source)
XLA Modules:
  0.0 52.6 jit_solution(13823513416817664124)
XLA Ops:
  0.6 0.7 %shard_map.149.own_ref = f32[8,256]{1,0:T(8,128)S(1)} custom-call(s32[1]{0:T(128)} %bitcast.me_ref, s32[2,3]{1,0:T(2,128)} %list_ref.1, f32[3,256]{1,0:T(4,128)} %pos_ref.1, s32[1,256]{1,0:T(1,128)} %bitcast.5), custom_call_target="tpu_custom_call" | custom-call | tf_op jit(solution)/shard_map/pallas_call | solution.py:560
  1.4 0.7 %collective-permute-start.1 = (f32[8,256]{1,0:T(8,128)S(1)}, f32[8,256]{1,0:T(8,128)S(1)}, u32[]{:S(2)}, u32[]{:S(2)}) collective-permute-start(f32[8,256]{1,0:T(8,128)S(1)} %shard_map.149.own_ref), channel_id=1, source_target_pairs={{1,2},{2,1},{3,4},{4,3},{5,6},{6,5},{7,8},{8,7},{9,10},{10,9},{11,... | collective-permute-start | bytes 24584 | tf_op jit(solution)/shard_map/ppermute | solution.py:531
  2.0 4.4 %collective-permute-start = (f32[8,256]{1,0:T(8,128)S(1)}, f32[8,256]{1,0:T(8,128)S(1)}, u32[]{:S(2)}, u32[]{:S(2)}) collective-permute-start(f32[8,256]{1,0:T(8,128)S(1)} %shard_map.149.own_ref), channel_id=1, source_target_pairs={{0,1},{1,0},{2,3},{3,2},{4,5},{5,4},{6,7},{7,6},{8,9},{9,8},{10,11... | collective-permute-start | bytes 24584 | tf_op jit(solution)/shard_map/ppermute | solution.py:526
  6.4 0.0 collective-permute-done.1.rb_ref
  6.4 0.8 %collective-permute-done.ra_ref = f32[8,256]{1,0:T(8,128)S(1)} collective-permute-done((f32[8,256]{1,0:T(8,128)S(1)}, f32[8,256]{1,0:T(8,128)S(1)}, u32[]{:S(2)}, u32[]{:S(2)}) %collective-permute-start) | collective-permute-done | bytes 8224 | tf_op jit(solution)/shard_map/ppermute | solution.py:526
  7.3 0.0 copy-start
  7.3 0.7 %copy-done = f32[2,16]{1,0:T(2,128)S(1)} copy-done((f32[2,16]{1,0:T(2,128)S(1)}, f32[2,16]{1,0:T(2,128)}, u32[]{:S(2)}) %copy-start) | copy-done | bytes 152
  7.9 0.0 copy-start.1
  7.9 15.8 %shard_map.150 = (f32[8,128]{1,0:T(8,128)S(1)}, f32[8,768]{1,0:T(8,128)S(1)}, f32[2,2,512]{2,1,0:T(2,128)S(1)}, bf16[512,512]{1,0:T(8,128)(2,1)S(1)}, f32[512,51...) custom-call(s32[1]{0:T(128)} %bitcast.me_ref, ...), custom_call_target="tpu_custom_call" | custom-call | flops 15032385536 | tf_op jit(solution)/shard_map/pallas_call | solution.py:577
  23.7 0.5 collective-permute-start.2
  24.2 0.8 %collective-permute-done.2 = f32[8,128]{1,0:T(8,128)S(1)} collective-permute-done((f32[8,128]{1,0:T(8,128)S(1)}, f32[8,128]{1,0:T(8,128)S(1)}, u32[]{:S(2)}, u32[]{:S(2)}) %collective-permute-start.2) | collective-permute-done | bytes 4128 | tf_op jit(solution)/shard_map/ppermute | solution.py:535
  25.0 2.4 %collective-permute-start.3 = (f32[8,128]{1,0:T(8,128)S(1)}, f32[8,128]{1,0:T(8,128)S(1)}, u32[]{:S(2)}, u32[]{:S(2)}) collective-permute-start(f32[8,128]{1,0:T(8,128)S(1)} %add.12._), channel_id=1, source_target_pairs={{0,2},{1,3},{2,0},{3,1},{4,6},{5,7},{6,4},{7,5},{8,10},{9,11},{10,... | collective-permute-start | bytes 12296 | tf_op jit(solution)/shard_map/ppermute | solution.py:535
  27.4 0.0 copy-done.1
  27.4 7.0 %shard_map.151 = (bf16[272,512]{1,0:T(8,128)(2,1)S(1)}, bf16[272,512]{1,0:T(8,128)(2,1)S(1)}, f32[256,512]{1,0:T(8,128)S(1)}, f32[256,512]{1,0:T(8,128)S(1)}, f32[2,128,384]{2,1,0:T(8,128)S(1)}) custom-call(s32[1]{0:T(128)} %bitcast.me_ref, f32[2,16]{1,0:T(2,128)S(1)} %copy-done.1, f32[8,128]{1,0:T(8,128)S(1)} %add.12._, ...), custom_call_target="tpu_custom_call" | custom-call | flops 9663676416 | tf_op jit(solution)/shard_map/pallas_call | solution.py:606
  34.4 0.0 collective-permute-done.3
  34.4 0.1 collective-permute-start.5
  34.6 0.9 %collective-permute-start.6 = (bf16[272,512]{1,0:T(8,128)(2,1)S(1)}, bf16[272,512]{1,0:T(8,128)(2,1)S(1)}, u32[]{:S(2)}, u32[]{:S(2)}) collective-permute-start(bf16[272,512]{1,0:T(8,128)(2,1)S(1)} %get-tuple-element.63), channel_id=1, source_target_pairs={{1,2},{2,1},{3,4},{4,3},{5,6},{6,5},{7,8},{8,7},{9,10},{10,9},{11,... | collective-permute-start | bytes 835592 | tf_op jit(solution)/shard_map/ppermute | solution.py:531
  35.5 2.9 %collective-permute-start.4 = (f32[8,128]{1,0:T(8,128)S(1)}, f32[8,128]{1,0:T(8,128)S(1)}, u32[]{:S(2)}, u32[]{:S(2)}) collective-permute-start(f32[8,128]{1,0:T(8,128)S(1)} %add.13), channel_id=1, source_target_pairs={{0,4},{1,5},{2,6},{3,7},{4,0},{5,1},{6,2},{7,3},{8,12},{9,13},{10,... | collective-permute-start | bytes 12296 | tf_op jit(solution)/shard_map/ppermute | solution.py:535
  38.4 4.3 %collective-permute-done.4 = f32[8,128]{1,0:T(8,128)S(1)} collective-permute-done((f32[8,128]{1,0:T(8,128)S(1)}, f32[8,128]{1,0:T(8,128)S(1)}, u32[]{:S(2)}, u32[]{:S(2)}) %collective-permute-start.4) | collective-permute-done | bytes 4128 | tf_op jit(solution)/shard_map/ppermute | solution.py:535
  42.7 3.6 %collective-permute-start.7 = (f32[8,128]{1,0:T(8,128)S(1)}, f32[8,128]{1,0:T(8,128)S(1)}, u32[]{:S(2)}, u32[]{:S(2)}) collective-permute-start(f32[8,128]{1,0:T(8,128)S(1)} %add.14._), channel_id=1, source_target_pairs={{0,8},{1,9},{2,10},{3,11},{4,12},{5,13},{6,14},{7,15},{8,0},{9,1},... | collective-permute-start | bytes 12296 | tf_op jit(solution)/shard_map/ppermute | solution.py:535
  46.2 0.0 collective-permute-done.5.paya_ref
  46.2 0.0 collective-permute-done.6.payb_ref
  46.2 5.8 %shard_map.152 = f32[3,256]{1,0:T(4,128)} custom-call(s32[1]{0:T(128)} %bitcast.me_ref, f32[2,16]{1,0:T(2,128)S(1)} %copy-done.1, f32[8,128]{1,0:T(8,128)S(1)} %add.14._, f32[8,768]{1,0:T(8,128)S(1)} %get-tuple-element.41.ext_ref, f32[2,2,512]{2,1,0:T(2,128)S(1)} %get-tuple-element.42.gains_ref, bf16[272,512]{1,0:T(8,128)(2,1)S(1)} %collective-permute-done.5.paya_ref, ...), custom_call_target="tpu_custom_call" | custom-call | flops 6442450944 | tf_op jit(solution)/shard_map/pallas_call | solution.py:622
  52.0 0.0 collective-permute-done.7
  52.0 0.5 slice.3
  (4 shorter events, 0.0 us)
Async XLA Ops:
  1.4 5.1 %collective-permute-start.1 = (f32[8,256]{1,0:T(8,128)S(1)}, f32[8,256]{1,0:T(8,128)S(1)}, u32[]{:S(2)}, u32[]{:S(2)}) collective-permute-start(f32[8,256]{1,0:T(8,128)S(1)} %shard_map.149.own_ref), channel_id=1, source_target_pairs={{1,2},{2,1},{3,4},{4,3},{5,6},{6,5},{7,8},{8,7},{9,10},{10,9},{11,... | collective-permute-start | bytes 24584 | tf_op jit(solution)/shard_map/ppermute | solution.py:531
  2.0 5.2 %collective-permute-start = (f32[8,256]{1,0:T(8,128)S(1)}, f32[8,256]{1,0:T(8,128)S(1)}, u32[]{:S(2)}, u32[]{:S(2)}) collective-permute-start(f32[8,256]{1,0:T(8,128)S(1)} %shard_map.149.own_ref), channel_id=1, source_target_pairs={{0,1},{1,0},{2,3},{3,2},{4,5},{5,4},{6,7},{7,6},{8,9},{9,8},{10,11... | collective-permute-start | bytes 24584 | tf_op jit(solution)/shard_map/ppermute | solution.py:526
  7.3 0.7 %copy-start = (f32[2,16]{1,0:T(2,128)S(1)}, f32[2,16]{1,0:T(2,128)}, u32[]{:S(2)}) copy-start(f32[2,16]{1,0:T(2,128)} %gam_ref.5) | copy-start | bytes 388
  7.9 19.4 %copy-start.1 = (f32[2,16]{1,0:T(2,128)S(1)}, f32[2,16]{1,0:T(2,128)}, u32[]{:S(2)}) copy-start(f32[2,16]{1,0:T(2,128)} %gam_ref.5) | copy-start | bytes 388
  23.7 1.3 %collective-permute-start.2 = (f32[8,128]{1,0:T(8,128)S(1)}, f32[8,128]{1,0:T(8,128)S(1)}, u32[]{:S(2)}, u32[]{:S(2)}) collective-permute-start(f32[8,128]{1,0:T(8,128)S(1)} %get-tuple-element.40), channel_id=1, source_target_pairs={{0,1},{1,0},{2,3},{3,2},{4,5},{5,4},{6,7},{7,6},{8,9},{9,8},{10,11... | collective-permute-start | bytes 12296 | tf_op jit(solution)/shard_map/ppermute | solution.py:535
  25.0 9.4 %collective-permute-start.3 = (f32[8,128]{1,0:T(8,128)S(1)}, f32[8,128]{1,0:T(8,128)S(1)}, u32[]{:S(2)}, u32[]{:S(2)}) collective-permute-start(f32[8,128]{1,0:T(8,128)S(1)} %add.12._), channel_id=1, source_target_pairs={{0,2},{1,3},{2,0},{3,1},{4,6},{5,7},{6,4},{7,5},{8,10},{9,11},{10,... | collective-permute-start | bytes 12296 | tf_op jit(solution)/shard_map/ppermute | solution.py:535
  34.4 11.8 %collective-permute-start.5 = (bf16[272,512]{1,0:T(8,128)(2,1)S(1)}, bf16[272,512]{1,0:T(8,128)(2,1)S(1)}, u32[]{:S(2)}, u32[]{:S(2)}) collective-permute-start(bf16[272,512]{1,0:T(8,128)(2,1)S(1)} %get-tuple-element.62), channel_id=1, source_target_pairs={{0,1},{1,0},{2,3},{3,2},{4,5},{5,4},{6,7},{7,6},{8,9},{9,8},{10,11... | collective-permute-start | bytes 835592 | tf_op jit(solution)/shard_map/ppermute | solution.py:526
  34.6 11.7 %collective-permute-start.6 = (bf16[272,512]{1,0:T(8,128)(2,1)S(1)}, bf16[272,512]{1,0:T(8,128)(2,1)S(1)}, u32[]{:S(2)}, u32[]{:S(2)}) collective-permute-start(bf16[272,512]{1,0:T(8,128)(2,1)S(1)} %get-tuple-element.63), channel_id=1, source_target_pairs={{1,2},{2,1},{3,4},{4,3},{5,6},{6,5},{7,8},{8,7},{9,10},{10,9},{11,... | collective-permute-start | bytes 835592 | tf_op jit(solution)/shard_map/ppermute | solution.py:531
  35.5 7.2 %collective-permute-start.4 = (f32[8,128]{1,0:T(8,128)S(1)}, f32[8,128]{1,0:T(8,128)S(1)}, u32[]{:S(2)}, u32[]{:S(2)}) collective-permute-start(f32[8,128]{1,0:T(8,128)S(1)} %add.13), channel_id=1, source_target_pairs={{0,4},{1,5},{2,6},{3,7},{4,0},{5,1},{6,2},{7,3},{8,12},{9,13},{10,... | collective-permute-start | bytes 12296 | tf_op jit(solution)/shard_map/ppermute | solution.py:535
  42.7 9.4 %collective-permute-start.7 = (f32[8,128]{1,0:T(8,128)S(1)}, f32[8,128]{1,0:T(8,128)S(1)}, u32[]{:S(2)}, u32[]{:S(2)}) collective-permute-start(f32[8,128]{1,0:T(8,128)S(1)} %add.14._), channel_id=1, source_target_pairs={{0,8},{1,9},{2,10},{3,11},{4,12},{5,13},{6,14},{7,15},{8,0},{9,1},... | collective-permute-start | bytes 12296 | tf_op jit(solution)/shard_map/ppermute | solution.py:535

commit v4 on v3

--- a/solution.py
+++ b/solution.py
@@ -11,8 +11,6 @@
 BLK = 128
 LANES = 128
 EPS = 1e-06
-LOG2E = math.log2(math.e)
-LN2 = math.log(2.0)
 FAR = 1e30
 F32 = jnp.float32
 BF16 = jnp.bfloat16
@@ -42,11 +40,13 @@
     return r * (t - x * (r * r * jnp.mean(x * t, axis=-1, keepdims=True)))
 
 
-def gelu_both(x):
-    sq = x * x
-    half = 0.5 + 0.5 * jnp.tanh(x * (C0 + (C0 * C1) * sq))
-    act = x * half
-    return act, half + act * (1.0 - half) * (2.0 * C0 + (6.0 * C0 * C1) * sq)
+def gelu_half(x):
+    return 0.5 + 0.5 * jnp.tanh(x * (C0 + (C0 * C1) * (x * x)))
+
+
+def gelu_slope(x):
+    half = gelu_half(x)
+    return half + (x * half) * (1.0 - half) * (2.0 * C0 + (6.0 * C0 * C1) * (x * x))
 
 
 def head_masks(rows, heads_per_group, hdim):
@@ -69,7 +69,8 @@
             for c in range(3):
                 diff = q[:, c : c + 1] - ext[c : c + 1, k0 : k0 + BLK]
                 tot = diff * diff if tot is None else tot + diff * diff
-            d2_ref[i, :, s * BLK : (s + 1) * BLK] = jnp.where(q[:, 4 + s : 5 + s] > 0.5, tot, FAR)
+            listed = ext[4 + s : 5 + s, (first + i) * BLK : (first + i + 1) * BLK] > 0.5
+            d2_ref[i, :, s * BLK : (s + 1) * BLK] = jnp.where(listed, tot, FAR)
 
 
 def stacked(x, masks):
@@ -130,12 +131,13 @@
 
 
 def small_scores(q, k, hdim):
-    return jnp.max(head_norms(q, hdim) * head_norms(k, hdim)) < 3600.0
+    return jnp.max(head_norms(q, hdim) * head_norms(k, hdim)) < 1600.0 * hdim
 
 
 def attend(exact, q_ref, k_ref, vm_ref, o_ref, rl_ref, e_ref, d2_ref, d2_first, gam_ref, layer, heads, hdim, count):
     per = LANES // hdim
     groups = heads // per
+    scale = hdim ** (-0.5)
     masks2 = head_masks(2 * BLK, per, hdim)
     ones2 = jnp.concatenate(masks2, axis=0)
     ones1 = jnp.concatenate([m[:BLK] for m in masks2], axis=0)
@@ -152,7 +154,7 @@
             outer_cols, shared_cols = window_parts(t)
             outers, shareds = [], []
             for h in range(per):
-                gam = gam_ref[layer, g * per + h] * LOG2E
+                gam = gam_ref[layer, g * per + h] / scale
                 outer, shared = scores[t][h]
                 outer = outer - gam * d2_ref[d2_first + i + t, :, outer_cols]
                 shared = shared - gam * d2_ref[d2_first + i + t, :, shared_cols]
@@ -160,8 +162,8 @@
                     peak = jnp.maximum(jnp.maximum(outer, shared[:, :BLK]), shared[:, BLK:])
                     peak = jnp.max(peak, axis=1, keepdims=True)
                     outer, shared = outer - peak, shared - peak
-                outer = jnp.exp2(outer).astype(BF16)
-                shared = jnp.exp2(shared).astype(BF16)
+                outer = jnp.exp(outer * scale).astype(BF16)
+                shared = jnp.exp(shared * scale).astype(BF16)
                 e_ref[i + t, g * per + h, :, outer_cols] = outer
                 e_ref[i + t, g * per + h, :, shared_cols] = shared
                 outers.append(outer)
@@ -229,9 +231,9 @@
 
 def first_kernel(
     nb, heads, hdim,
-    me_ref, gam_ref, own_ref, ra_ref, rb_ref, embed_ref, gains_ref, outg_ref, ro_ref,
+    me_ref, gam_ref, gamv_ref, own_ref, ra_ref, rb_ref, embed_ref, gains_ref, outg_ref, ro_ref,
     wq_h, wk_h, wv_h, wo_h, wu_h, wd_h,
-    e_out, ext_ref, gk_ref, o_ref, rl_ref, v_ref, x1_ref, gd_ref, e_ref, wo0, wu0, wd0,
+    e_out, ext_ref, gk_ref, gamk_ref, par_out, o_ref, rl_ref, v_ref, x1_ref, gd_ref, e_ref, wo0, wu0, wd0,
     st_ref, q1_ref, k1_ref, v1_ref, o1_ref, rl1_ref, e1_ref, x11_ref, gd1_ref, top_ref, wq1, wk1, wv1, wo1, wu1, wd1,
     wq0, wk0, wv0, d2_ref, x0_ref, q_ref, k_ref, vm_ref, vm1_ref, sem,
 ):
@@ -253,6 +255,10 @@
     ext = jnp.concatenate([before, own, after], axis=1)
     ext_ref[...] = ext
     gk_ref[...] = gains_ref[...]
+    par_out[...] = jnp.full(par_out.shape, par.astype(F32))
+    rates = gamv_ref[...].T
+    for layer in range(2):
+        gamk_ref[layer] = jnp.broadcast_to(rates[:, layer : layer + 1], (heads, LANES))
     ext_t = ext.T
     distances(ext, ext_t, 1, d2_ref, qb)
 
@@ -266,7 +272,7 @@
     x0_ref[...] = mm(onehot_q, embed_ref[...])
     for c in copies[0][:3]:
         c.wait()
-    q_table = (mm(normed, wq0[...]) * (scale * LOG2E)).astype(BF16)
+    q_table = mm(normed, wq0[...]).astype(BF16)
     q_ref[...] = mm(onehot_q, q_table).astype(BF16)
     k_table = mm(normed, wk0[...]).astype(BF16)
     k_ref[...] = mm(onehot, k_table).astype(BF16)
@@ -285,29 +291,29 @@
 
         def feed(layer, x1, w_up, w_down, keep):
             inner = (x1 * inv_rms(x1) * gains_ref[layer, 1:2]).astype(BF16)
-            act, slope = gelu_both(mm(inner, w_up[...]))
-            keep(slope.astype(BF16))
-            return x1 + mm(act.astype(BF16), w_down[...])
+            pre = mm(inner, w_up[...])
+            keep(pre)
+            return x1 + mm((pre * gelu_half(pre)).astype(BF16), w_down[...])
 
         step = 4 * BLK
         for r in range(0, qb * BLK, step):
             rows = slice(r, r + step)
             x1 = x0_ref[rows] + mm(o_ref[rows], wo0[...])
             x1_ref[rows] = x1
-            st_ref[rows] = feed(0, x1, wu0, wd0, lambda slope: gd_ref.__setitem__(rows, slope))
+            st_ref[rows] = feed(0, x1, wu0, wd0, lambda pre: gd_ref.__setitem__(rows, pre))
 
         arrived(copies[1])
         gain = gains_ref[1, 0:1]
         st = st_ref[...]
         normed = (st * inv_rms(st) * gain).astype(BF16)
-        q1_ref[...] = (mm(normed[mid], wq1[...]) * (scale * LOG2E)).astype(BF16)
+        q1_ref[...] = mm(normed[mid], wq1[...]).astype(BF16)
         k1_ref[...] = mm(normed, wk1[...]).astype(BF16)
         v1_ref[...] = mm(normed, wv1[...]).astype(BF16)
         split_heads(v1_ref, vm1_ref, hdim)
         attend(exact, q1_ref, k1_ref, vm1_ref, o1_ref, rl1_ref, e1_ref, d2_ref, 1, gam_ref, 1, heads, hdim, nb)
         x1 = st_ref[mid] + mm(o1_ref[...], wo1[...])
         x11_ref[...] = x1
-        x2 = feed(1, x1, wu1, wd1, lambda slope: gd1_ref.__setitem__(..., slope))
+        x2 = feed(1, x1, wu1, wd1, lambda pre: gd1_ref.__setitem__(..., pre))
 
         w = outg_ref[...] * ro_ref[...]
         r = inv_rms(x2)
@@ -326,7 +332,7 @@
 
 def middle_kernel(
     nb, heads, hdim,
-    me_ref, gam_ref, _, ext_ref, gains_ref, st_ref, q1_ref, k1_ref, v1_ref, o1_ref, rl1_ref, e1_ref, x1_ref, gd_ref, top_ref,
+    par_ref, gam_ref, _, ext_ref, gains_ref, st_ref, q1_ref, k1_ref, v1_ref, o1_ref, rl1_ref, e1_ref, x1_ref, gd_ref, top_ref,
     wq, wk, wv, wo, wu, wd,
     paya_ref, payb_ref, part_ref, halo_ref, g1_ref,
     dq_ref, dk_ref, dv_ref, datt_ref,
@@ -335,12 +341,12 @@
     mid = slice(BLK, (nb + 1) * BLK)
     scale = hdim ** (-0.5)
     width = st_ref.shape[1]
-    par = lax.rem(me_ref[0], 2)
+    even = par_ref[0:1, 0:1] < 0.5
     ext = ext_ref[...]
     ext_t = ext.T
     grad = top_ref[...]
     du = mm_nt(grad.astype(BF16), wd[...]).astype(BF16).astype(F32)
-    dinner = mm_nt((du * gd_ref[...].astype(F32)).astype(BF16), wu[...]).astype(BF16).astype(F32)
+    dinner = mm_nt((du * gelu_slope(gd_ref[...])).astype(BF16), wu[...]).astype(BF16).astype(F32)
     grad = grad + rms_back(x1_ref[...], gains_ref[1, 1:2], dinner)
     datt_ref[...] = mm_nt(grad.astype(BF16), wo[...]).astype(BF16).astype(F32)
 
@@ -360,36 +366,42 @@
         prods, each_do = pair_products(d_o.astype(BF16), v1_ref[blocks_at(i, 4), cols], masks2, per)
         q = q1_ref[rows2, cols]
         each_q = [q * m for m in masks2]
+        es, dss = [], []
         for t in range(2):
             at = slice(t * BLK, (t + 1) * BLK)
             rows, win = blocks_at(i + t, 1), blocks_at(i + t, 3)
             outer_cols, shared_cols = window_parts(t)
-            dos = jnp.concatenate([x[at] for x in each_do], axis=0)
-            qs = jnp.concatenate([x[at] for x in each_q], axis=0)
-            parts, es = [], []
+            parts = []
             pair_outer = g1_ref[i + t, :, outer_cols]
             pair_shared = g1_ref[i + t, :, shared_cols]
             for h in range(per):
-                e = e1_ref[i + t, g * per + h]
+                e_outer, e_shared = e1_ref[i + t, g * per + h, :, outer_cols], e1_ref[i + t, g * per + h, :, shared_cols]
                 outer, shared = prods[t][h]
-                gam = gam_ref[1, g * per + h]
-                outer = e[:, outer_cols].astype(F32) * (outer - delta[h][at])
-                shared = e[:, shared_cols].astype(F32) * (shared - delta[h][at])
+                gam = gam_ref[1, g * per + h : g * per + h + 1]
+                outer = e_outer.astype(F32) * (outer - delta[h][at])
+                shared = e_shared.astype(F32) * (shared - delta[h][at])
                 pair_outer = pair_outer + gam * outer
-                pair_shared = pair_shared + gam * shared
+                pair_shared = pair_shared + jnp.concatenate([gam, gam], axis=1) * shared
                 outer, shared = outer.astype(BF16), shared.astype(BF16)
                 parts.append(jnp.concatenate([outer, shared] if t == 0 else [shared, outer], axis=1))
-                es.append(e)
+                es.append((e_outer, e_shared))
+                dss.append((outer, shared))
             g1_ref[i + t, :, outer_cols] = pair_outer
             g1_ref[i + t, :, shared_cols] = pair_shared
             ks = stacked(k1_ref[win, cols], masks3)
             dq_ref[rows, cols] = (mm(jnp.concatenate(parts, axis=1), ks) * scale).astype(BF16)
-            dk_ref[win, cols] += mm_tn(jnp.concatenate(parts, axis=0), qs)
-            dv_ref[win, cols] += mm_tn(jnp.concatenate(es, axis=0), dos)
+        for ref, each, weights in ((dk_ref, each_q, dss), (dv_ref, each_do, es)):
+            left = jnp.concatenate([x[t * BLK : (t + 1) * BLK] for t in range(2) for x in each], axis=0).T
+            ref[cols, blocks_at(i + 1, 2)] += mm(left, jnp.concatenate([w[1] for w in weights], axis=0))
+            for t in range(2):
+                some = slice(t * per, (t + 1) * per)
+                ref[cols, blocks_at(i + 3 * t, 1)] += mm(
+                    left[:, t * per * BLK : (t + 1) * per * BLK], jnp.concatenate([w[0] for w in weights[some]], axis=0)
+                )
 
     over(nb // 2, groups, body)
-    dk = (dk_ref[...] * LN2).astype(BF16)
-    dv = dv_ref[...].astype(BF16)
+    dk = (dk_ref[...] * scale).astype(BF16).T
+    dv = dv_ref[...].astype(BF16).T
     dnorm = mm_nt(dk, wk[...]) + mm_nt(dv, wv[...])
     dq = mm_nt(dq_ref[...], wq[...])
     zeros = jnp.zeros((BLK, width), F32)
@@ -404,43 +416,37 @@
     _, rows_high = fold(g1_ref[nb - 1, :, 2 * BLK :], ext, ext_t, nb + 1, nb + 2)
     pad = jnp.zeros((8, width - LANES), F32)
 
-    def payload(ref, halo, edge, rows):
-        ref[:BLK] = halo.astype(BF16)
-        ref[BLK : 2 * BLK] = edge.astype(BF16)
+    def payload(halo, edge, rows):
         tail = jnp.concatenate([three_rows(rows), pad], axis=1)
-        ref[2 * BLK :] = jnp.concatenate([tail, jnp.zeros_like(tail)], axis=0).astype(BF16)
-
-    def low(ref):
-        payload(ref, back[:BLK], part[:BLK], rows_low)
-
-    def high(ref):
-        payload(ref, back[(qb - 1) * BLK :], part[(nb - 1) * BLK :], rows_high)
-
-    @pl.when(par == 0)
-    def _():
-        high(paya_ref)
-        low(payb_ref)
-
-    @pl.when(par != 0)
-    def _():
-        low(paya_ref)
-        high(payb_ref)
+        return halo, edge, jnp.concatenate([tail, jnp.zeros_like(tail)], axis=0)
+
+    low = payload(back[:BLK], part[:BLK], rows_low)
+    high = payload(back[(qb - 1) * BLK :], part[(nb - 1) * BLK :], rows_high)
+    at = 0
+    for x, y in zip(high, low):
+        rows = slice(at, at + x.shape[0])
+        paya_ref[rows] = jnp.where(even, x, y).astype(BF16)
+        payb_ref[rows] = jnp.where(even, y, x).astype(BF16)
+        at += x.shape[0]
+
+
+def slope_kernel(_, pre_ref, out_ref):
+    out_ref[...] = gelu_slope(pre_ref[...]).astype(BF16)
 
 
 def last_kernel(
     nb, heads, hdim,
-    me_ref, gam_ref, _, ext_ref, gains_ref, paya_ref, payb_ref, part_ref, halo_ref, g1_ref,
+    par_ref, gam_ref, _, ext_ref, gains_ref, paya_ref, payb_ref, part_ref, halo_ref, g1_ref,
     o_ref, rl_ref, v_ref, x1_ref, gd_ref, e_ref, wo, wu, wd,
     f_ref,
     datt_ref, sum_ref, ends_ref,
 ):
     qb = nb + 2
-    par = lax.rem(me_ref[0], 2)
     ext = ext_ref[...]
     ext_t = ext.T
-    from_low, _, from_high = arrange(par, None, paya_ref[...], payb_ref[...])
-    from_low = from_low.astype(F32)
-    from_high = from_high.astype(F32)
+    even = par_ref[0:1, 0:1] < 0.5
+    from_a, from_b = paya_ref[...].astype(F32), payb_ref[...].astype(F32)
+    from_low, from_high = jnp.where(even, from_b, from_a), jnp.where(even, from_a, from_b)
     part = part_ref[...]
     pieces = [halo_ref[:BLK] + from_low[BLK : 2 * BLK]]
     own_parts = [part[i * BLK : (i + 1) * BLK] for i in range(nb)]
@@ -464,7 +470,7 @@
         lane = lax.broadcasted_iota(jnp.int32, (1, LANES), 1) // hdim
         gam = jnp.zeros((1, LANES), F32)
         for h in range(per):
-            gam = jnp.where(lane == h, gam_ref[0, g * per + h], gam)
+            gam = jnp.where(lane == h, gam_ref[0, g * per + h : g * per + h + 1], gam)
         d_o = datt_ref[rows, cols] * rl_ref[rows, cols] * gam
         return d_o.astype(BF16), delta_of(d_o * o_ref[rows, cols].astype(F32), per, hdim)
 
@@ -572,21 +578,23 @@
         send_b = jnp.where(me % 2 == 0, first, last)
     near_a, near_b = swap_a(send_a), swap_b(send_b)
     pin = functools.partial(pltpu.with_memory_space_constraint, memory_space=pltpu.HBM)
+    gammas = pin(gammas)
     weights = (w_query, w_key, w_value, w_out, w_up, w_down)
     shapes = [vm((width, width), BF16)] * 4 + [vm((width, ff), BF16), vm((ff, width), BF16)]
     first = pl.pallas_call(
         functools.partial(first_kernel, nb, heads, hdim),
         out_shape=[
             vm((8, LANES), F32), vm((8, kb * BLK), F32), vm(norm_gains.shape, F32),
+            vm((layers, heads, LANES), F32), vm((8, LANES), F32),
             vm((qb * BLK, width), BF16), vm((qb * BLK, width), F32), vm((kb * BLK, width), BF16),
-            vm((qb * BLK, width), F32), vm((qb * BLK, ff), BF16), vm((qb, heads, BLK, 3 * BLK), BF16), *shapes[3:],
+            vm((qb * BLK, width), F32), vm((qb * BLK, ff), F32), vm((qb, heads, BLK, 3 * BLK), BF16), *shapes[3:],
             vm((qb * BLK, width), F32), vm((nb * BLK, width), BF16), vm((qb * BLK, width), BF16),
             vm((qb * BLK, width), BF16), vm((nb * BLK, width), BF16), vm((nb * BLK, width), F32),
-            vm((nb, heads, BLK, 3 * BLK), BF16), vm((nb * BLK, width), F32), vm((nb * BLK, ff), BF16),
+            vm((nb, heads, BLK, 3 * BLK), BF16), vm((nb * BLK, width), F32), vm((nb * BLK, ff), F32),
             vm((nb * BLK, width), F32), *shapes,
         ],
-        in_specs=[smem, smem] + [vmem] * 7 + [pl.BlockSpec(memory_space=pltpu.HBM)] * 6,
-        out_specs=[vmem] * 28,
+        in_specs=[smem, smem] + [vmem] * 8 + [pl.BlockSpec(memory_space=pltpu.HBM)] * 6,
+        out_specs=[vmem] * 30,
         scratch_shapes=[
             *shapes[:3], vm((qb, BLK, 3 * BLK), F32), vm((qb * BLK, width), F32), vm((qb * BLK, width), BF16),
             vm((kb * BLK, width), BF16), vm((LANES // hdim, kb * BLK, width), BF16),
@@ -595,40 +603,51 @@
         compiler_params=pltpu.CompilerParams(vmem_limit_bytes=20 * 1024 * 1024),
         cost_estimate=work(qb * 7),
     )(
-        place, gammas, keep(own), keep(near_a), keep(near_b), pin(embed), pin(norm_gains),
+        place, gammas, gammas, keep(own), keep(near_a), keep(near_b), pin(embed), pin(norm_gains),
         pin(out_gain.reshape(1, width)), pin(readout.reshape(1, width)), *(pin(w) for w in weights),
     )
     energy, ext, gains = first[0], keep(first[1]), keep(first[2])
-    saved0 = [keep(x) for x in first[3:12]]
-    saved1 = [keep(x) for x in first[12:]]
+    rates, side = keep(first[3]), keep(first[4])
+    saved0 = [keep(x) for x in first[5:14]]
+    saved1 = [keep(x) for x in first[14:]]
     energy = energy + hop(energy, 1)
     pay = vm((2 * BLK + 16, width), BF16)
     pay_a, pay_b, part, halo, pairs = pl.pallas_call(
         functools.partial(middle_kernel, nb, heads, hdim),
         out_shape=[pay, pay, vm((nb * BLK, width), F32), vm((2 * BLK, width), F32), vm((nb, BLK, 3 * BLK), F32)],
-        in_specs=[smem, smem] + [vmem] * 19,
+        in_specs=[vmem] * 21,
         out_specs=[vmem] * 5,
         scratch_shapes=[
-            vm((nb * BLK, width), BF16), vm((qb * BLK, width), F32), vm((qb * BLK, width), F32), vm((nb * BLK, width), F32),
+            vm((nb * BLK, width), BF16), vm((width, qb * BLK), F32), vm((width, qb * BLK), F32), vm((nb * BLK, width), F32),
         ],
         compiler_params=pltpu.CompilerParams(vmem_limit_bytes=20 * 1024 * 1024),
         cost_estimate=work(nb * 9),
-    )(place, gammas, keep(energy), ext, gains, *saved1)
+    )(side, rates, keep(energy), ext, gains, *saved1)
     energy = energy + hop(energy, 2)
     energy, pay_a, pay_b = lax.optimization_barrier((energy, pay_a, pay_b))
+    saved0[4] = keep(
+        pl.pallas_call(
+            slope_kernel,
+            out_shape=vm((qb * BLK, ff), BF16),
+            in_specs=[vmem, vmem],
+            out_specs=vmem,
+            compiler_params=pltpu.CompilerParams(vmem_limit_bytes=8 * 1024 * 1024),
+            cost_estimate=work(qb),
+        )(keep(energy), saved0[4])
+    )
     arriving = hop(energy, 4)
     got_a, got_b = swap_a(pay_a), swap_b(pay_b)
     energy = energy + arriving
     forces = pl.pallas_call(
         functools.partial(last_kernel, nb, heads, hdim),
         out_shape=jax.ShapeDtypeStruct((3, atoms), F32),
-        in_specs=[smem, smem] + [vmem] * 17,
+        in_specs=[vmem] * 19,
         out_specs=vmem,
         scratch_shapes=[vm((qb * BLK, width), F32), vm((nb, BLK, 3 * BLK), F32), vm((2, BLK, BLK), F32)],
         compiler_params=pltpu.CompilerParams(vmem_limit_bytes=20 * 1024 * 1024),
         cost_estimate=work(qb * 3),
     )(
-        place, gammas, keep(energy), ext, gains, keep(got_a), keep(got_b), keep(part), keep(halo), keep(pairs), *saved0
+        side, rates, keep(energy), ext, gains, keep(got_a), keep(got_b), keep(part), keep(halo), keep(pairs), *saved0
     )
     if count > 8:
         arriving = hop(energy, 8)

time: 52.8 us -> 50.4 us (0.955)
  waiting for transfers between devices: 5.96 us -> 4.98 us
  local copies, waits for them, and re-layouts: 1.2 us -> 0.52 us
  Pallas kernels: 29.3 us -> 28.7 us
    ppermute x4, waiting for transfers between devices: 5.13 us -> 4.14 us  [hop(): lax.ppermute(x, 'chain', [(i, i ^ step) for i in range(lax.axis_size('cha...]
    pallas_call x0 -> x1, Pallas kernels: none -> 0.99 us  [local(): pl.pallas_call(slope_kernel, out_shape=vm((qb * BLK, ff), BF16), in_specs...]
    unnamed x4 -> x0, local copies, waits for them, and re-layouts: 0.68 us -> none
    pallas_call x1, Pallas kernels: 7.03 us -> 6.36 us  [local(): pl.pallas_call(functools.partial(middle_kernel, nb, heads, hdim), out_sha...]
  transfers between devices with their start and end apart: 8 -> 8, of which waited for: 3 -> 3; matrix products, arithmetic and copies ran while one was open for 0% -> 0% of each run, Pallas kernels for 24% -> 25%
where the time goes in v4:
time: 50.4 us; the launch traced here: 50.2 us
  Pallas kernels  28.7 us (57%)
  starting transfers between devices  15.4 us (31%)
  waiting for transfers between devices  4.98 us (10%)
  between operations  0.69 us (1%)
  local copies, waits for them, and re-layouts  0.52 us (1%)
    pallas_call x1, Pallas kernels, local(): pl.pallas_call(functools.partial(first_kernel, nb, heads, hdim), out_shap...  15.3 us
    ppermute x4, starting transfers between devices, hop(): lax.ppermute(x, 'chain', [(i, i ^ step) for i in range(lax.axis_size('cha...  9.32 us
    pallas_call x1, Pallas kernels, local(): pl.pallas_call(functools.partial(middle_kernel, nb, heads, hdim), out_sha...  6.36 us
    pallas_call x1, Pallas kernels, local(): pl.pallas_call(functools.partial(last_kernel, nb, heads, hdim), out_shape...  5.3 us
    ppermute x2, starting transfers between devices, swap_a(): return lax.ppermute(x, 'chain', [(i, i ^ 1) for i in range(n)])  4.52 us
    ppermute x4, waiting for transfers between devices, hop(): lax.ppermute(x, 'chain', [(i, i ^ step) for i in range(lax.axis_size('cha...  4.14 us
    ppermute x2, starting transfers between devices, swap_b(): lax.ppermute(x, 'chain', [(i, (i + 1 ^ 1) - 1) for i in range(1, n - 1)])  1.55 us
  transfers between devices with their start and end apart: 8, of which 3 were waited for; matrix products, arithmetic and copies ran while one was open for 0% of the time, Pallas kernels for 25%

profile of v4, /device:TPU:0, one launch (start us, length us, event | category | flops | bytes accessed | tf_op | source)
XLA Modules:
  0.0 50.2 jit_solution(8707803519428713393)
XLA Ops:
  0.6 0.7 %shard_map.149.own_ref = f32[8,256]{1,0:T(8,128)S(1)} custom-call(s32[1]{0:T(128)} %bitcast.me_ref, s32[2,3]{1,0:T(2,128)} %list_ref.1, f32[3,256]{1,0:T(4,128)} %pos_ref.1, s32[1,256]{1,0:T(1,128)} %bitcast.5), custom_call_target="tpu_custom_call" | custom-call | tf_op jit(solution)/shard_map/pallas_call | solution.py:566
  1.4 0.7 %collective-permute-start.1 = (f32[8,256]{1,0:T(8,128)S(1)}, f32[8,256]{1,0:T(8,128)S(1)}, u32[]{:S(2)}, u32[]{:S(2)}) collective-permute-start(f32[8,256]{1,0:T(8,128)S(1)} %shard_map.149.own_ref), channel_id=1, source_target_pairs={{1,2},{2,1},{3,4},{4,3},{5,6},{6,5},{7,8},{8,7},{9,10},{10,9},{11,... | collective-permute-start | bytes 24584 | tf_op jit(solution)/shard_map/ppermute | solution.py:537
  2.0 4.4 %collective-permute-start = (f32[8,256]{1,0:T(8,128)S(1)}, f32[8,256]{1,0:T(8,128)S(1)}, u32[]{:S(2)}, u32[]{:S(2)}) collective-permute-start(f32[8,256]{1,0:T(8,128)S(1)} %shard_map.149.own_ref), channel_id=1, source_target_pairs={{0,1},{1,0},{2,3},{3,2},{4,5},{5,4},{6,7},{7,6},{8,9},{9,8},{10,11... | collective-permute-start | bytes 24584 | tf_op jit(solution)/shard_map/ppermute | solution.py:532
  6.4 0.0 collective-permute-done.1.rb_ref
  6.4 0.8 %collective-permute-done.ra_ref = f32[8,256]{1,0:T(8,128)S(1)} collective-permute-done((f32[8,256]{1,0:T(8,128)S(1)}, f32[8,256]{1,0:T(8,128)S(1)}, u32[]{:S(2)}, u32[]{:S(2)}) %collective-permute-start) | collective-permute-done | bytes 8224 | tf_op jit(solution)/shard_map/ppermute | solution.py:532
  7.3 15.3 %shard_map.150 = (f32[8,128]{1,0:T(8,128)S(1)}, f32[8,768]{1,0:T(8,128)S(1)}, f32[2,2,512]{2,1,0:T(2,128)S(1)}, f32[2,16,128]{2,1,0:T(8,128)S(1)}, f32[8,128]{1,...) custom-call(s32[1]{0:T(128)} %bitcast.me_ref, ...), custom_call_target="tpu_custom_call" | custom-call | flops 15032385536 | tf_op jit(solution)/shard_map/pallas_call | solution.py:584
  22.6 0.5 collective-permute-start.2
  23.1 0.8 %collective-permute-done.2 = f32[8,128]{1,0:T(8,128)S(1)} collective-permute-done((f32[8,128]{1,0:T(8,128)S(1)}, f32[8,128]{1,0:T(8,128)S(1)}, u32[]{:S(2)}, u32[]{:S(2)}) %collective-permute-start.2) | collective-permute-done | bytes 4128 | tf_op jit(solution)/shard_map/ppermute | solution.py:541
  23.9 2.4 %collective-permute-start.3 = (f32[8,128]{1,0:T(8,128)S(1)}, f32[8,128]{1,0:T(8,128)S(1)}, u32[]{:S(2)}, u32[]{:S(2)}) collective-permute-start(f32[8,128]{1,0:T(8,128)S(1)} %add.12._), channel_id=1, source_target_pairs={{0,2},{1,3},{2,0},{3,1},{4,6},{5,7},{6,4},{7,5},{8,10},{9,11},{10,... | collective-permute-start | bytes 12296 | tf_op jit(solution)/shard_map/ppermute | solution.py:541
  26.2 6.4 %shard_map.151 = (bf16[272,512]{1,0:T(8,128)(2,1)S(1)}, bf16[272,512]{1,0:T(8,128)(2,1)S(1)}, f32[256,512]{1,0:T(8,128)S(1)}, f32[256,512]{1,0:T(8,128)S(1)}, f32[2,128,384]{2,1,0:T(8,128)S(1)}) custom-call(f32[8,128]{1,0:T(8,128)S(1)} %get-tuple-element.43.par_ref, f32[2,16,128]{2,1,0:T(8,128)S(1)} %get-tuple-element.44.gam_ref, f32[8,128]{1,0:T(8,128)S(1)} %add.12._, ...), custom_call_target="tpu_custom_call" | custom-call | flops 9663676416 | tf_op jit(solution)/shard_map/pallas_call | solution.py:615
  32.6 0.0 collective-permute-done.3
  32.6 0.1 collective-permute-start.5
  32.7 0.9 %collective-permute-start.6 = (bf16[272,512]{1,0:T(8,128)(2,1)S(1)}, bf16[272,512]{1,0:T(8,128)(2,1)S(1)}, u32[]{:S(2)}, u32[]{:S(2)}) collective-permute-start(bf16[272,512]{1,0:T(8,128)(2,1)S(1)} %get-tuple-element.67), channel_id=1, source_target_pairs={{1,2},{2,1},{3,4},{4,3},{5,6},{6,5},{7,8},{8,7},{9,10},{10,9},{11,... | collective-permute-start | bytes 835592 | tf_op jit(solution)/shard_map/ppermute | solution.py:537
  33.6 2.9 %collective-permute-start.4 = (f32[8,128]{1,0:T(8,128)S(1)}, f32[8,128]{1,0:T(8,128)S(1)}, u32[]{:S(2)}, u32[]{:S(2)}) collective-permute-start(f32[8,128]{1,0:T(8,128)S(1)} %add.13._), channel_id=1, source_target_pairs={{0,4},{1,5},{2,6},{3,7},{4,0},{5,1},{6,2},{7,3},{8,12},{9,13},{10,... | collective-permute-start | bytes 12296 | tf_op jit(solution)/shard_map/ppermute | solution.py:541
  36.5 1.0 %shard_map.152.gd_ref = bf16[512,1024]{1,0:T(8,128)(2,1)S(1)} custom-call(f32[8,128]{1,0:T(8,128)S(1)} %add.13._, f32[512,1024]{1,0:T(8,128)S(1)} %get-tuple-element.75.pre_ref), custom_call_target="tpu_custom_call" | custom-call | flops 2147483648 | tf_op jit(solution)/shard_map/pallas_call | solution.py:629
  37.5 3.3 %collective-permute-done.4 = f32[8,128]{1,0:T(8,128)S(1)} collective-permute-done((f32[8,128]{1,0:T(8,128)S(1)}, f32[8,128]{1,0:T(8,128)S(1)}, u32[]{:S(2)}, u32[]{:S(2)}) %collective-permute-start.4) | collective-permute-done | bytes 4128 | tf_op jit(solution)/shard_map/ppermute | solution.py:541
  40.8 3.6 %collective-permute-start.7 = (f32[8,128]{1,0:T(8,128)S(1)}, f32[8,128]{1,0:T(8,128)S(1)}, u32[]{:S(2)}, u32[]{:S(2)}) collective-permute-start(f32[8,128]{1,0:T(8,128)S(1)} %add.14._), channel_id=1, source_target_pairs={{0,8},{1,9},{2,10},{3,11},{4,12},{5,13},{6,14},{7,15},{8,0},{9,1},... | collective-permute-start | bytes 12296 | tf_op jit(solution)/shard_map/ppermute | solution.py:541
  44.4 0.0 collective-permute-done.5.paya_ref
  44.4 0.0 collective-permute-done.6.payb_ref
  44.4 5.3 %shard_map.153 = f32[3,256]{1,0:T(4,128)} custom-call(f32[8,128]{1,0:T(8,128)S(1)} %get-tuple-element.43.par_ref, f32[2,16,128]{2,1,0:T(8,128)S(1)} %get-tuple-element.44.gam_ref, f32[8,128]{1,0:T(8,128)S(1)} %add.14._, f32[8,768]{1,0:T(8,128)S(1)} %get-tuple-element.45.ext_ref, f32[2,2,512]{2,1,0:T(2,128)S(1)} %get-tuple-element.46.gains_ref, ...), custom_call_target="tpu_custom_call" | custom-call | flops 6442450944 | tf_op jit(solution)/shard_map/pallas_call | solution.py:641
  49.7 0.0 collective-permute-done.7
  49.7 0.5 %slice.3 = f32[1,1]{1,0:T(1,128)} slice(f32[8,128]{1,0:T(8,128)S(1)} %add.15), slice={[0:1], [0:1]} | slice | bytes 8 | tf_op jit(solution)/shard_map/slice | solution.py:660
  (4 shorter events, 0.0 us)
Async XLA Ops:
  1.4 5.1 %collective-permute-start.1 = (f32[8,256]{1,0:T(8,128)S(1)}, f32[8,256]{1,0:T(8,128)S(1)}, u32[]{:S(2)}, u32[]{:S(2)}) collective-permute-start(f32[8,256]{1,0:T(8,128)S(1)} %shard_map.149.own_ref), channel_id=1, source_target_pairs={{1,2},{2,1},{3,4},{4,3},{5,6},{6,5},{7,8},{8,7},{9,10},{10,9},{11,... | collective-permute-start | bytes 24584 | tf_op jit(solution)/shard_map/ppermute | solution.py:537
  2.0 5.2 %collective-permute-start = (f32[8,256]{1,0:T(8,128)S(1)}, f32[8,256]{1,0:T(8,128)S(1)}, u32[]{:S(2)}, u32[]{:S(2)}) collective-permute-start(f32[8,256]{1,0:T(8,128)S(1)} %shard_map.149.own_ref), channel_id=1, source_target_pairs={{0,1},{1,0},{2,3},{3,2},{4,5},{5,4},{6,7},{7,6},{8,9},{9,8},{10,11... | collective-permute-start | bytes 24584 | tf_op jit(solution)/shard_map/ppermute | solution.py:532
  22.6 1.3 %collective-permute-start.2 = (f32[8,128]{1,0:T(8,128)S(1)}, f32[8,128]{1,0:T(8,128)S(1)}, u32[]{:S(2)}, u32[]{:S(2)}) collective-permute-start(f32[8,128]{1,0:T(8,128)S(1)} %get-tuple-element.42), channel_id=1, source_target_pairs={{0,1},{1,0},{2,3},{3,2},{4,5},{5,4},{6,7},{7,6},{8,9},{9,8},{10,11... | collective-permute-start | bytes 12296 | tf_op jit(solution)/shard_map/ppermute | solution.py:541
  23.9 8.7 %collective-permute-start.3 = (f32[8,128]{1,0:T(8,128)S(1)}, f32[8,128]{1,0:T(8,128)S(1)}, u32[]{:S(2)}, u32[]{:S(2)}) collective-permute-start(f32[8,128]{1,0:T(8,128)S(1)} %add.12._), channel_id=1, source_target_pairs={{0,2},{1,3},{2,0},{3,1},{4,6},{5,7},{6,4},{7,5},{8,10},{9,11},{10,... | collective-permute-start | bytes 12296 | tf_op jit(solution)/shard_map/ppermute | solution.py:541
  32.6 11.8 %collective-permute-start.5 = (bf16[272,512]{1,0:T(8,128)(2,1)S(1)}, bf16[272,512]{1,0:T(8,128)(2,1)S(1)}, u32[]{:S(2)}, u32[]{:S(2)}) collective-permute-start(bf16[272,512]{1,0:T(8,128)(2,1)S(1)} %get-tuple-element.66), channel_id=1, source_target_pairs={{0,1},{1,0},{2,3},{3,2},{4,5},{5,4},{6,7},{7,6},{8,9},{9,8},{10,11... | collective-permute-start | bytes 835592 | tf_op jit(solution)/shard_map/ppermute | solution.py:532
  32.7 11.7 %collective-permute-start.6 = (bf16[272,512]{1,0:T(8,128)(2,1)S(1)}, bf16[272,512]{1,0:T(8,128)(2,1)S(1)}, u32[]{:S(2)}, u32[]{:S(2)}) collective-permute-start(bf16[272,512]{1,0:T(8,128)(2,1)S(1)} %get-tuple-element.67), channel_id=1, source_target_pairs={{1,2},{2,1},{3,4},{4,3},{5,6},{6,5},{7,8},{8,7},{9,10},{10,9},{11,... | collective-permute-start | bytes 835592 | tf_op jit(solution)/shard_map/ppermute | solution.py:537
  33.6 7.2 %collective-permute-start.4 = (f32[8,128]{1,0:T(8,128)S(1)}, f32[8,128]{1,0:T(8,128)S(1)}, u32[]{:S(2)}, u32[]{:S(2)}) collective-permute-start(f32[8,128]{1,0:T(8,128)S(1)} %add.13._), channel_id=1, source_target_pairs={{0,4},{1,5},{2,6},{3,7},{4,0},{5,1},{6,2},{7,3},{8,12},{9,13},{10,... | collective-permute-start | bytes 12296 | tf_op jit(solution)/shard_map/ppermute | solution.py:541
  40.8 8.9 %collective-permute-start.7 = (f32[8,128]{1,0:T(8,128)S(1)}, f32[8,128]{1,0:T(8,128)S(1)}, u32[]{:S(2)}, u32[]{:S(2)}) collective-permute-start(f32[8,128]{1,0:T(8,128)S(1)} %add.14._), channel_id=1, source_target_pairs={{0,8},{1,9},{2,10},{3,11},{4,12},{5,13},{6,14},{7,15},{8,0},{9,1},... | collective-permute-start | bytes 12296 | tf_op jit(solution)/shard_map/ppermute | solution.py:541

commit v5 on v4

--- a/solution.py
+++ b/solution.py
@@ -54,10 +54,8 @@
     return [(lane == h).astype(F32).astype(BF16) for h in range(heads_per_group)]
 
 
-def arrange(par, own, from_a, from_b):
-    before = jnp.where(par == 0, from_b, from_a)
-    after = jnp.where(par == 0, from_a, from_b)
-    return before, own, after
+def arrange(even, from_a, from_b):
+    return jnp.where(even, from_b, from_a), jnp.where(even, from_a, from_b)
 
 
 def distances(ext, ext_t, first, d2_ref, count):
@@ -154,10 +152,10 @@
             outer_cols, shared_cols = window_parts(t)
             outers, shareds = [], []
             for h in range(per):
-                gam = gam_ref[layer, g * per + h] / scale
+                gam = gam_ref[layer, g * per + h, 0:1] / scale
                 outer, shared = scores[t][h]
                 outer = outer - gam * d2_ref[d2_first + i + t, :, outer_cols]
-                shared = shared - gam * d2_ref[d2_first + i + t, :, shared_cols]
+                shared = shared - jnp.concatenate([gam, gam], axis=1) * d2_ref[d2_first + i + t, :, shared_cols]
                 if exact:
                     peak = jnp.maximum(jnp.maximum(outer, shared[:, :BLK]), shared[:, BLK:])
                     peak = jnp.max(peak, axis=1, keepdims=True)
@@ -218,8 +216,9 @@
     return out
 
 
-def pack_kernel(nb, me_ref, list_ref, pos_ref, spec_ref, own_ref):
+def pack_kernel(nb, me_ref, list_ref, pos_ref, spec_ref, own_ref, side_ref):
     own_ref[...] = jnp.zeros_like(own_ref)
+    side_ref[...] = jnp.full(side_ref.shape, lax.rem(me_ref[0], 2).astype(F32))
     own_ref[0:3] = pos_ref[...]
     own_ref[3:4] = spec_ref[...].astype(F32)
     for b in range(nb):
@@ -229,54 +228,71 @@
             own_ref[4 + s : 5 + s, b * BLK : (b + 1) * BLK] = jnp.full((1, BLK), ok.astype(F32))
 
 
+def table_kernel(
+    wq_h, embed_h, gains_h, wk_h, wv_h, gam_h, outg_h, ro_h,
+    q_out, k_out, v_out, embed_out, gains_out, w_out, rates_out,
+    wq, wk, wv, gam_ref, outg, ro, sem,
+):
+    pairs = (
+        (embed_h, embed_out), (gains_h, gains_out), (wq_h.at[0], wq), (wk_h.at[0], wk), (wv_h.at[0], wv),
+        (gam_h, gam_ref), (outg_h, outg), (ro_h, ro),
+    )
+    copies = [pltpu.make_async_copy(src, dst, sem.at[n]) for n, (src, dst) in enumerate(pairs)]
+    for c in copies:
+        c.start()
+    for c in copies[:2]:
+        c.wait()
+    embed = embed_out[...].astype(F32)
+    normed = (embed * inv_rms(embed) * gains_out[0, 0:1]).astype(BF16)
+    for c in copies[2:]:
+        c.wait()
+    for w, out in ((wq, q_out), (wk, k_out), (wv, v_out)):
+        out[...] = mm(normed, w[...]).astype(BF16)
+    w_out[...] = jnp.broadcast_to(outg[...] * ro[...], w_out.shape)
+    layers, heads = gam_ref.shape
+    rates = gam_ref[...].T
+    for layer in range(layers):
+        for h in range(heads):
+            rates_out[layer, h] = jnp.broadcast_to(rates[h : h + 1, layer : layer + 1], (8, LANES))
+
+
 def first_kernel(
     nb, heads, hdim,
-    me_ref, gam_ref, gamv_ref, own_ref, ra_ref, rb_ref, embed_ref, gains_ref, outg_ref, ro_ref,
+    par_ref, gam_ref, own_ref, ra_ref, rb_ref, qt_ref, kt_ref, vt_ref, embed_ref, gains_ref, w_ref,
     wq_h, wk_h, wv_h, wo_h, wu_h, wd_h,
-    e_out, ext_ref, gk_ref, gamk_ref, par_out, o_ref, rl_ref, v_ref, x1_ref, gd_ref, e_ref, wo0, wu0, wd0,
+    e_out, ext_ref, o_ref, rl_ref, v_ref, x1_ref, gd_ref, e_ref, wo0, wu0, wd0,
     st_ref, q1_ref, k1_ref, v1_ref, o1_ref, rl1_ref, e1_ref, x11_ref, gd1_ref, top_ref, wq1, wk1, wv1, wo1, wu1, wd1,
-    wq0, wk0, wv0, d2_ref, x0_ref, q_ref, k_ref, vm_ref, vm1_ref, sem,
+    d2_ref, x0_ref, q_ref, k_ref, vm_ref, vm1_ref, sem,
 ):
     qb = nb + 2
     kb = nb + 4
     mid = slice(BLK, (nb + 1) * BLK)
     sources = (wq_h, wk_h, wv_h, wo_h, wu_h, wd_h)
-    targets = ((wq0, wk0, wv0, wo0, wu0, wd0), (wq1, wk1, wv1, wo1, wu1, wd1))
+    targets = ((None, None, None, wo0, wu0, wd0), (wq1, wk1, wv1, wo1, wu1, wd1))
     copies = []
     for layer in range(2):
         copies.append([
             pltpu.make_async_copy(src.at[layer], dst, sem.at[layer, n])
             for n, (src, dst) in enumerate(zip(sources, targets[layer]))
+            if dst is not None
         ])
         for c in copies[layer]:
             c.start()
-    par = lax.rem(me_ref[0], 2)
-    before, own, after = arrange(par, own_ref[...], ra_ref[...], rb_ref[...])
-    ext = jnp.concatenate([before, own, after], axis=1)
+    before, after = arrange(par_ref[0:1, 0:1] < 0.5, ra_ref[...], rb_ref[...])
+    ext = jnp.concatenate([before, own_ref[...], after], axis=1)
     ext_ref[...] = ext
-    gk_ref[...] = gains_ref[...]
-    par_out[...] = jnp.full(par_out.shape, par.astype(F32))
-    rates = gamv_ref[...].T
-    for layer in range(2):
-        gamk_ref[layer] = jnp.broadcast_to(rates[:, layer : layer + 1], (heads, LANES))
     ext_t = ext.T
     distances(ext, ext_t, 1, d2_ref, qb)
 
-    embed = embed_ref[...].astype(F32)
-    normed = (embed * inv_rms(embed) * gains_ref[0, 0:1]).astype(BF16)
     scale = hdim ** (-0.5)
     spec = ext_t[:, 3:4].astype(jnp.int32)
     nspec = embed_ref.shape[0]
     onehot = (spec == lax.broadcasted_iota(jnp.int32, (kb * BLK, nspec), 1)).astype(F32).astype(BF16)
     onehot_q = onehot[BLK : (qb + 1) * BLK]
     x0_ref[...] = mm(onehot_q, embed_ref[...])
-    for c in copies[0][:3]:
-        c.wait()
-    q_table = mm(normed, wq0[...]).astype(BF16)
-    q_ref[...] = mm(onehot_q, q_table).astype(BF16)
-    k_table = mm(normed, wk0[...]).astype(BF16)
-    k_ref[...] = mm(onehot, k_table).astype(BF16)
-    v_ref[...] = mm(onehot, mm(normed, wv0[...]).astype(BF16)).astype(BF16)
+    q_ref[...] = mm(onehot_q, qt_ref[...]).astype(BF16)
+    k_ref[...] = mm(onehot, kt_ref[...]).astype(BF16)
+    v_ref[...] = mm(onehot, vt_ref[...]).astype(BF16)
     split_heads(v_ref, vm_ref, hdim)
 
     def run(exact):
@@ -287,7 +303,7 @@
 
         attend(exact, q_ref, k_ref, vm_ref, o_ref, rl_ref, e_ref, d2_ref, 0, gam_ref, 0, heads, hdim, qb)
 
-        arrived(copies[0][3:])
+        arrived(copies[0])
 
         def feed(layer, x1, w_up, w_down, keep):
             inner = (x1 * inv_rms(x1) * gains_ref[layer, 1:2]).astype(BF16)
@@ -315,7 +331,7 @@
         x11_ref[...] = x1
         x2 = feed(1, x1, wu1, wd1, lambda pre: gd1_ref.__setitem__(..., pre))
 
-        w = outg_ref[...] * ro_ref[...]
+        w = w_ref[0:1]
         r = inv_rms(x2)
         along = jnp.sum(x2 * w, axis=1, keepdims=True)
         e_out[...] = jnp.broadcast_to(jnp.sum(along * r), e_out.shape)
@@ -323,7 +339,7 @@
         top_ref[...] = r * (w - x2 * (r * r * along * (1.0 / width)))
 
     run(False)
-    small = jnp.logical_and(small_scores(q_table, k_table, hdim), small_scores(q1_ref[...], k1_ref[...], hdim))
+    small = jnp.logical_and(small_scores(qt_ref[...], kt_ref[...], hdim), small_scores(q1_ref[...], k1_ref[...], hdim))
 
     @pl.when(jnp.logical_not(small))
     def _():
@@ -377,7 +393,7 @@
             for h in range(per):
                 e_outer, e_shared = e1_ref[i + t, g * per + h, :, outer_cols], e1_ref[i + t, g * per + h, :, shared_cols]
                 outer, shared = prods[t][h]
-                gam = gam_ref[1, g * per + h : g * per + h + 1]
+                gam = gam_ref[1, g * per + h, 0:1]
                 outer = e_outer.astype(F32) * (outer - delta[h][at])
                 shared = e_shared.astype(F32) * (shared - delta[h][at])
                 pair_outer = pair_outer + gam * outer
@@ -436,7 +452,7 @@
 
 def last_kernel(
     nb, heads, hdim,
-    par_ref, gam_ref, _, ext_ref, gains_ref, paya_ref, payb_ref, part_ref, halo_ref, g1_ref,
+    par_ref, gam_ref, energy_ref, ext_ref, gains_ref, paya_ref, payb_ref, part_ref, halo_ref, g1_ref,
     o_ref, rl_ref, v_ref, x1_ref, gd_ref, e_ref, wo, wu, wd,
     f_ref,
     datt_ref, sum_ref, ends_ref,
@@ -444,9 +460,10 @@
     qb = nb + 2
     ext = ext_ref[...]
     ext_t = ext.T
+
     even = par_ref[0:1, 0:1] < 0.5
     from_a, from_b = paya_ref[...].astype(F32), payb_ref[...].astype(F32)
-    from_low, from_high = jnp.where(even, from_b, from_a), jnp.where(even, from_a, from_b)
+    from_low, from_high = arrange(even, from_a, from_b)
     part = part_ref[...]
     pieces = [halo_ref[:BLK] + from_low[BLK : 2 * BLK]]
     own_parts = [part[i * BLK : (i + 1) * BLK] for i in range(nb)]
@@ -470,7 +487,7 @@
         lane = lax.broadcasted_iota(jnp.int32, (1, LANES), 1) // hdim
         gam = jnp.zeros((1, LANES), F32)
         for h in range(per):
-            gam = jnp.where(lane == h, gam_ref[0, g * per + h : g * per + h + 1], gam)
+            gam = jnp.where(lane == h, gam_ref[0, g * per + h, 0:1], gam)
         d_o = datt_ref[rows, cols] * rl_ref[rows, cols] * gam
         return d_o.astype(BF16), delta_of(d_o * o_ref[rows, cols].astype(F32), per, hdim)
 
@@ -562,13 +579,13 @@
 
     vmem = pl.BlockSpec(memory_space=vm)
     keep = functools.partial(pltpu.with_memory_space_constraint, memory_space=vm)
-    place = me.reshape(1)
-    own = pl.pallas_call(
+    pin = functools.partial(pltpu.with_memory_space_constraint, memory_space=pltpu.HBM)
+    own, side = pl.pallas_call(
         functools.partial(pack_kernel, nb),
-        out_shape=vm((8, atoms), F32),
+        out_shape=[vm((8, atoms), F32), vm((8, LANES), F32)],
         in_specs=[smem, smem, vmem, vmem],
-        out_specs=vmem,
-    )(place, block_list, positions, species.reshape(1, atoms))
+        out_specs=[vmem, vmem],
+    )(me.reshape(1), block_list, positions, species.reshape(1, atoms))
     edge = 2 * BLK
     if atoms == edge:
         send_a = send_b = own
@@ -577,15 +594,35 @@
         send_a = jnp.where(me % 2 == 0, last, first)
         send_b = jnp.where(me % 2 == 0, first, last)
     near_a, near_b = swap_a(send_a), swap_b(send_b)
-    pin = functools.partial(pltpu.with_memory_space_constraint, memory_space=pltpu.HBM)
-    gammas = pin(gammas)
+    hbm = pl.BlockSpec(memory_space=pltpu.HBM)
+    table = vm(embed.shape, BF16)
+    square = vm((width, width), BF16)
+    small = pl.pallas_call(
+        table_kernel,
+        out_shape=[
+            table, table, table, table, vm(norm_gains.shape, F32), vm((8, width), F32),
+            vm((layers, heads, 8, LANES), F32),
+        ],
+        in_specs=[hbm] * 8,
+        out_specs=[vmem] * 7,
+        scratch_shapes=[
+            square, square, square, vm((layers, heads), F32), vm((1, width), F32), vm((1, width), F32),
+            pltpu.SemaphoreType.DMA((8,)),
+        ],
+        compiler_params=pltpu.CompilerParams(vmem_limit_bytes=8 * 1024 * 1024),
+        cost_estimate=work(1),
+    )(
+        pin(w_query), pin(embed), pin(norm_gains), pin(w_key), pin(w_value), pin(gammas),
+        pin(out_gain.reshape(1, width)), pin(readout.reshape(1, width)),
+    )
+    *tables, gains, w, rates = (keep(x) for x in small)
+    side = keep(side)
     weights = (w_query, w_key, w_value, w_out, w_up, w_down)
     shapes = [vm((width, width), BF16)] * 4 + [vm((width, ff), BF16), vm((ff, width), BF16)]
     first = pl.pallas_call(
         functools.partial(first_kernel, nb, heads, hdim),
         out_shape=[
-            vm((8, LANES), F32), vm((8, kb * BLK), F32), vm(norm_gains.shape, F32),
-            vm((layers, heads, LANES), F32), vm((8, LANES), F32),
+            vm((8, LANES), F32), vm((8, kb * BLK), F32),
             vm((qb * BLK, width), BF16), vm((qb * BLK, width), F32), vm((kb * BLK, width), BF16),
             vm((qb * BLK, width), F32), vm((qb * BLK, ff), F32), vm((qb, heads, BLK, 3 * BLK), BF16), *shapes[3:],
             vm((qb * BLK, width), F32), vm((nb * BLK, width), BF16), vm((qb * BLK, width), BF16),
@@ -593,23 +630,21 @@
             vm((nb, heads, BLK, 3 * BLK), BF16), vm((nb * BLK, width), F32), vm((nb * BLK, ff), F32),
             vm((nb * BLK, width), F32), *shapes,
         ],
-        in_specs=[smem, smem] + [vmem] * 8 + [pl.BlockSpec(memory_space=pltpu.HBM)] * 6,
-        out_specs=[vmem] * 30,
+        in_specs=[vmem] * 11 + [hbm] * 6,
+        out_specs=[vmem] * 27,
         scratch_shapes=[
-            *shapes[:3], vm((qb, BLK, 3 * BLK), F32), vm((qb * BLK, width), F32), vm((qb * BLK, width), BF16),
+            vm((qb, BLK, 3 * BLK), F32), vm((qb * BLK, width), F32), vm((qb * BLK, width), BF16),
             vm((kb * BLK, width), BF16), vm((LANES // hdim, kb * BLK, width), BF16),
             vm((LANES // hdim, qb * BLK, width), BF16), pltpu.SemaphoreType.DMA((2, 6)),
         ],
         compiler_params=pltpu.CompilerParams(vmem_limit_bytes=20 * 1024 * 1024),
         cost_estimate=work(qb * 7),
     )(
-        place, gammas, gammas, keep(own), keep(near_a), keep(near_b), pin(embed), pin(norm_gains),
-        pin(out_gain.reshape(1, width)), pin(readout.reshape(1, width)), *(pin(w) for w in weights),
+        side, rates, keep(own), keep(near_a), keep(near_b), *tables, gains, w, *(pin(x) for x in weights),
     )
-    energy, ext, gains = first[0], keep(first[1]), keep(first[2])
-    rates, side = keep(first[3]), keep(first[4])
-    saved0 = [keep(x) for x in first[5:14]]
-    saved1 = [keep(x) for x in first[14:]]
+    energy, ext = first[0], keep(first[1])
+    saved0 = [keep(x) for x in first[2:11]]
+    saved1 = [keep(x) for x in first[11:]]
     energy = energy + hop(energy, 1)
     pay = vm((2 * BLK + 16, width), BF16)
     pay_a, pay_b, part, halo, pairs = pl.pallas_call(

time: 50.4 us -> 49 us (0.972)
  starting transfers between devices: 15.4 us -> 13.9 us
  waiting for transfers between devices: 4.98 us -> 4.47 us
    pallas_call x1 -> x2, Pallas kernels: 0.72 us -> 2.63 us  [the longest x1 1.91 us: local(): pl.pallas_call(table_kernel, out_shape=[table, table, table, table, vm(no...]
    pallas_call x1, Pallas kernels: 15.3 us -> 13.8 us  [local(): pl.pallas_call(functools.partial(first_kernel, nb, heads, hdim), out_shap...]
    ppermute x4, starting transfers between devices: 9.32 us -> 7.87 us  [hop(): lax.ppermute(x, 'chain', [(i, i ^ step) for i in range(lax.axis_size('cha...]
    ppermute x2, waiting for transfers between devices: 0.83 us -> 0.01 us  [swap_a(): return lax.ppermute(x, 'chain', [(i, i ^ 1) for i in range(n)])]
  transfers between devices with their start and end apart: 8 -> 8, of which waited for: 3 -> 2; matrix products, arithmetic and copies ran while one was open for 0% -> 0% of each run, Pallas kernels for 25% -> 30%
where the time goes in v5:
time: 49 us; the launch traced here: 48.8 us
  Pallas kernels  29.2 us (60%)
  starting transfers between devices  13.9 us (28%)
  waiting for transfers between devices  4.47 us (9%)
  between operations  0.72 us (1%)
  local copies, waits for them, and re-layouts  0.52 us (1%)
    pallas_call x1, Pallas kernels, local(): pl.pallas_call(functools.partial(first_kernel, nb, heads, hdim), out_shap...  13.8 us
    ppermute x4, starting transfers between devices, hop(): lax.ppermute(x, 'chain', [(i, i ^ step) for i in range(lax.axis_size('cha...  7.87 us
    pallas_call x1, Pallas kernels, local(): pl.pallas_call(functools.partial(middle_kernel, nb, heads, hdim), out_sha...  6.38 us
    pallas_call x1, Pallas kernels, local(): pl.pallas_call(functools.partial(last_kernel, nb, heads, hdim), out_shape...  5.4 us
    ppermute x2, starting transfers between devices, swap_a(): return lax.ppermute(x, 'chain', [(i, i ^ 1) for i in range(n)])  4.47 us
    ppermute x4, waiting for transfers between devices, hop(): lax.ppermute(x, 'chain', [(i, i ^ step) for i in range(lax.axis_size('cha...  4.46 us
    pallas_call x1, Pallas kernels, local(): pl.pallas_call(table_kernel, out_shape=[table, table, table, table, vm(no...  1.91 us
    ppermute x2, starting transfers between devices, swap_b(): lax.ppermute(x, 'chain', [(i, (i + 1 ^ 1) - 1) for i in range(1, n - 1)])  1.56 us
  transfers between devices with their start and end apart: 8, of which 2 were waited for; matrix products, arithmetic and copies ran while one was open for 0% of the time, Pallas kernels for 30%

profile of v5, /device:TPU:0, one launch (start us, length us, event | category | flops | bytes accessed | tf_op | source)
XLA Modules:
  0.0 48.8 jit_solution(9587663073978285575)
XLA Ops:
  0.6 0.7 %shard_map.149 = (f32[8,256]{1,0:T(8,128)S(1)}, f32[8,128]{1,0:T(8,128)S(1)}) custom-call(s32[1]{0:T(128)} %bitcast.me_ref, s32[2,3]{1,0:T(2,128)} %list_ref.1, f32[3,256]{1,0:T(4,128)} %pos_ref.1, s32[1,256]{1,0:T(1,128)} %bitcast.7), custom_call_target="tpu_custom_call" | custom-call | tf_op jit(solution)/shard_map/pallas_call | solution.py:583
  1.4 0.7 %collective-permute-start.1 = (f32[8,256]{1,0:T(8,128)S(1)}, f32[8,256]{1,0:T(8,128)S(1)}, u32[]{:S(2)}, u32[]{:S(2)}) collective-permute-start(f32[8,256]{1,0:T(8,128)S(1)} %get-tuple-element.50.own_ref), channel_id=1, source_target_pairs={{1,2},{2,1},{3,4},{4,3},{5,6},{6,5},{7,8},{8,7},{9,10},{10,9},{11,... | collective-permute-start | bytes 24584 | tf_op jit(solution)/shard_map/ppermute | solution.py:554
  2.0 4.4 %collective-permute-start = (f32[8,256]{1,0:T(8,128)S(1)}, f32[8,256]{1,0:T(8,128)S(1)}, u32[]{:S(2)}, u32[]{:S(2)}) collective-permute-start(f32[8,256]{1,0:T(8,128)S(1)} %get-tuple-element.50.own_ref), channel_id=1, source_target_pairs={{0,1},{1,0},{2,3},{3,2},{4,5},{5,4},{6,7},{7,6},{8,9},{9,8},{10,11... | collective-permute-start | bytes 24584 | tf_op jit(solution)/shard_map/ppermute | solution.py:549
  6.4 1.9 %shard_map.150 = (bf16[128,512]{1,0:T(8,128)(2,1)S(1)}, bf16[128,512]{1,0:T(8,128)(2,1)S(1)}, bf16[128,512]{1,0:T(8,128)(2,1)S(1)}, bf16[128,512]{1,0:T(8,128)(2...) custom-call(bf16[2,512,512]{2,1,0:T(8,128)(2,1)} %wq_h.3, ...), custom_call_target="tpu_custom_call" | custom-call | flops 536870912 | tf_op jit(solution)/shard_map/pallas_call | solution.py:600
  8.3 0.0 collective-permute-done.1.rb_ref
  8.4 0.0 collective-permute-done.ra_ref
  8.4 13.8 %shard_map.151 = (f32[8,128]{1,0:T(8,128)S(1)}, f32[8,768]{1,0:T(8,128)S(1)}, bf16[512,512]{1,0:T(8,128)(2,1)S(1)}, f32[512,512]{1,0:T(8,128)S(1)}, bf16[768,512...) custom-call(f32[8,128]{1,0:T(8,128)S(1)} %get-tuple-element.48.par_r, ...), custom_call_target="tpu_custom_call" | custom-call | flops 15032385536 | tf_op jit(solution)/shard_map/pallas_call | solution.py:622
  22.1 0.1 collective-permute-start.2
  22.2 1.1 %collective-permute-done.2 = f32[8,128]{1,0:T(8,128)S(1)} collective-permute-done((f32[8,128]{1,0:T(8,128)S(1)}, f32[8,128]{1,0:T(8,128)S(1)}, u32[]{:S(2)}, u32[]{:S(2)}) %collective-permute-start.2) | collective-permute-done | bytes 4128 | tf_op jit(solution)/shard_map/ppermute | solution.py:558
  23.4 1.5 %collective-permute-start.3 = (f32[8,128]{1,0:T(8,128)S(1)}, f32[8,128]{1,0:T(8,128)S(1)}, u32[]{:S(2)}, u32[]{:S(2)}) collective-permute-start(f32[8,128]{1,0:T(8,128)S(1)} %add.12._), channel_id=1, source_target_pairs={{0,2},{1,3},{2,0},{3,1},{4,6},{5,7},{6,4},{7,5},{8,10},{9,11},{10,... | collective-permute-start | bytes 12296 | tf_op jit(solution)/shard_map/ppermute | solution.py:558
  24.9 6.4 %shard_map.152 = (bf16[272,512]{1,0:T(8,128)(2,1)S(1)}, bf16[272,512]{1,0:T(8,128)(2,1)S(1)}, f32[256,512]{1,0:T(8,128)S(1)}, f32[256,512]{1,0:T(8,128)S(1)}, f32[2,128,384]{2,1,0:T(8,128)S(1)}) custom-call(f32[8,128]{1,0:T(8,128)S(1)} %get-tuple-element.48.par_ref, f32[2,16,8,128]{3,2,1,0:T(8,128)S(1)} %get-tuple-element.49.gam_ref, f32[8,128]{1,0:T(8,128)S(1)} %add.12._, ...), custom_call_target="tpu_custom_call" | custom-call | flops 9663676416 | tf_op jit(solution)/shard_map/pallas_call | solution.py:650
  31.3 0.0 collective-permute-done.3
  31.3 0.1 collective-permute-start.5
  31.4 0.9 %collective-permute-start.6 = (bf16[272,512]{1,0:T(8,128)(2,1)S(1)}, bf16[272,512]{1,0:T(8,128)(2,1)S(1)}, u32[]{:S(2)}, u32[]{:S(2)}) collective-permute-start(bf16[272,512]{1,0:T(8,128)(2,1)S(1)} %get-tuple-element.79), channel_id=1, source_target_pairs={{1,2},{2,1},{3,4},{4,3},{5,6},{6,5},{7,8},{8,7},{9,10},{10,9},{11,... | collective-permute-start | bytes 835592 | tf_op jit(solution)/shard_map/ppermute | solution.py:554
  32.3 3.4 %collective-permute-start.4 = (f32[8,128]{1,0:T(8,128)S(1)}, f32[8,128]{1,0:T(8,128)S(1)}, u32[]{:S(2)}, u32[]{:S(2)}) collective-permute-start(f32[8,128]{1,0:T(8,128)S(1)} %add.13._), channel_id=1, source_target_pairs={{0,4},{1,5},{2,6},{3,7},{4,0},{5,1},{6,2},{7,3},{8,12},{9,13},{10,... | collective-permute-start | bytes 12296 | tf_op jit(solution)/shard_map/ppermute | solution.py:558
  35.6 1.0 %shard_map.153.gd_ref = bf16[512,1024]{1,0:T(8,128)(2,1)S(1)} custom-call(f32[8,128]{1,0:T(8,128)S(1)} %add.13._, f32[512,1024]{1,0:T(8,128)S(1)} %get-tuple-element.87.pre_ref), custom_call_target="tpu_custom_call" | custom-call | flops 2147483648 | tf_op jit(solution)/shard_map/pallas_call | solution.py:664
  36.6 3.3 %collective-permute-done.4 = f32[8,128]{1,0:T(8,128)S(1)} collective-permute-done((f32[8,128]{1,0:T(8,128)S(1)}, f32[8,128]{1,0:T(8,128)S(1)}, u32[]{:S(2)}, u32[]{:S(2)}) %collective-permute-start.4) | collective-permute-done | bytes 4128 | tf_op jit(solution)/shard_map/ppermute | solution.py:558
  39.9 2.9 %collective-permute-start.7 = (f32[8,128]{1,0:T(8,128)S(1)}, f32[8,128]{1,0:T(8,128)S(1)}, u32[]{:S(2)}, u32[]{:S(2)}) collective-permute-start(f32[8,128]{1,0:T(8,128)S(1)} %add.14.energy_ref), channel_id=1, source_target_pairs={{0,8},{1,9},{2,10},{3,11},{4,12},{5,13},{6,14},{7,15},{8,0},{9,1},... | collective-permute-start | bytes 12296 | tf_op jit(solution)/shard_map/ppermute | solution.py:558
  42.8 0.0 collective-permute-done.5.paya_ref
  42.9 0.0 collective-permute-done.6.payb_ref
  42.9 5.4 %shard_map.154 = f32[3,256]{1,0:T(4,128)} custom-call(f32[8,128]{1,0:T(8,128)S(1)} %get-tuple-element.48.par_ref, f32[2,16,8,128]{3,2,1,0:T(8,128)S(1)} %get-tuple-element.49.gam_ref, f32[8,128]{1,0:T(8,128)S(1)} %add.14.energy_ref, f32[8,768]{1,0:T(8,128)S(1)} %get-tuple-element.58.ext_ref, f32[2,2,512]{2,1,0:T(2,128)S(1)} %get-tuple-element.55.gains_ref, ...), custom_call_target="tpu_custom_call" | custom-call | flops 6442450944 | tf_op jit(solution)/shard_map/pallas_call | solution.py:676
  48.2 0.0 collective-permute-done.7
  48.3 0.5 %slice.3 = f32[1,1]{1,0:T(1,128)} slice(f32[8,128]{1,0:T(8,128)S(1)} %add.15), slice={[0:1], [0:1]} | slice | bytes 8 | tf_op jit(solution)/shard_map/slice | solution.py:695
  (4 shorter events, 0.0 us)
Async XLA Ops:
  1.4 7.0 %collective-permute-start.1 = (f32[8,256]{1,0:T(8,128)S(1)}, f32[8,256]{1,0:T(8,128)S(1)}, u32[]{:S(2)}, u32[]{:S(2)}) collective-permute-start(f32[8,256]{1,0:T(8,128)S(1)} %get-tuple-element.50.own_ref), channel_id=1, source_target_pairs={{1,2},{2,1},{3,4},{4,3},{5,6},{6,5},{7,8},{8,7},{9,10},{10,9},{11,... | collective-permute-start | bytes 24584 | tf_op jit(solution)/shard_map/ppermute | solution.py:554
  2.0 6.3 %collective-permute-start = (f32[8,256]{1,0:T(8,128)S(1)}, f32[8,256]{1,0:T(8,128)S(1)}, u32[]{:S(2)}, u32[]{:S(2)}) collective-permute-start(f32[8,256]{1,0:T(8,128)S(1)} %get-tuple-element.50.own_ref), channel_id=1, source_target_pairs={{0,1},{1,0},{2,3},{3,2},{4,5},{5,4},{6,7},{7,6},{8,9},{9,8},{10,11... | collective-permute-start | bytes 24584 | tf_op jit(solution)/shard_map/ppermute | solution.py:549
  22.1 1.2 %collective-permute-start.2 = (f32[8,128]{1,0:T(8,128)S(1)}, f32[8,128]{1,0:T(8,128)S(1)}, u32[]{:S(2)}, u32[]{:S(2)}) collective-permute-start(f32[8,128]{1,0:T(8,128)S(1)} %get-tuple-element.57), channel_id=1, source_target_pairs={{0,1},{1,0},{2,3},{3,2},{4,5},{5,4},{6,7},{7,6},{8,9},{9,8},{10,11... | collective-permute-start | bytes 12296 | tf_op jit(solution)/shard_map/ppermute | solution.py:558
  23.4 7.9 %collective-permute-start.3 = (f32[8,128]{1,0:T(8,128)S(1)}, f32[8,128]{1,0:T(8,128)S(1)}, u32[]{:S(2)}, u32[]{:S(2)}) collective-permute-start(f32[8,128]{1,0:T(8,128)S(1)} %add.12._), channel_id=1, source_target_pairs={{0,2},{1,3},{2,0},{3,1},{4,6},{5,7},{6,4},{7,5},{8,10},{9,11},{10,... | collective-permute-start | bytes 12296 | tf_op jit(solution)/shard_map/ppermute | solution.py:558
  31.3 11.6 %collective-permute-start.5 = (bf16[272,512]{1,0:T(8,128)(2,1)S(1)}, bf16[272,512]{1,0:T(8,128)(2,1)S(1)}, u32[]{:S(2)}, u32[]{:S(2)}) collective-permute-start(bf16[272,512]{1,0:T(8,128)(2,1)S(1)} %get-tuple-element.78), channel_id=1, source_target_pairs={{0,1},{1,0},{2,3},{3,2},{4,5},{5,4},{6,7},{7,6},{8,9},{9,8},{10,11... | collective-permute-start | bytes 835592 | tf_op jit(solution)/shard_map/ppermute | solution.py:549
  31.4 11.5 %collective-permute-start.6 = (bf16[272,512]{1,0:T(8,128)(2,1)S(1)}, bf16[272,512]{1,0:T(8,128)(2,1)S(1)}, u32[]{:S(2)}, u32[]{:S(2)}) collective-permute-start(bf16[272,512]{1,0:T(8,128)(2,1)S(1)} %get-tuple-element.79), channel_id=1, source_target_pairs={{1,2},{2,1},{3,4},{4,3},{5,6},{6,5},{7,8},{8,7},{9,10},{10,9},{11,... | collective-permute-start | bytes 835592 | tf_op jit(solution)/shard_map/ppermute | solution.py:554
  32.3 7.7 %collective-permute-start.4 = (f32[8,128]{1,0:T(8,128)S(1)}, f32[8,128]{1,0:T(8,128)S(1)}, u32[]{:S(2)}, u32[]{:S(2)}) collective-permute-start(f32[8,128]{1,0:T(8,128)S(1)} %add.13._), channel_id=1, source_target_pairs={{0,4},{1,5},{2,6},{3,7},{4,0},{5,1},{6,2},{7,3},{8,12},{9,13},{10,... | collective-permute-start | bytes 12296 | tf_op jit(solution)/shard_map/ppermute | solution.py:558
  39.9 8.3 %collective-permute-start.7 = (f32[8,128]{1,0:T(8,128)S(1)}, f32[8,128]{1,0:T(8,128)S(1)}, u32[]{:S(2)}, u32[]{:S(2)}) collective-permute-start(f32[8,128]{1,0:T(8,128)S(1)} %add.14.energy_ref), channel_id=1, source_target_pairs={{0,8},{1,9},{2,10},{3,11},{4,12},{5,13},{6,14},{7,15},{8,0},{9,1},... | collective-permute-start | bytes 12296 | tf_op jit(solution)/shard_map/ppermute | solution.py:558

commit v6 on v5

--- a/solution.py
+++ b/solution.py
@@ -346,12 +346,21 @@
         run(True)
 
 
+def feed_back_kernel(gains_ref, x1_ref, gd_ref, top_ref, wo, wu, wd, grad_ref, datt_ref):
+    grad = top_ref[...]
+    du = mm_nt(grad.astype(BF16), wd[...]).astype(BF16).astype(F32)
+    dinner = mm_nt((du * gelu_slope(gd_ref[...])).astype(BF16), wu[...]).astype(BF16).astype(F32)
+    grad = grad + rms_back(x1_ref[...], gains_ref[1, 1:2], dinner)
+    grad_ref[...] = grad
+    datt_ref[...] = mm_nt(grad.astype(BF16), wo[...]).astype(BF16).astype(F32)
+
+
 def middle_kernel(
     nb, heads, hdim,
-    par_ref, gam_ref, _, ext_ref, gains_ref, st_ref, q1_ref, k1_ref, v1_ref, o1_ref, rl1_ref, e1_ref, x1_ref, gd_ref, top_ref,
-    wq, wk, wv, wo, wu, wd,
+    par_ref, gam_ref, _, ext_ref, gains_ref, st_ref, q1_ref, k1_ref, v1_ref, o1_ref, rl1_ref, e1_ref, grad_ref, datt_ref,
+    wq, wk, wv,
     paya_ref, payb_ref, part_ref, halo_ref, g1_ref,
-    dq_ref, dk_ref, dv_ref, datt_ref,
+    dq_ref, dk_ref, dv_ref,
 ):
     qb = nb + 2
     mid = slice(BLK, (nb + 1) * BLK)
@@ -360,11 +369,7 @@
     even = par_ref[0:1, 0:1] < 0.5
     ext = ext_ref[...]
     ext_t = ext.T
-    grad = top_ref[...]
-    du = mm_nt(grad.astype(BF16), wd[...]).astype(BF16).astype(F32)
-    dinner = mm_nt((du * gelu_slope(gd_ref[...])).astype(BF16), wu[...]).astype(BF16).astype(F32)
-    grad = grad + rms_back(x1_ref[...], gains_ref[1, 1:2], dinner)
-    datt_ref[...] = mm_nt(grad.astype(BF16), wo[...]).astype(BF16).astype(F32)
+    grad = grad_ref[...]
 
     per = LANES // hdim
     groups = heads // per
@@ -647,17 +652,29 @@
     saved1 = [keep(x) for x in first[11:]]
     energy = energy + hop(energy, 1)
     pay = vm((2 * BLK + 16, width), BF16)
+    (st, q1, k1, v1, o1, rl1, e1, x11, gd1, top), (wq1, wk1, wv1, wo1, wu1, wd1) = saved1[:10], saved1[10:]
+    own_rows = vm((nb * BLK, width), F32)
+    grad, datt = pl.pallas_call(
+        feed_back_kernel,
+        out_shape=[own_rows, own_rows],
+        in_specs=[vmem] * 7,
+        out_specs=[vmem] * 2,
+        compiler_params=pltpu.CompilerParams(vmem_limit_bytes=12 * 1024 * 1024),
+        cost_estimate=work(nb * 3),
+    )(gains, x11, gd1, top, wo1, wu1, wd1)
     pay_a, pay_b, part, halo, pairs = pl.pallas_call(
         functools.partial(middle_kernel, nb, heads, hdim),
         out_shape=[pay, pay, vm((nb * BLK, width), F32), vm((2 * BLK, width), F32), vm((nb, BLK, 3 * BLK), F32)],
-        in_specs=[vmem] * 21,
+        in_specs=[vmem] * 17,
         out_specs=[vmem] * 5,
         scratch_shapes=[
-            vm((nb * BLK, width), BF16), vm((width, qb * BLK), F32), vm((width, qb * BLK), F32), vm((nb * BLK, width), F32),
+            vm((nb * BLK, width), BF16), vm((width, qb * BLK), F32), vm((width, qb * BLK), F32),
         ],
         compiler_params=pltpu.CompilerParams(vmem_limit_bytes=20 * 1024 * 1024),
         cost_estimate=work(nb * 9),
-    )(side, rates, keep(energy), ext, gains, *saved1)
+    )(
+        side, rates, keep(energy), ext, gains, st, q1, k1, v1, o1, rl1, e1, keep(grad), keep(datt), wq1, wk1, wv1
+    )
     energy = energy + hop(energy, 2)
     energy, pay_a, pay_b = lax.optimization_barrier((energy, pay_a, pay_b))
     saved0[4] = keep(

time: 49 us -> 48 us (0.980)
  waiting for transfers between devices: 4.47 us -> 3.34 us
    ppermute x4, starting transfers between devices: 7.87 us -> 11.9 us  [hop(): lax.ppermute(x, 'chain', [(i, i ^ step) for i in range(lax.axis_size('cha...]
    ppermute x2, starting transfers between devices: 4.47 us -> 0.59 us  [swap_a(): return lax.ppermute(x, 'chain', [(i, i ^ 1) for i in range(n)])]
    pallas_call x0 -> x1, Pallas kernels: none -> 1.39 us  [local(): pl.pallas_call(feed_back_kernel, out_shape=[own_rows, own_rows], in_specs...]
    pallas_call x1, Pallas kernels: 6.38 us -> 5.14 us  [local(): pl.pallas_call(functools.partial(middle_kernel, nb, heads, hdim), out_sha...]
    ppermute x4, waiting for transfers between devices: 4.46 us -> 3.33 us  [hop(): lax.ppermute(x, 'chain', [(i, i ^ step) for i in range(lax.axis_size('cha...]
  transfers between devices with their start and end apart: 8 -> 8, of which waited for: 2 -> 1; matrix products, arithmetic and copies ran while one was open for 0% -> 0% of each run, Pallas kernels for 30% -> 31%
where the time goes in v6:
time: 48 us; the launch traced here: 47.9 us
  Pallas kernels  29.2 us (61%)
  starting transfers between devices  14 us (29%)
  waiting for transfers between devices  3.34 us (7%)
  between operations  0.74 us (2%)
  local copies, waits for them, and re-layouts  0.52 us (1%)
    pallas_call x1, Pallas kernels, local(): pl.pallas_call(functools.partial(first_kernel, nb, heads, hdim), out_shap...  13.7 us
    ppermute x4, starting transfers between devices, hop(): lax.ppermute(x, 'chain', [(i, i ^ step) for i in range(lax.axis_size('cha...  11.9 us
    pallas_call x1, Pallas kernels, local(): pl.pallas_call(functools.partial(last_kernel, nb, heads, hdim), out_shape...  5.34 us
    pallas_call x1, Pallas kernels, local(): pl.pallas_call(functools.partial(middle_kernel, nb, heads, hdim), out_sha...  5.14 us
    ppermute x4, waiting for transfers between devices, hop(): lax.ppermute(x, 'chain', [(i, i ^ step) for i in range(lax.axis_size('cha...  3.33 us
    pallas_call x1, Pallas kernels, local(): pl.pallas_call(table_kernel, out_shape=[table, table, table, table, vm(no...  1.92 us
    ppermute x2, starting transfers between devices, swap_b(): lax.ppermute(x, 'chain', [(i, (i + 1 ^ 1) - 1) for i in range(1, n - 1)])  1.55 us
    pallas_call x1, Pallas kernels, local(): pl.pallas_call(feed_back_kernel, out_shape=[own_rows, own_rows], in_specs...  1.39 us
  transfers between devices with their start and end apart: 8, of which 1 were waited for; matrix products, arithmetic and copies ran while one was open for 0% of the time, Pallas kernels for 31%

profile of v6, /device:TPU:0, one launch (start us, length us, event | category | flops | bytes accessed | tf_op | source)
XLA Modules:
  0.0 47.9 jit_solution(18249381694657762406)
XLA Ops:
  0.6 0.7 %shard_map.149 = (f32[8,256]{1,0:T(8,128)S(1)}, f32[8,128]{1,0:T(8,128)S(1)}) custom-call(s32[1]{0:T(128)} %bitcast.me_ref, s32[2,3]{1,0:T(2,128)} %list_ref.1, f32[3,256]{1,0:T(4,128)} %pos_ref.1, s32[1,256]{1,0:T(1,128)} %bitcast.7), custom_call_target="tpu_custom_call" | custom-call | tf_op jit(solution)/shard_map/pallas_call | solution.py:588
  1.4 0.5 %collective-permute-start = (f32[8,256]{1,0:T(8,128)S(1)}, f32[8,256]{1,0:T(8,128)S(1)}, u32[]{:S(2)}, u32[]{:S(2)}) collective-permute-start(f32[8,256]{1,0:T(8,128)S(1)} %get-tuple-element.52.own_ref), channel_id=1, source_target_pairs={{0,1},{1,0},{2,3},{3,2},{4,5},{5,4},{6,7},{7,6},{8,9},{9,8},{10,11... | collective-permute-start | bytes 24584 | tf_op jit(solution)/shard_map/ppermute | solution.py:554
  1.9 0.6 %collective-permute-start.1 = (f32[8,256]{1,0:T(8,128)S(1)}, f32[8,256]{1,0:T(8,128)S(1)}, u32[]{:S(2)}, u32[]{:S(2)}) collective-permute-start(f32[8,256]{1,0:T(8,128)S(1)} %get-tuple-element.52.own_ref), channel_id=1, source_target_pairs={{1,2},{2,1},{3,4},{4,3},{5,6},{6,5},{7,8},{8,7},{9,10},{10,9},{11,... | collective-permute-start | bytes 24584 | tf_op jit(solution)/shard_map/ppermute | solution.py:559
  2.5 1.9 %shard_map.150 = (bf16[128,512]{1,0:T(8,128)(2,1)S(1)}, bf16[128,512]{1,0:T(8,128)(2,1)S(1)}, bf16[128,512]{1,0:T(8,128)(2,1)S(1)}, bf16[128,512]{1,0:T(8,128)(2...) custom-call(bf16[2,512,512]{2,1,0:T(8,128)(2,1)} %wq_h.3, ...), custom_call_target="tpu_custom_call" | custom-call | flops 536870912 | tf_op jit(solution)/shard_map/pallas_call | solution.py:605
  4.5 0.0 collective-permute-done.ra_ref
  4.5 0.0 collective-permute-done.1.rb_ref
  4.5 13.7 %shard_map.151 = (f32[8,128]{1,0:T(8,128)S(1)}, f32[8,768]{1,0:T(8,128)S(1)}, bf16[512,512]{1,0:T(8,128)(2,1)S(1)}, f32[512,512]{1,0:T(8,128)S(1)}, bf16[768,512...) custom-call(f32[8,128]{1,0:T(8,128)S(1)} %get-tuple-element.50.par_r, ...), custom_call_target="tpu_custom_call" | custom-call | flops 15032385536 | tf_op jit(solution)/shard_map/pallas_call | solution.py:627
  18.2 4.0 %collective-permute-start.2 = (f32[8,128]{1,0:T(8,128)S(1)}, f32[8,128]{1,0:T(8,128)S(1)}, u32[]{:S(2)}, u32[]{:S(2)}) collective-permute-start(f32[8,128]{1,0:T(8,128)S(1)} %get-tuple-element.59), channel_id=1, source_target_pairs={{0,1},{1,0},{2,3},{3,2},{4,5},{5,4},{6,7},{7,6},{8,9},{9,8},{10,11... | collective-permute-start | bytes 12296 | tf_op jit(solution)/shard_map/ppermute | solution.py:563
  22.2 1.4 %shard_map.152 = (f32[256,512]{1,0:T(8,128)S(1)}, f32[256,512]{1,0:T(8,128)S(1)}) custom-call(f32[2,2,512]{2,1,0:T(2,128)S(1)} %get-tuple-element.57.gains_ref, f32[256,512]{1,0:T(8,128)S(1)} %get-tuple-element.68.x1_ref, f32[256,1024]{1,0:T(8,128)S(1)} %get-tuple-element.69.gd_ref, f32[256,512]{1,0:T(8,128)S(1)} %get-tuple-element.70.top_ref, ...), custom_call_target="tpu_custom_call" | custom-call | flops 3221225472 | tf_op jit(solution)/shard_map/pallas_call | solution.py:657
  23.6 0.0 collective-permute-done.2
  23.6 2.4 %collective-permute-start.3 = (f32[8,128]{1,0:T(8,128)S(1)}, f32[8,128]{1,0:T(8,128)S(1)}, u32[]{:S(2)}, u32[]{:S(2)}) collective-permute-start(f32[8,128]{1,0:T(8,128)S(1)} %add.12._), channel_id=1, source_target_pairs={{0,2},{1,3},{2,0},{3,1},{4,6},{5,7},{6,4},{7,5},{8,10},{9,11},{10,... | collective-permute-start | bytes 12296 | tf_op jit(solution)/shard_map/ppermute | solution.py:563
  26.0 5.1 %shard_map.153 = (bf16[272,512]{1,0:T(8,128)(2,1)S(1)}, bf16[272,512]{1,0:T(8,128)(2,1)S(1)}, f32[256,512]{1,0:T(8,128)S(1)}, f32[256,512]{1,0:T(8,128)S(1)}, f32[2,128,384]{2,1,0:T(8,128)S(1)}) custom-call(f32[8,128]{1,0:T(8,128)S(1)} %get-tuple-element.50.par_ref, f32[2,16,8,128]{3,2,1,0:T(8,128)S(1)} %get-tuple-element.51.gam_ref, f32[8,128]{1,0:T(8,128)S(1)} %add.12._, ...), custom_call_target="tpu_custom_call" | custom-call | flops 9663676416 | tf_op jit(solution)/shard_map/pallas_call | solution.py:665
  31.2 0.0 collective-permute-done.3
  31.2 0.1 collective-permute-start.5
  31.3 0.9 %collective-permute-start.6 = (bf16[272,512]{1,0:T(8,128)(2,1)S(1)}, bf16[272,512]{1,0:T(8,128)(2,1)S(1)}, u32[]{:S(2)}, u32[]{:S(2)}) collective-permute-start(bf16[272,512]{1,0:T(8,128)(2,1)S(1)} %get-tuple-element.83), channel_id=1, source_target_pairs={{1,2},{2,1},{3,4},{4,3},{5,6},{6,5},{7,8},{8,7},{9,10},{10,9},{11,... | collective-permute-start | bytes 835592 | tf_op jit(solution)/shard_map/ppermute | solution.py:559
  32.2 2.9 %collective-permute-start.4 = (f32[8,128]{1,0:T(8,128)S(1)}, f32[8,128]{1,0:T(8,128)S(1)}, u32[]{:S(2)}, u32[]{:S(2)}) collective-permute-start(f32[8,128]{1,0:T(8,128)S(1)} %add.13._), channel_id=1, source_target_pairs={{0,4},{1,5},{2,6},{3,7},{4,0},{5,1},{6,2},{7,3},{8,12},{9,13},{10,... | collective-permute-start | bytes 12296 | tf_op jit(solution)/shard_map/ppermute | solution.py:563
  35.0 1.0 %shard_map.154.gd_ref = bf16[512,1024]{1,0:T(8,128)(2,1)S(1)} custom-call(f32[8,128]{1,0:T(8,128)S(1)} %add.13._, f32[512,1024]{1,0:T(8,128)S(1)} %get-tuple-element.91.pre_ref), custom_call_target="tpu_custom_call" | custom-call | flops 2147483648 | tf_op jit(solution)/shard_map/pallas_call | solution.py:681
  36.0 3.3 %collective-permute-done.4 = f32[8,128]{1,0:T(8,128)S(1)} collective-permute-done((f32[8,128]{1,0:T(8,128)S(1)}, f32[8,128]{1,0:T(8,128)S(1)}, u32[]{:S(2)}, u32[]{:S(2)}) %collective-permute-start.4) | collective-permute-done | bytes 4128 | tf_op jit(solution)/shard_map/ppermute | solution.py:563
  39.4 2.6 %collective-permute-start.7 = (f32[8,128]{1,0:T(8,128)S(1)}, f32[8,128]{1,0:T(8,128)S(1)}, u32[]{:S(2)}, u32[]{:S(2)}) collective-permute-start(f32[8,128]{1,0:T(8,128)S(1)} %add.14.energy_ref), channel_id=1, source_target_pairs={{0,8},{1,9},{2,10},{3,11},{4,12},{5,13},{6,14},{7,15},{8,0},{9,1},... | collective-permute-start | bytes 12296 | tf_op jit(solution)/shard_map/ppermute | solution.py:563
  42.0 0.0 collective-permute-done.5.paya_ref
  42.0 0.0 collective-permute-done.6.payb_ref
  42.0 5.3 %shard_map.155 = f32[3,256]{1,0:T(4,128)} custom-call(f32[8,128]{1,0:T(8,128)S(1)} %get-tuple-element.50.par_ref, f32[2,16,8,128]{3,2,1,0:T(8,128)S(1)} %get-tuple-element.51.gam_ref, f32[8,128]{1,0:T(8,128)S(1)} %add.14.energy_ref, f32[8,768]{1,0:T(8,128)S(1)} %get-tuple-element.60.ext_ref, f32[2,2,512]{2,1,0:T(2,128)S(1)} %get-tuple-element.57.gains_ref, ...), custom_call_target="tpu_custom_call" | custom-call | flops 6442450944 | tf_op jit(solution)/shard_map/pallas_call | solution.py:693
  47.3 0.0 collective-permute-done.7
  47.3 0.5 %slice.3 = f32[1,1]{1,0:T(1,128)} slice(f32[8,128]{1,0:T(8,128)S(1)} %add.15), slice={[0:1], [0:1]} | slice | bytes 8 | tf_op jit(solution)/shard_map/slice | solution.py:712
  (4 shorter events, 0.0 us)
Async XLA Ops:
  1.4 3.1 %collective-permute-start = (f32[8,256]{1,0:T(8,128)S(1)}, f32[8,256]{1,0:T(8,128)S(1)}, u32[]{:S(2)}, u32[]{:S(2)}) collective-permute-start(f32[8,256]{1,0:T(8,128)S(1)} %get-tuple-element.52.own_ref), channel_id=1, source_target_pairs={{0,1},{1,0},{2,3},{3,2},{4,5},{5,4},{6,7},{7,6},{8,9},{9,8},{10,11... | collective-permute-start | bytes 24584 | tf_op jit(solution)/shard_map/ppermute | solution.py:554
  1.9 2.6 %collective-permute-start.1 = (f32[8,256]{1,0:T(8,128)S(1)}, f32[8,256]{1,0:T(8,128)S(1)}, u32[]{:S(2)}, u32[]{:S(2)}) collective-permute-start(f32[8,256]{1,0:T(8,128)S(1)} %get-tuple-element.52.own_ref), channel_id=1, source_target_pairs={{1,2},{2,1},{3,4},{4,3},{5,6},{6,5},{7,8},{8,7},{9,10},{10,9},{11,... | collective-permute-start | bytes 24584 | tf_op jit(solution)/shard_map/ppermute | solution.py:559
  18.2 5.4 %collective-permute-start.2 = (f32[8,128]{1,0:T(8,128)S(1)}, f32[8,128]{1,0:T(8,128)S(1)}, u32[]{:S(2)}, u32[]{:S(2)}) collective-permute-start(f32[8,128]{1,0:T(8,128)S(1)} %get-tuple-element.59), channel_id=1, source_target_pairs={{0,1},{1,0},{2,3},{3,2},{4,5},{5,4},{6,7},{7,6},{8,9},{9,8},{10,11... | collective-permute-start | bytes 12296 | tf_op jit(solution)/shard_map/ppermute | solution.py:563
  23.6 7.6 %collective-permute-start.3 = (f32[8,128]{1,0:T(8,128)S(1)}, f32[8,128]{1,0:T(8,128)S(1)}, u32[]{:S(2)}, u32[]{:S(2)}) collective-permute-start(f32[8,128]{1,0:T(8,128)S(1)} %add.12._), channel_id=1, source_target_pairs={{0,2},{1,3},{2,0},{3,1},{4,6},{5,7},{6,4},{7,5},{8,10},{9,11},{10,... | collective-permute-start | bytes 12296 | tf_op jit(solution)/shard_map/ppermute | solution.py:563
  31.2 10.8 %collective-permute-start.5 = (bf16[272,512]{1,0:T(8,128)(2,1)S(1)}, bf16[272,512]{1,0:T(8,128)(2,1)S(1)}, u32[]{:S(2)}, u32[]{:S(2)}) collective-permute-start(bf16[272,512]{1,0:T(8,128)(2,1)S(1)} %get-tuple-element.82), channel_id=1, source_target_pairs={{0,1},{1,0},{2,3},{3,2},{4,5},{5,4},{6,7},{7,6},{8,9},{9,8},{10,11... | collective-permute-start | bytes 835592 | tf_op jit(solution)/shard_map/ppermute | solution.py:554
  31.3 10.7 %collective-permute-start.6 = (bf16[272,512]{1,0:T(8,128)(2,1)S(1)}, bf16[272,512]{1,0:T(8,128)(2,1)S(1)}, u32[]{:S(2)}, u32[]{:S(2)}) collective-permute-start(bf16[272,512]{1,0:T(8,128)(2,1)S(1)} %get-tuple-element.83), channel_id=1, source_target_pairs={{1,2},{2,1},{3,4},{4,3},{5,6},{6,5},{7,8},{8,7},{9,10},{10,9},{11,... | collective-permute-start | bytes 835592 | tf_op jit(solution)/shard_map/ppermute | solution.py:559
  32.2 7.2 %collective-permute-start.4 = (f32[8,128]{1,0:T(8,128)S(1)}, f32[8,128]{1,0:T(8,128)S(1)}, u32[]{:S(2)}, u32[]{:S(2)}) collective-permute-start(f32[8,128]{1,0:T(8,128)S(1)} %add.13._), channel_id=1, source_target_pairs={{0,4},{1,5},{2,6},{3,7},{4,0},{5,1},{6,2},{7,3},{8,12},{9,13},{10,... | collective-permute-start | bytes 12296 | tf_op jit(solution)/shard_map/ppermute | solution.py:563
  39.4 8.0 %collective-permute-start.7 = (f32[8,128]{1,0:T(8,128)S(1)}, f32[8,128]{1,0:T(8,128)S(1)}, u32[]{:S(2)}, u32[]{:S(2)}) collective-permute-start(f32[8,128]{1,0:T(8,128)S(1)} %add.14.energy_ref), channel_id=1, source_target_pairs={{0,8},{1,9},{2,10},{3,11},{4,12},{5,13},{6,14},{7,15},{8,0},{9,1},... | collective-permute-start | bytes 12296 | tf_op jit(solution)/shard_map/ppermute | solution.py:563
